TPU v7x, 32 devices: a whole 2x2x4 slice. The times are simulated.
32 devices in a mesh: seq: 8 (over z, core), section: 2 (over y), tp: 2 (over x).
Axes of the slice: x: 2, y: 2, z: 4, core: 2. Of those that a mesh axis runs over, the one named last changes fastest.
Arguments:
- h_in: bfloat16 [2, 2048, 3072], P('section', 'seq', 'tp'), may hold values from -32 to 32
- memory: bfloat16 [2, 2048, 3072], P('section', 'seq', 'tp'), may hold values from -32 to 32
- cotangent: bfloat16 [2, 2048, 3072], P('section', 'seq', 'tp'), may hold values from -6 to 6
- block_docs: int32 [2, 16], P('section', 'seq'), may hold values from 0 to 3, never falling along the last dimension, each value on 1 to 12 neighbouring positions
- w_query: bfloat16 [2, 3072, 1536], P('section', None, 'tp'), may hold values from -0.109375 to 0.109375
- w_out: bfloat16 [2, 1536, 3072], P('section', 'tp'), may hold values from -0.15625 to 0.15625
- self_key_value_weight: bfloat16 [3072, 2, 512], P(None, None, 'tp'), may hold values from -0.109375 to 0.109375
- cache_key_value_weight: bfloat16 [3072, 2, 512], P(None, None, 'tp'), may hold values from -0.109375 to 0.109375
Outputs:
- passed_forward: bfloat16 [2, 2048, 3072], P('section', 'seq', 'tp')
- grad_input: bfloat16 [2, 2048, 3072], P('section', 'seq', 'tp')
- grad_memory: bfloat16 [2, 2048, 3072], P('section', 'seq', 'tp')
- grad_w_query: float32 [2, 3072, 1536], P('section', 'seq', 'tp')
- grad_w_out: float32 [2, 1536, 3072], P('section', 'tp', 'seq')
- grad_w_self_kv: float32 [3072, 2, 512], P(('seq', 'section'), None, 'tp')
- grad_w_cache: float32 [3072, 2, 512], P(('seq', 'section'), None, 'tp')
Inputs may be any that keep to these rules, and one draw needn't show every extreme that they name: block_docs[s, b] is the document of tokens b * 128 to b * 128 + 127 of section s; numbers never fall along a row, and in every row one document spans exactly 12 blocks.
All inputs are finite; a program needn't handle non-finite values.
Results may differ from a plain program's by a relative error of at most 0.02.
Values may be sent and summed in bfloat16 or wider, within the bound.
No kernel may reach another device: no remote copies, remote signals or barrier semaphores. Data moves between devices by JAX's collectives and lax.ppermute only.
A program may use at most 128 MiB of HBM per device.

v0:
```python
import math

import jax
import jax.numpy as jnp
from jax import lax
from jax.sharding import PartitionSpec as P

HEAD_DIM = 128
BLK = 128
WIN = 1024


score_scale = 40.0
norm_eps = 1e-06


def passed_along(value, axis, steps):
    count = lax.axis_size(axis)
    pairs = [(source, (source + steps) % count) for source in range(count)]
    return lax.ppermute(value, axis, pairs)


def row_norm(values):
    wide_vals = values.astype(jnp.float32)
    factor = lax.rsqrt(jnp.mean(wide_vals * wide_vals, axis=-1) + norm_eps)
    return ((wide_vals * factor[:, None]).astype(jnp.bfloat16), factor)


def unit_rows(values):
    return values * lax.rsqrt(jnp.sum(values * values, axis=-1, keepdims=True) + norm_eps)


def visible(query_pos, query_doc, key_pos, key_doc, self_section):
    upper_bound = jnp.where(self_section, query_pos, query_pos // BLK * BLK + BLK - 1)
    lower_bound = jnp.where(self_section, query_pos - WIN, -1)
    same_doc = query_doc[:, None] == key_doc[None, :]
    return (
        same_doc
        & (key_pos[None, :] <= upper_bound[:, None])
        & (key_pos[None, :] > lower_bound[:, None])
    )


def contract_rows(left, right):
    return lax.dot_general(
        left, right, (((0,), (0,)), ((), ())), preferred_element_type=jnp.float32
    )


def contract_cols(left, right):
    return lax.dot_general(
        left, right, (((1,), (1,)), ((), ())), preferred_element_type=jnp.float32
    )


def on_device(
    h_in,
    memory,
    cotangent,
    block_docs,
    w_query,
    w_out,
    self_key_value_weight,
    cache_key_value_weight,
):
    section_id = lax.axis_index("section")
    shard_id = lax.axis_index("seq")
    self_section = section_id == 0
    hidden = h_in[0]
    source = jnp.where(self_section, hidden, memory[0])
    full_rows, full_source = (
        lax.all_gather(hidden, "tp", axis=1, tiled=True),
        lax.all_gather(source, "tp", axis=1, tiled=True),
    )
    row_count = hidden.shape[0]
    hidden_model_width = full_rows.shape[1]
    normalized_input, row_factor = row_norm(full_rows)
    normalized_source, source_factor = row_norm(full_source)
    query_projection_weight = w_query[0]
    out_weight = w_out[0]
    key_value_matrix = jnp.where(self_section, self_key_value_weight, cache_key_value_weight)
    kv_heads = self_key_value_weight.shape[2] // HEAD_DIM
    query_heads = query_projection_weight.shape[1] // HEAD_DIM
    query_group_width = query_heads // kv_heads
    key_value_flattened = key_value_matrix.reshape(hidden_model_width, 2 * kv_heads * HEAD_DIM)
    query_matrix = jnp.dot(
        normalized_input, query_projection_weight, preferred_element_type=jnp.float32
    ).reshape(row_count, kv_heads, query_group_width, HEAD_DIM)
    key_value_pairs = jnp.dot(
        normalized_source, key_value_flattened, preferred_element_type=jnp.float32
    ).reshape(row_count, 2, kv_heads, HEAD_DIM)
    query_unit = unit_rows(query_matrix).astype(jnp.bfloat16)
    key_raw = key_value_pairs[:, 0]
    key_unit = unit_rows(key_raw).astype(jnp.bfloat16)
    value_bf = key_value_pairs[:, 1].astype(jnp.bfloat16)
    packed = jnp.stack([key_unit, value_bf], axis=1).reshape(row_count, 2, kv_heads * HEAD_DIM)
    all_kv, all_docs = (
        lax.all_gather(packed, "seq", axis=0, tiled=True),
        lax.all_gather(block_docs[0], "seq", axis=0, tiled=True),
    )
    sequence_length_total = all_kv.shape[0]
    span_len = math.gcd(sequence_length_total, 512)
    block_count = sequence_length_total // span_len
    key_all = all_kv[:, 0].reshape(block_count, span_len, kv_heads, HEAD_DIM)
    value_all = all_kv[:, 1].reshape(block_count, span_len, kv_heads, HEAD_DIM)
    key_doc_all = jnp.repeat(all_docs, BLK).reshape(block_count, span_len)
    key_pos_all = jnp.arange(sequence_length_total, dtype=jnp.int32).reshape(block_count, span_len)
    query_pos = shard_id * row_count + jnp.arange(row_count, dtype=jnp.int32)
    query_doc = jnp.repeat(block_docs[0], BLK)

    def block_scores(key_block, key_pos, key_doc):
        allowed = visible(query_pos, query_doc, key_pos, key_doc, self_section)[:, None, None, :]
        scores = score_scale * jnp.einsum(
            "tgjd,ugd->tgju", query_unit, key_block, preferred_element_type=jnp.float32
        )
        return (allowed, scores)

    def forward_step(running, pieces):
        numerator, softmax_denominator = running
        key_block, value_block, key_pos, key_doc = pieces
        allowed, scores = block_scores(key_block, key_pos, key_doc)
        weights = jnp.where(allowed, jnp.exp(scores), 0.0)
        softmax_denominator = softmax_denominator + jnp.sum(weights, axis=-1)
        numerator = numerator + jnp.einsum(
            "tgju,ugd->tgjd",
            weights.astype(jnp.bfloat16),
            value_block,
            preferred_element_type=jnp.float32,
        )
        return ((numerator, softmax_denominator), None)

    start_num = jnp.zeros((row_count, kv_heads, query_group_width, HEAD_DIM), jnp.float32)
    start_den = jnp.zeros((row_count, kv_heads, query_group_width), jnp.float32)
    (numerator, softmax_denominator), _ = lax.scan(
        forward_step, (start_num, start_den), (key_all, value_all, key_pos_all, key_doc_all)
    )
    attention_output = (numerator / softmax_denominator[..., None]).astype(jnp.bfloat16)
    attn_flat = attention_output.reshape(row_count, query_heads * HEAD_DIM)
    projected = jnp.dot(attn_flat, out_weight, preferred_element_type=jnp.float32)
    projected = lax.psum_scatter(
        projected.astype(jnp.bfloat16), "tp", scatter_dimension=1, tiled=True
    ).astype(jnp.float32)
    h_out = (hidden.astype(jnp.float32) + projected).astype(jnp.bfloat16)
    passed = passed_along(h_out, "section", 1)
    grad_local = cotangent[0]
    grad_rows = lax.all_gather(grad_local, "tp", axis=1, tiled=True)
    attention_gradient = (
        contract_cols(grad_rows, out_weight)
        .astype(jnp.bfloat16)
        .reshape(row_count, kv_heads, query_group_width, HEAD_DIM)
    )
    delta = jnp.sum(
        attention_gradient.astype(jnp.float32) * attention_output.astype(jnp.float32), axis=-1
    )

    def backward_step(running, pieces):
        key_block, value_block, key_pos, key_doc = pieces
        allowed, scores = block_scores(key_block, key_pos, key_doc)
        probs = jnp.where(allowed, jnp.exp(scores) / softmax_denominator[..., None], 0.0)
        grad_probs = jnp.einsum(
            "tgjd,ugd->tgju", attention_gradient, value_block, preferred_element_type=jnp.float32
        )
        grad_scores = (probs * (grad_probs - delta[..., None])).astype(jnp.bfloat16)
        running = running + score_scale * jnp.einsum(
            "tgju,ugd->tgjd", grad_scores, key_block, preferred_element_type=jnp.float32
        )
        grad_key = score_scale * jnp.einsum(
            "tgju,tgjd->ugd", grad_scores, query_unit, preferred_element_type=jnp.float32
        )
        value_gradient = jnp.einsum(
            "tgju,tgjd->ugd",
            probs.astype(jnp.bfloat16),
            attention_gradient,
            preferred_element_type=jnp.float32,
        )
        return (running, jnp.stack([grad_key, value_gradient], axis=1))

    query_gradient, kv_terms = lax.scan(
        backward_step, jnp.zeros_like(start_num), (key_all, value_all, key_pos_all, key_doc_all)
    )
    kv_terms = kv_terms.reshape(sequence_length_total, 2, kv_heads * HEAD_DIM)
    kv_grads = lax.psum_scatter(
        kv_terms.astype(jnp.bfloat16), "seq", scatter_dimension=0, tiled=True
    ).astype(jnp.float32)
    _, query_pull = jax.vjp(unit_rows, query_matrix)
    grad_queries = (
        query_pull(query_gradient)[0]
        .reshape(row_count, query_heads * HEAD_DIM)
        .astype(jnp.bfloat16)
    )
    _, key_pull = jax.vjp(unit_rows, key_raw)
    key_gradient_rows = key_pull(kv_grads[:, 0].reshape(row_count, kv_heads, HEAD_DIM))[0]
    grad_values = kv_grads[:, 1].reshape(row_count, kv_heads, HEAD_DIM)
    key_value_gradient = (
        jnp.stack([key_gradient_rows, grad_values], axis=1)
        .reshape(row_count, 2 * kv_heads * HEAD_DIM)
        .astype(jnp.bfloat16)
    )
    back_rows = contract_cols(grad_queries, query_projection_weight)
    back_source = contract_cols(key_value_gradient, key_value_flattened)
    rows_part, source_part = (
        lax.psum_scatter(
            back_rows.astype(jnp.bfloat16), "tp", scatter_dimension=1, tiled=True
        ).astype(jnp.float32),
        lax.psum_scatter(
            back_source.astype(jnp.bfloat16), "tp", scatter_dimension=1, tiled=True
        ).astype(jnp.float32),
    )
    hidden_wide = hidden.astype(jnp.float32)
    source_wide = source.astype(jnp.float32)
    row_dot = jnp.sum(rows_part * hidden_wide, axis=1)
    source_dot = jnp.sum(source_part * source_wide, axis=1)
    row_total, source_total = lax.psum((row_dot, source_dot), "tp")
    row_cube = row_factor * row_factor * row_factor
    source_cube = source_factor * source_factor * source_factor
    grad_input = (
        grad_local.astype(jnp.float32)
        + row_factor[:, None] * rows_part
        - hidden_wide * (row_cube * row_total / hidden_model_width)[:, None]
    )
    grad_memory = (
        source_factor[:, None] * source_part
        - source_wide * (source_cube * source_total / hidden_model_width)[:, None]
    )
    weight_share = lax.psum_scatter(
        jnp.stack(
            [contract_rows(normalized_input, grad_queries), contract_rows(grad_rows, attn_flat)],
            axis=1,
        ).astype(jnp.bfloat16),
        "seq",
        scatter_dimension=0,
        tiled=True,
    ).astype(jnp.float32)
    query_grad = weight_share[:, 0]
    out_grad_flip = weight_share[:, 1]
    per_section = lax.psum_scatter(
        contract_rows(normalized_source, key_value_gradient).astype(jnp.bfloat16),
        "seq",
        scatter_dimension=0,
        tiled=True,
    ).astype(jnp.float32)
    by_kind = jnp.stack(
        [jnp.where(self_section, per_section, 0.0), jnp.where(self_section, 0.0, per_section)],
        axis=0,
    )
    shared = jnp.moveaxis(
        lax.psum_scatter(
            by_kind.astype(jnp.bfloat16), "section", scatter_dimension=1, tiled=True
        ).astype(jnp.float32),
        0,
        1,
    )
    share_rows = shared.shape[0]
    self_grad = shared[:, 0].reshape(share_rows, 2, kv_heads * HEAD_DIM)
    cache_grad = shared[:, 1].reshape(share_rows, 2, kv_heads * HEAD_DIM)
    return (
        passed[None],
        grad_input.astype(jnp.bfloat16)[None],
        grad_memory.astype(jnp.bfloat16)[None],
        query_grad[None],
        out_grad_flip.T[None],
        self_grad,
        cache_grad,
    )


def solution(mesh):
    return jax.shard_map(
        on_device,
        mesh=mesh,
        in_specs=(
            P("section", "seq", "tp"),
            P("section", "seq", "tp"),
            P("section", "seq", "tp"),
            P("section", "seq"),
            P("section", None, "tp"),
            P("section", "tp", None),
            P(None, None, "tp"),
            P(None, None, "tp"),
        ),
        out_specs=(
            P("section", "seq", "tp"),
            P("section", "seq", "tp"),
            P("section", "seq", "tp"),
            P("section", "seq", "tp"),
            P("section", "tp", "seq"),
            P(("seq", "section"), None, "tp"),
            P(("seq", "section"), None, "tp"),
        ),
        check_vma=False,
    )
```

profile of v0, /device:TPU:0, one launch (start us, length us, event | category | flops | bytes accessed | tf_op | source)
XLA Modules:
  0.0 507.8 jit_solution(8051703932636332150)
XLA Ops:
  7.2 2.3 broadcast_select_fusion.1
  12.1 3.5 copy.55
  15.6 24.5 %all-gather.15.cloned.1.call-done = bf16[1,256,3072]{2,1,0:T(8,128)(2,1)} async-done(((bf16[1,256,1536]{2,1,0:T(8,128)(2,1)}), bf16[1,256,3072]{2,1,0:T(8,128)(2,1)}) %all-gather.15.cloned.1.call-update) | async-done | bytes 1572880 | tf_op jit(solution)/shard_map/all_gather | solution.py:73
  42.4 3.5 fusion.91
  49.8 8.9 %all-reduce = s32[16]{0:T(128)S(1)} all-reduce(s32[16]{0:T(128)S(1)} %bitcast_dynamic-update-slice_fusion), channel_id=2, replica_groups=mesh['seq'=8,'section'=2,'tp'=2] {'seq'}, use_global_device_ids=true, to_apply=%add | all-reduce | flops 16 | bytes 128
  58.8 6.6 %copy.58 = bf16[1,3072,768]{1,2,0:T(8,128)(2,1)} copy(bf16[1,3072,768]{2,1,0:T(8,128)(2,1)} %param.16) | data formatting | bytes 9437184 | tf_op args[4]
  65.4 3.4 all-gather.13.cloned.1.call-done
  68.9 4.2 fusion.95
  73.5 24.2 %all-gather.11.cloned.1.call-done = bf16[1,256,3072]{2,1,0:T(8,128)(2,1)} async-done(((bf16[1,256,1536]{2,1,0:T(8,128)(2,1)}), bf16[1,256,3072]{2,1,0:T(8,128)(2,1)}) %all-gather.11.cloned.1.call-update) | async-done | bytes 1572880 | tf_op jit(solution)/shard_map/all_gather | solution.py:72
  99.5 4.3 multiply_reduce_fusion.2
  105.0 23.8 %all-gather.9.cloned.1.call-done = bf16[2048,2,256]{2,0,1:T(8,128)(2,1)} async-done(((bf16[256,2,256]{2,0,1:T(8,128)(2,1)}), bf16[2048,2,256]{2,0,1:T(8,128)(2,1)}) %all-gather.9.cloned.1.call-update) | async-done | bytes 2097168 | tf_op jit(solution)/shard_map/all_gather | solution.py:98
  128.8 3.0 fusion.117
  136.4 17.4 %while.40 = (s32[]{:T(128)}, f32[256,2,3,128]{0,3,2,1:T(8,128)S(1)}, f32[256,2,3]{0,2,1:T(4,128)S(1)}, bf16[4,512,2,128]{3,2,1,0:T(2,128)(2,1)}, s32[4,512]{1,0:...) while((s32[]{:T(128)}, ...), condition=%wide.region_6.7_spmd.clone.clone.clone, body=%wide.region_4.6_spmd.clone.clone.clone.sunk | while | flops 408427776 | bytes 10269361 | solution.py:134
  155.6 34.8 %while.41 = (s32[]{:T(128)}, f32[256,2,3,128]{0,3,2,1:T(8,128)S(1)}, bf16[4,512,2,2,128]{4,1,3,2,0:T(8,128)(2,1)}, bf16[4,512,2,128]{3,1,2,0:T(8,128)(2,1)}, s32...) while((s32[]{:T(128)}, ...), condition=%wide.region_10.11_spmd.clone.clone.clone, body=%wide.region_9.10_spmd.clone.clone.clone.sunk | while | flops 1014699776 | bytes 20480720 | solution.py:178
  190.4 3.7 copy.67
  194.1 2.9 convert_element_type.162
  197.1 35.4 %reduce-scatter.12.cloned.1.call-done = bf16[256,2,256]{2,0,1:T(8,128)(2,1)} async-done(((bf16[2048,2,256]{2,0,1:T(8,128)(2,1)}), bf16[256,2,256]{2,0,1:T(8,128)(2,1)}) %reduce-scatter.12.cloned.1.call-update) | async-done | bytes 262160 | tf_op jit(solution)/shard_map/reduce_scatter | solution.py:182
  239.5 2.8 convolution_convert_fusion.2
  244.5 5.1 %fusion.74 = bf16[256,3072]{1,0:T(8,128)(2,1)} fusion(bf16[256,768]{0,1:T(8,128)(2,1)S(1)} %bitcast.319, bf16[1,3072,768]{2,1,0:T(8,128)(2,1)} %param.16), kind=kOutput, calls=%fused_computation.98 | convolution fusion | flops 1208745984 | bytes 6684672 | tf_op jit(solution)/shard_map/dot_general | solution.py:51
  249.7 3.1 convolution_convert_fusion.3
  252.9 5.0 fusion.71
  257.9 23.6 %reduce-scatter.18.cloned.1.call-done = bf16[384,512]{1,0:T(8,128)(2,1)} async-done(((bf16[3072,512]{1,0:T(8,128)(2,1)}), bf16[384,512]{1,0:T(8,128)(2,1)}) %reduce-scatter.18.cloned.1.call-update) | async-done | bytes 393232 | tf_op jit(solution)/shard_map/reduce_scatter | solution.py:236
  283.7 5.2 %fusion.70 = bf16[3072,1,768]{2,0,1:T(8,128)(2,1)} fusion(bf16[256,768]{0,1:T(8,128)(2,1)S(1)} %bitcast.308, bf16[1,256,3072]{2,1,0:T(8,128)(2,1)} %all-gather.13.cloned.1.call-done), kind=kOutput, calls=%fused_computation.91 | convolution fusion | flops 1210318848 | bytes 6684672 | tf_op jit(solution)/shard_map/dot_general | solution.py:45
  288.9 3.7 fusion.69
  292.6 8.3 %pad_maximum_fusion = bf16[3072,2,768]{2,0,1:T(8,128)(2,1)} fusion(bf16[3072,1,768]{2,0,1:T(8,128)(2,1)} %fusion.70, bf16[3072,1,768]{2,0,1:T(8,128)(2,1)} %fusion.69), kind=kLoop, calls=%fused_computation.80 | loop fusion | flops 4718592 | bytes 18874368 | tf_op jit(solution)/shard_map/stack | solution.py:226
  300.9 8.0 %reduce-scatter.10.cloned.1.call-done = bf16[256,1536]{1,0:T(8,128)(2,1)} async-done(((bf16[256,3072]{1,0:T(8,128)(2,1)}), bf16[256,1536]{1,0:T(8,128)(2,1)}) %reduce-scatter.10.cloned.1.call-update) | async-done | bytes 786448 | tf_op jit(solution)/shard_map/reduce_scatter | solution.py:202
  310.3 27.0 %reduce-scatter.14.cloned.1.call-done = bf16[256,1536]{1,0:T(8,128)(2,1)} async-done(((bf16[256,3072]{1,0:T(8,128)(2,1)}), bf16[256,1536]{1,0:T(8,128)(2,1)}) %reduce-scatter.14.cloned.1.call-update) | async-done | bytes 786448 | tf_op jit(solution)/shard_map/reduce_scatter | solution.py:205
  338.8 5.2 %all-reduce.1 = (f32[256]{0:T(256)S(1)}, f32[256]{0:T(256)S(1)}) all-reduce(f32[256]{0:T(256)S(1)} %fusion.88, f32[256]{0:T(256)S(1)} %fusion.86), channel_id=1, replica_groups=mesh['seq'=8,'section'=2,'tp'=2] {'tp'}, use_global_device_ids=true, to_apply=%region_14.15 | all-reduce | flops 512 | bytes 4096 | tf_op jit(solution)/shard_map/psum | solution.py:213
  344.1 21.6 %reduce-scatter.8.cloned.1.call-done = bf16[256,1536]{1,0:T(8,128)(2,1)} async-done(((bf16[256,3072]{1,0:T(8,128)(2,1)}), bf16[256,1536]{1,0:T(8,128)(2,1)}) %reduce-scatter.8.cloned.1.call-update) | async-done | bytes 786448 | tf_op jit(solution)/shard_map/reduce_scatter | solution.py:140
  365.7 2.8 fusion.104
  371.2 25.0 %collective-permute-done = bf16[256,1536]{1,0:T(8,128)(2,1)S(1)} collective-permute-done((bf16[256,1536]{1,0:T(8,128)(2,1)S(1)}, bf16[256,1536]{1,0:T(8,128)(2,1)S(1)}, u32[]{:S(2)}, u32[]{:S(2)}) %collective-permute-start) | collective-permute-done | bytes 786464 | tf_op jit(solution)/shard_map/ppermute | solution.py:20
  399.3 97.0 %reduce-scatter.16.cloned.1.call-done = bf16[384,2,768]{2,0,1:T(8,128)(2,1)} async-done(((bf16[3072,2,768]{2,0,1:T(8,128)(2,1)}), bf16[384,2,768]{2,0,1:T(8,128)(2,1)}) %reduce-scatter.16.cloned.1.call-update) | async-done | bytes 1179664 | tf_op jit(solution)/shard_map/reduce_scatter | solution.py:225
  (251 shorter events, 94.7 us)
Async XLA Ops:
  7.2 32.9 %all-gather.15.cloned.1.call-start = ((), (), s32[]{:S(2)}) async-start(), calls=%async_computation.17 | async-start | bytes 2359296 | tf_op jit(solution)/shard_map/all_gather | solution.py:73
  9.5 59.3 %all-gather.13.cloned.1.call-start = ((), (), s32[]{:S(2)}) async-start(), calls=%async_computation.16 | async-start | bytes 2359296 | tf_op jit(solution)/shard_map/all_gather | solution.py:146
  10.3 87.4 %all-gather.11.cloned.1.call-start = ((), (), s32[]{:S(2)}) async-start(), calls=%async_computation.15 | async-start | bytes 2359296 | tf_op jit(solution)/shard_map/all_gather | solution.py:72
  11.0 117.8 %all-gather.9.cloned.1.call-start = ((), (), s32[]{:S(2)}) async-start(), calls=%async_computation.7 | async-start | bytes 2359296 | tf_op jit(solution)/shard_map/all_gather | solution.py:98
  42.4 5.9 %copy-start.35 = (u32[32]{0:T(128)S(1)}, u32[32]{0:T(128)}, u32[]{:S(2)}) copy-start(u32[32]{0:T(128)} %constant.260) | copy-start | bytes 388
  42.4 7.2 %copy-start.34 = (s32[1,2]{1,0:T(1,128)S(1)}, s32[1,2]{1,0:T(1,128)}, u32[]{:S(2)}) copy-start(s32[1,2]{1,0:T(1,128)} %param.15) | copy-start | bytes 28
  48.3 184.2 %reduce-scatter.12.cloned.1.call-start = ((), (), s32[]{:S(2)}) async-start(), calls=%async_computation.10 | async-start | bytes 2359296 | tf_op jit(solution)/shard_map/reduce_scatter | solution.py:182
  73.3 30.6 %copy-start.8 = (bf16[256,768]{0,1:T(8,128)(2,1)}, bf16[256,768]{0,1:T(8,128)(2,1)S(1)}, u32[]{:S(2)}) copy-start(bf16[256,768]{0,1:T(8,128)(2,1)S(1)} %copy.62) | copy-start | bytes 1179652
  103.9 29.3 %copy-start.20 = (f32[256,2,3]{0,2,1:T(4,128)}, f32[256,2,3]{0,2,1:T(4,128)S(1)}, u32[]{:S(2)}) copy-start(f32[256,2,3]{0,2,1:T(4,128)S(1)} %get-tuple-element.1053) | copy-start | bytes 18436
  103.9 29.3 %copy-start.18 = (f32[256,2,3]{0,2,1:T(4,128)}, f32[256,2,3]{0,2,1:T(4,128)S(1)}, u32[]{:S(2)}) copy-start(f32[256,2,3]{0,2,1:T(4,128)S(1)} %add_rsqrt_fusion) | copy-start | bytes 18436
  197.0 41.4 %copy-start.13 = (f32[256,2,2,128]{0,3,2,1:T(8,128)S(1)}, f32[256,2,2,128]{0,3,2,1:T(8,128)}, u32[]{:S(2)}) copy-start(f32[256,2,2,128]{0,3,2,1:T(8,128)} %copy-done.12) | copy-start | bytes 1572868
  197.0 41.5 %copy-start.25 = (f32[256,2]{0,1:T(2,128)S(1)}, f32[256,2]{0,1:T(2,128)}, u32[]{:S(2)}) copy-start(f32[256,2]{0,1:T(2,128)} %copy-done.24) | copy-start | bytes 6148
  197.0 41.5 %copy-start.23 = (f32[256,2]{0,1:T(2,128)S(1)}, f32[256,2]{0,1:T(2,128)}, u32[]{:S(2)}) copy-start(f32[256,2]{0,1:T(2,128)} %copy-done.22) | copy-start | bytes 6148
  197.0 42.5 %copy-start.2 = (bf16[1,256,3072]{2,1,0:T(8,128)(2,1)S(1)}, bf16[1,256,3072]{2,1,0:T(8,128)(2,1)}, u32[]{:S(2)}) copy-start(bf16[1,256,3072]{2,1,0:T(8,128)(2,1)} %all-gather.15.cloned.1.call-done) | copy-start | bytes 4718596
  197.0 42.5 %copy-start.27 = (f32[256]{0:T(256)S(1)}, f32[256]{0:T(256)}, u32[]{:S(2)}) copy-start(f32[256]{0:T(256)} %copy-done.26) | copy-start | bytes 3076
  197.0 84.5 %reduce-scatter.18.cloned.1.call-start = ((), (), s32[]{:S(2)}) async-start(), calls=%async_computation.13 | async-start | bytes 3538944 | tf_op jit(solution)/shard_map/reduce_scatter | solution.py:236
  242.3 66.6 %reduce-scatter.10.cloned.1.call-start = ((), (), s32[]{:S(2)}) async-start(), calls=%async_computation.9 | async-start | bytes 2359296 | tf_op jit(solution)/shard_map/reduce_scatter | solution.py:202
  244.5 5.2 %copy-start.1 = (bf16[384,8,2,256]{3,1,2,0:T(8,128)(2,1)S(1)}, bf16[384,8,2,256]{3,1,2,0:T(8,128)(2,1)}, u32[]{:S(2)}) copy-start(bf16[384,8,2,256]{3,1,2,0:T(8,128)(2,1)} %copy-done) | copy-start | bytes 9437188
  249.6 87.7 %reduce-scatter.14.cloned.1.call-start = ((), (), s32[]{:S(2)}) async-start(), calls=%async_computation.11 | async-start | bytes 2359296 | tf_op jit(solution)/shard_map/reduce_scatter | solution.py:205
  252.8 112.8 %reduce-scatter.8.cloned.1.call-start = ((), (), s32[]{:S(2)}) async-start(), calls=%async_computation.8 | async-start | bytes 2359296 | tf_op jit(solution)/shard_map/reduce_scatter | solution.py:140
  257.9 138.3 %reduce-scatter.20.cloned.1.call-start = ((), (), s32[]{:S(2)}) async-start(), calls=%async_computation.14 | async-start | bytes 1179648 | tf_op jit(solution)/shard_map/reduce_scatter | solution.py:247
  283.6 5.3 %copy-start.5 = (bf16[1,256,3072]{2,1,0:T(8,128)(2,1)S(1)}, bf16[1,256,3072]{2,1,0:T(8,128)(2,1)}, u32[]{:S(2)}) copy-start(bf16[1,256,3072]{2,1,0:T(8,128)(2,1)} %all-gather.11.cloned.1.call-done) | copy-start | bytes 4718596
  283.6 5.3 %copy-start.16 = (bf16[256,2,3,128]{0,3,2,1:T(8,128)(2,1)S(1)}, bf16[256,2,3,128]{0,3,2,1:T(8,128)(2,1)}, u32[]{:S(2)}) copy-start(bf16[256,2,3,128]{0,3,2,1:T(8,128)(2,1)} %copy-done.15) | copy-start | bytes 1179652
  283.6 5.3 %copy-start.29 = (f32[256]{0:T(256)S(1)}, f32[256]{0:T(256)}, u32[]{:S(2)}) copy-start(f32[256]{0:T(256)} %copy-done.28) | copy-start | bytes 3076
  283.6 212.7 %reduce-scatter.16.cloned.1.call-start = ((), (), s32[]{:S(2)}) async-start(), calls=%async_computation.12 | async-start | bytes 10616832 | tf_op jit(solution)/shard_map/reduce_scatter | solution.py:225
  300.9 8.0 %copy-start.4 = (bf16[1,256,1536]{2,1,0:T(8,128)(2,1)S(1)}, bf16[1,256,1536]{2,1,0:T(8,128)(2,1)}, u32[]{:S(2)}) copy-start(bf16[1,256,1536]{2,1,0:T(8,128)(2,1)} %param.12) | copy-start | bytes 2359300
  300.9 36.4 %copy-start.3 = (bf16[1,256,1536]{2,1,0:T(8,128)(2,1)S(1)}, bf16[1,256,1536]{2,1,0:T(8,128)(2,1)}, u32[]{:S(2)}) copy-start(bf16[1,256,1536]{2,1,0:T(8,128)(2,1)} %broadcast_select_fusion.1) | copy-start | bytes 2359300
  300.9 43.1 %copy-start.33 = (f32[256]{0:T(256)S(1)}, f32[256]{0:T(256)}, u32[]{:S(2)}) copy-start(f32[256]{0:T(256)} %copy-done.32) | copy-start | bytes 3076
  300.9 64.8 %copy-start.11 = (bf16[1,256,1536]{2,1,0:T(8,128)(2,1)S(1)}, bf16[1,256,1536]{2,1,0:T(8,128)(2,1)}, u32[]{:S(2)}) copy-start(bf16[1,256,1536]{2,1,0:T(8,128)(2,1)} %param.14) | copy-start | bytes 2359300
  310.3 59.7 %copy-start.31 = (f32[256]{0:T(256)S(1)}, f32[256]{0:T(256)}, u32[]{:S(2)}) copy-start(f32[256]{0:T(256)} %copy-done.30) | copy-start | bytes 3076
  337.3 32.6 %copy-start.10 = (bf16[256,1536]{1,0:T(8,128)(2,1)S(1)}, bf16[256,1536]{1,0:T(8,128)(2,1)}, u32[]{:S(2)}) copy-start(bf16[256,1536]{1,0:T(8,128)(2,1)} %reduce-scatter.14.cloned.1.call-done) | copy-start | bytes 2359300
  368.5 27.7 %collective-permute-start = (bf16[256,1536]{1,0:T(8,128)(2,1)S(1)}, bf16[256,1536]{1,0:T(8,128)(2,1)S(1)}, u32[]{:S(2)}, u32[]{:S(2)}) collective-permute-start(bf16[256,1536]{1,0:T(8,128)(2,1)S(1)} %get-tuple-element.1050), channel_id=1, source_target_pairs={{0,2},{2,0},{1,3},{3,1},{4,6},{6,4},{5,7},{7,5},{8,10},{10,8},{9,1... | collective-permute-start | bytes 2359304 | tf_op jit(solution)/shard_map/ppermute | solution.py:20
  (16 other events, 31.0 us)
Sparse Core Ops, SparseCore 0:
  10.1 29.8 all-gather.14
  41.6 27.2 all-gather.12
  70.4 27.2 all-gather.10
  99.7 29.0 all-gather.8
  197.2 35.2 reduce-scatter.11
  242.5 39.0 reduce-scatter.17
  283.8 25.0 reduce-scatter.9
  311.2 26.0 reduce-scatter.13
  339.6 26.0 reduce-scatter.7
  368.4 26.0 reduce-scatter.19
  396.8 99.5 reduce-scatter.15
where the time goes:
time: 510 us; the launch traced here: 508 us
  waiting for transfers between devices  315 us (62%)
  matrix products  67.3 us (13%)
  local copies, waits for them, and re-layouts  59 us (12%)
  other arithmetic  34.9 us (7%)
  between operations  15.1 us (3%)
  blocking collectives  14.1 us (3%)
    reduce_scatter x1, waiting for transfers between devices, on_device(): lax.psum_scatter(jnp.stack([contract_rows(normalized_input, grad_queries)...  97 us
    reduce_scatter x1, waiting for transfers between devices, on_device(): lax.psum_scatter(kv_terms.astype(jnp.bfloat16), 'seq', scatter_dimension=...  35.4 us
    reduce_scatter x1, waiting for transfers between devices, on_device(): lax.psum_scatter(back_source.astype(jnp.bfloat16), 'tp', scatter_dimensio...  27 us
    ppermute x1, waiting for transfers between devices, passed_along(): return lax.ppermute(value, axis, pairs)  25 us
    all_gather x1, waiting for transfers between devices, on_device(): lax.all_gather(source, 'tp', axis=1, tiled=True)  24.5 us
    all_gather x1, waiting for transfers between devices, on_device(): lax.all_gather(hidden, 'tp', axis=1, tiled=True)  24.2 us
    all_gather x1, waiting for transfers between devices, on_device(): lax.all_gather(packed, 'seq', axis=0, tiled=True)  23.8 us
    reduce_scatter x1, waiting for transfers between devices, on_device(): lax.psum_scatter(contract_rows(normalized_source, key_value_gradient).ast...  23.6 us
  transfers between devices with their start and end apart: 12, of which 11 were waited for; matrix products, arithmetic and copies ran while one was open for 14% of the time, Pallas kernels for 0%

commit v1 on v0

v1 whole, which is shorter than its diff:
```python
import functools

import jax
import jax.numpy as jnp
from jax import lax
from jax.experimental import pallas as pl
from jax.experimental.pallas import tpu as pltpu
from jax.sharding import PartitionSpec as P

HEAD_DIM = 128
BLK = 128
WIN = 1024

score_scale = 40.0
norm_eps = 1e-06

F32 = jnp.float32
BF16 = jnp.bfloat16
NN = (((1,), (0,)), ((), ()))
NT = (((1,), (1,)), ((), ()))
TN = (((0,), (0,)), ((), ()))

VMEM = pl.BlockSpec(memory_space=pltpu.VMEM)
SMEM = pl.BlockSpec(memory_space=pltpu.SMEM)


def dot(left, right, dims):
    return lax.dot_general(left, right, dims, preferred_element_type=F32)


def shifted(value, axis, steps):
    count = lax.axis_size(axis)
    pairs = [(source, (source + steps) % count) for source in range(count)]
    return lax.ppermute(value, axis, pairs)


def call(body, out_shape, inputs, smem_count, flops, scratch=(), limit=40):
    moved = sum(v.size * v.dtype.itemsize for v in inputs) + sum(
        o.size * o.dtype.itemsize for o in out_shape
    )
    return pl.pallas_call(
        body,
        out_shape=out_shape,
        in_specs=[SMEM] * smem_count + [VMEM] * (len(inputs) - smem_count),
        out_specs=[VMEM] * len(out_shape),
        scratch_shapes=list(scratch),
        compiler_params=pltpu.CompilerParams(vmem_limit_bytes=limit * 1024 * 1024),
        cost_estimate=pl.CostEstimate(flops=flops, bytes_accessed=moved, transcendentals=0),
    )(*inputs)


def struct(shape, dtype):
    return jax.ShapeDtypeStruct(shape, dtype)


def offset(me, count, step, width):
    return pl.multiple_of(lax.rem(me + count - step, count) * width, width)


def normalize(pieces, me, normed_ref, factor_ref):
    count = len(pieces)
    width = pieces[0].shape[1]
    total = 0.0
    for piece in pieces:
        wide = piece[...].astype(F32)
        total = total + jnp.sum(wide * wide, axis=1, keepdims=True)
    factor = lax.rsqrt(total / (count * width) + norm_eps)
    factor_ref[...] = jnp.broadcast_to(factor, factor_ref.shape)
    for step, piece in enumerate(pieces):
        normed_ref[:, pl.ds(offset(me, count, step, width), width)] = (
            piece[...].astype(F32) * factor
        ).astype(BF16)


def unit(raw):
    return raw * lax.rsqrt(jnp.sum(raw * raw, axis=1, keepdims=True) + norm_eps)


def unit_back(raw, grad):
    scale = lax.rsqrt(jnp.sum(raw * raw, axis=1, keepdims=True) + norm_eps)
    along = jnp.sum(raw * grad, axis=1, keepdims=True)
    return scale * grad - raw * (scale * scale * scale * along)


def query_body(count, me_ref, *refs):
    pieces, (weight, normed_ref, factor_ref, unit_ref, raw_ref) = refs[:count], refs[count:]
    normalize(pieces, me_ref[0], normed_ref, factor_ref)
    for head in range(unit_ref.shape[0]):
        cols = slice(head * HEAD_DIM, (head + 1) * HEAD_DIM)
        if head % 2 == 0:
            last = min(head + 2, unit_ref.shape[0]) * HEAD_DIM
            pair = dot(normed_ref[...], weight[:, head * HEAD_DIM : last], NN)
        raw = pair[:, (head % 2) * HEAD_DIM : (head % 2 + 1) * HEAD_DIM]
        raw_ref[head] = raw
        unit_ref[head] = unit(raw).astype(BF16)


def key_body(count, me_ref, *refs):
    pieces, (weight, normed_ref, factor_ref, packed_ref, raw_ref) = refs[:count], refs[count:]
    normalize(pieces, me_ref[0], normed_ref, factor_ref)
    both = dot(normed_ref[...], weight[...], NN)
    half = both.shape[1] // 2
    for head in range(half // HEAD_DIM):
        cols = slice(head * HEAD_DIM, (head + 1) * HEAD_DIM)
        packed_ref[:, cols] = unit(both[:, cols]).astype(BF16)
    packed_ref[:, half:] = both[:, half:].astype(BF16)
    raw_ref[...] = both[:, :half]


def allowed_block(meta, block, rows):
    per = rows // BLK
    shard, self_section = meta[0], meta[1]
    shape = (rows, rows)
    row = lax.broadcasted_iota(jnp.int32, shape, 0)
    col = lax.broadcasted_iota(jnp.int32, shape, 1)
    query_doc = jnp.full(shape, meta[3 + shard * per], jnp.int32)
    key_doc = jnp.full(shape, meta[3 + block * per], jnp.int32)
    for part in range(1, per):
        query_doc = jnp.where(row >= part * BLK, meta[3 + shard * per + part], query_doc)
        key_doc = jnp.where(col >= part * BLK, meta[3 + block * per + part], key_doc)
    query_pos = shard * rows + row
    key_pos = block * rows + col
    is_self = jnp.full(shape, self_section, jnp.int32) == 1
    upper = jnp.where(is_self, query_pos, query_pos // BLK * BLK + BLK - 1)
    lower = jnp.where(is_self, query_pos - WIN, -1)
    return (query_doc == key_doc) & (key_pos <= upper) & (key_pos > lower)


def forward_body(kv_heads, meta, query_ref, kv_ref, out_ref, inverse_ref, number_ref, denom_ref):
    heads, rows, _ = query_ref.shape
    group = heads // kv_heads
    number_ref[...] = jnp.zeros_like(number_ref)
    denom_ref[...] = jnp.zeros_like(denom_ref)

    def step(block, carry):
        allowed = allowed_block(meta, block, rows)
        span = pl.ds(pl.multiple_of(block * rows, rows), rows)
        for kv_head in range(kv_heads):
            key = kv_ref[span, kv_head * HEAD_DIM : (kv_head + 1) * HEAD_DIM]
            first = (kv_heads + kv_head) * HEAD_DIM
            value = kv_ref[span, first : first + HEAD_DIM]
            for head in range(kv_head * group, (kv_head + 1) * group):
                score = dot(query_ref[head], key, NT)
                weight = jnp.where(allowed, jnp.exp(score_scale * score), 0.0)
                folded = weight[:, :HEAD_DIM]
                for part in range(1, rows // HEAD_DIM):
                    folded = folded + weight[:, part * HEAD_DIM : (part + 1) * HEAD_DIM]
                denom_ref[head] += folded
                number_ref[head] += dot(weight.astype(BF16), value, NN)
        return carry

    lax.fori_loop(meta[2], meta[0] + 1, step, 0)
    for head in range(heads):
        inverse = 1.0 / jnp.sum(denom_ref[head], axis=1, keepdims=True)
        inverse_ref[head] = jnp.broadcast_to(inverse, (rows, HEAD_DIM))
        out_ref[:, head * HEAD_DIM : (head + 1) * HEAD_DIM] = (number_ref[head] * inverse).astype(BF16)


def grad_attn_body(count, me_ref, *refs):
    pieces, (weight, full_ref, grad_ref) = refs[:count], refs[count:]
    width = pieces[0].shape[1]
    for step, piece in enumerate(pieces):
        full_ref[:, pl.ds(offset(me_ref[0], count, step, width), width)] = piece[...]
    for head in range(grad_ref.shape[0]):
        if head % 2 == 0:
            last = min(head + 2, grad_ref.shape[0]) * HEAD_DIM
            pair = dot(full_ref[...], weight[head * HEAD_DIM : last, :], NT)
        grad_ref[head] = pair[:, (head % 2) * HEAD_DIM : (head % 2 + 1) * HEAD_DIM].astype(BF16)


def backward_body(
    kv_heads, meta, query_ref, raw_ref, grad_ref, out_ref, inverse_ref, kv_ref,
    terms_ref, queries_ref, running_ref, delta_ref,
):
    heads, rows, _ = query_ref.shape
    group = heads // kv_heads
    running_ref[...] = jnp.zeros_like(running_ref)
    terms_ref[...] = jnp.zeros_like(terms_ref)
    for head in range(heads):
        product = grad_ref[head].astype(F32) * out_ref[
            :, head * HEAD_DIM : (head + 1) * HEAD_DIM
        ].astype(F32)
        delta_ref[head] = jnp.broadcast_to(jnp.sum(product, axis=1, keepdims=True), (rows, HEAD_DIM))

    def step(block, carry):
        allowed = allowed_block(meta, block, rows)
        span = pl.ds(pl.multiple_of(block * rows, rows), rows)
        for kv_head in range(kv_heads):
            key = kv_ref[span, kv_head * HEAD_DIM : (kv_head + 1) * HEAD_DIM]
            first = (kv_heads + kv_head) * HEAD_DIM
            value = kv_ref[span, first : first + HEAD_DIM]
            grad_key = jnp.zeros((rows, HEAD_DIM), F32)
            grad_value = jnp.zeros((rows, HEAD_DIM), F32)
            for head in range(kv_head * group, (kv_head + 1) * group):
                score = dot(query_ref[head], key, NT)
                probs = jnp.where(
                    allowed, jnp.exp(score_scale * score) * inverse_ref[head][:, :1], 0.0
                )
                grad_probs = dot(grad_ref[head], value, NT)
                grad_scores = (probs * (grad_probs - delta_ref[head][:, :1])).astype(BF16)
                running_ref[head] += dot(grad_scores, key, NN)
                grad_key = grad_key + dot(grad_scores, query_ref[head], TN)
                grad_value = grad_value + dot(probs.astype(BF16), grad_ref[head], TN)
            terms_ref[span, kv_head * HEAD_DIM : (kv_head + 1) * HEAD_DIM] = (
                score_scale * grad_key
            ).astype(BF16)
            terms_ref[span, first : first + HEAD_DIM] = grad_value.astype(BF16)
        return carry

    lax.fori_loop(meta[2], meta[0] + 1, step, 0)
    for head in range(heads):
        queries_ref[:, head * HEAD_DIM : (head + 1) * HEAD_DIM] = unit_back(
            raw_ref[head], score_scale * running_ref[head]
        ).astype(BF16)


def key_grad_body(raw_ref, grad_ref, out_ref):
    half = raw_ref.shape[1]
    for first in range(0, half, HEAD_DIM):
        cols = slice(first, first + HEAD_DIM)
        out_ref[:, cols] = unit_back(raw_ref[:, cols], grad_ref[:, cols].astype(F32)).astype(BF16)
    out_ref[:, half:] = grad_ref[:, half:]


def split_body(count, transposed, dotted, me_ref, left_ref, weight_ref, *refs):
    pieces = refs[:count] if dotted else ()
    refs = refs[len(pieces) :]
    outs = refs[:count]
    width = outs[0].shape[1]
    total = 0.0
    for step in list(range(1, count)) + [0]:
        span = pl.ds(offset(me_ref[0], count, step, width), width)
        if transposed:
            part = dot(left_ref[...], weight_ref[span, :], NT).astype(BF16)
        else:
            part = dot(left_ref[...], weight_ref[:, span], NN).astype(BF16)
        outs[step][...] = part
        if dotted:
            total = total + jnp.sum(
                part.astype(F32) * pieces[step][...].astype(F32), axis=1, keepdims=True
            )
    if dotted:
        refs[count][...] = jnp.broadcast_to(total, refs[count].shape)


def on_device(
    h_in,
    memory,
    cotangent,
    block_docs,
    w_query,
    w_out,
    self_key_value_weight,
    cache_key_value_weight,
):
    section_id = lax.axis_index("section")
    section_count = lax.axis_size("section")
    shard_id = lax.axis_index("seq")
    tp_id = lax.axis_index("tp")
    tp_count = lax.axis_size("tp")
    self_section = section_id == 0
    hidden = h_in[0]
    grad_local = cotangent[0]
    source = jnp.where(self_section, hidden, memory[0])

    def gathered(own):
        return [own] + [shifted(own, "tp", step) for step in range(1, tp_count)]

    source_pieces = gathered(source)
    hidden_pieces = gathered(hidden)
    grad_pieces = gathered(grad_local)

    rows, width = hidden.shape
    model = width * tp_count
    per = rows // BLK
    query_weight = w_query[0]
    out_weight = w_out[0]
    kv_weight = jnp.where(self_section, self_key_value_weight, cache_key_value_weight)
    kv_cols = self_key_value_weight.shape[2]
    kv_heads = kv_cols // HEAD_DIM
    query_cols = query_weight.shape[1]
    heads = query_cols // HEAD_DIM
    kv_flat = kv_weight.reshape(model, 2 * kv_cols)
    me = tp_id.astype(jnp.int32).reshape(1)

    all_docs = lax.all_gather(block_docs[0], "seq", axis=0, tiled=True)
    first_doc = lax.dynamic_slice_in_dim(all_docs, shard_id * per, 1)[0]
    first_block = jnp.sum((all_docs < first_doc).astype(jnp.int32)) // per
    window_block = jnp.maximum(shard_id * rows - WIN + 1, 0) // rows
    first_block = jnp.where(self_section, jnp.maximum(first_block, window_block), first_block)
    meta = jnp.concatenate(
        [
            jnp.stack([shard_id, self_section.astype(jnp.int32), first_block]).astype(jnp.int32),
            all_docs,
        ]
    )

    source_normed, source_factor, packed, key_raw = call(
        functools.partial(key_body, tp_count),
        [
            struct((rows, model), BF16),
            struct((rows, HEAD_DIM), F32),
            struct((rows, 2 * kv_cols), BF16),
            struct((rows, kv_cols), F32),
        ],
        [me, *source_pieces, kv_flat],
        1,
        2 * rows * model * 2 * kv_cols,
    )
    all_kv = lax.all_gather(packed, "seq", axis=0, tiled=True)
    length = all_kv.shape[0]

    normed, row_factor, query_unit, query_raw = call(
        functools.partial(query_body, tp_count),
        [
            struct((rows, model), BF16),
            struct((rows, HEAD_DIM), F32),
            struct((heads, rows, HEAD_DIM), BF16),
            struct((heads, rows, HEAD_DIM), F32),
        ],
        [me, *hidden_pieces, query_weight],
        1,
        2 * rows * model * query_cols,
    )
    attn_flat, inverse = call(
        functools.partial(forward_body, kv_heads),
        [struct((rows, query_cols), BF16), struct((heads, rows, HEAD_DIM), F32)],
        [meta, query_unit, all_kv],
        1,
        4 * rows * length * query_cols,
        [pltpu.VMEM((heads, rows, HEAD_DIM), F32)] * 2,
    )
    grad_rows, grad_attn = call(
        functools.partial(grad_attn_body, tp_count),
        [struct((rows, model), BF16), struct((heads, rows, HEAD_DIM), BF16)],
        [me, *grad_pieces, out_weight],
        1,
        2 * rows * model * query_cols,
    )
    kv_terms, grad_queries = call(
        functools.partial(backward_body, kv_heads),
        [struct((length, 2 * kv_cols), BF16), struct((rows, query_cols), BF16)],
        [meta, query_unit, query_raw, grad_attn, attn_flat, inverse, all_kv],
        1,
        10 * rows * length * query_cols,
        [pltpu.VMEM((heads, rows, HEAD_DIM), F32)] * 2,
    )

    def summed(parts):
        total = parts[0].astype(F32)
        for step in range(1, tp_count):
            total = total + shifted(parts[step], "tp", -step).astype(F32)
        return total

    def summed_dot(value):
        own = value[:, 0]
        total = own
        for step in range(1, tp_count):
            total = total + shifted(own, "tp", step)
        return total

    pieces_out = [struct((rows, width), BF16)] * tp_count
    projected = summed(
        call(
            functools.partial(split_body, tp_count, False, False),
            pieces_out,
            [me, attn_flat, out_weight],
            1,
            2 * rows * model * query_cols,
        )
    )
    h_out = (hidden.astype(F32) + projected).astype(BF16)
    passed = shifted(h_out, "section", 1)

    kv_grads = lax.psum_scatter(kv_terms, "seq", scatter_dimension=0, tiled=True)

    *rows_parts, row_dot = call(
        functools.partial(split_body, tp_count, True, True),
        pieces_out + [struct((rows, HEAD_DIM), F32)],
        [me, grad_queries, query_weight, *hidden_pieces],
        1,
        2 * rows * model * query_cols,
    )
    rows_part = summed(rows_parts)
    row_total = summed_dot(row_dot)
    hidden_wide = hidden.astype(F32)
    factor = row_factor[:, 0]
    grad_input = (
        grad_local.astype(F32)
        + factor[:, None] * rows_part
        - hidden_wide * (factor * factor * factor * row_total / model)[:, None]
    )

    (kv_grad,) = call(
        key_grad_body, [struct((rows, 2 * kv_cols), BF16)], [key_raw, kv_grads], 0, rows * kv_cols
    )
    *source_parts, source_dot = call(
        functools.partial(split_body, tp_count, True, True),
        pieces_out + [struct((rows, HEAD_DIM), F32)],
        [me, kv_grad, kv_flat, *source_pieces],
        1,
        4 * rows * model * kv_cols,
    )
    source_part = summed(source_parts)
    source_total = summed_dot(source_dot)
    source_wide = source.astype(F32)
    src = source_factor[:, 0]
    grad_memory = (
        src[:, None] * source_part
        - source_wide * (src * src * src * source_total / model)[:, None]
    )

    def over_tokens(left, right):
        return lax.psum_scatter(
            dot(left, right, TN).astype(BF16), "seq", scatter_dimension=0, tiled=True
        )

    out_share = over_tokens(grad_rows, attn_flat).astype(F32)
    query_share = over_tokens(normed, grad_queries).astype(F32)
    kv_share = over_tokens(source_normed, kv_grad)

    share_rows = kv_share.shape[0] // section_count
    own = lax.dynamic_slice_in_dim(kv_share, section_id * share_rows, share_rows, 0)
    self_grad = jnp.where(self_section, own, 0.0).astype(F32)
    cache_grad = jnp.where(self_section, 0.0, own).astype(F32)
    for step in range(1, section_count):
        target = lax.rem(section_id + step, section_count)
        piece = lax.dynamic_slice_in_dim(kv_share, target * share_rows, share_rows, 0)
        came = shifted(piece, "section", step).astype(F32)
        from_self = section_id == step
        self_grad = self_grad + jnp.where(from_self, came, 0.0)
        cache_grad = cache_grad + jnp.where(from_self, 0.0, came)
    return (
        passed[None],
        grad_input.astype(BF16)[None],
        grad_memory.astype(BF16)[None],
        query_share[None],
        out_share.T[None],
        self_grad.reshape(share_rows, 2, kv_cols),
        cache_grad.reshape(share_rows, 2, kv_cols),
    )


def solution(mesh):
    return jax.shard_map(
        on_device,
        mesh=mesh,
        in_specs=(
            P("section", "seq", "tp"),
            P("section", "seq", "tp"),
            P("section", "seq", "tp"),
            P("section", "seq"),
            P("section", None, "tp"),
            P("section", "tp", None),
            P(None, None, "tp"),
            P(None, None, "tp"),
        ),
        out_specs=(
            P("section", "seq", "tp"),
            P("section", "seq", "tp"),
            P("section", "seq", "tp"),
            P("section", "seq", "tp"),
            P("section", "tp", "seq"),
            P(("seq", "section"), None, "tp"),
            P(("seq", "section"), None, "tp"),
        ),
        check_vma=False,
    )
```

time: 510 us -> 310 us (0.61)
  waiting for transfers between devices: 315 us -> 176 us
  matrix products: 67.3 us -> 14.4 us
  Pallas kernels: 0 us -> 22.8 us
  other arithmetic: 34.9 us -> 13.9 us
  local copies, waits for them, and re-layouts: 59 us -> 38.5 us
  starting transfers between devices: 1.93 us -> 14.3 us
    reduce_scatter x7 -> x4, waiting for transfers between devices: 213 us -> 113 us  [the longest x3 69.7 us: over_tokens(): lax.psum_scatter(dot(left, right, TN).astype(BF16), 'seq', scatter_dimens...]
    all_gather x4 -> x1, waiting for transfers between devices: 75.9 us -> 0.01 us  [on_device(): all_kv = lax.all_gather(packed, 'seq', axis=0, tiled=True)]
    dot_general x37 -> x3, matrix products: 67.3 us -> 14.4 us  [dot(): return lax.dot_general(left, right, dims, preferred_element_type=F32)]
    ppermute x1 -> x10, waiting for transfers between devices: 25 us -> 62.6 us  [shifted(): return lax.ppermute(value, axis, pairs)]
    pallas_call x0 -> x9, Pallas kernels: none -> 22.8 us  [call(): pl.pallas_call(body, out_shape=out_shape, in_specs=[SMEM] * smem_count +...]
    unnamed x84 -> x79, local copies, waits for them, and re-layouts: 17 us -> 34.2 us
    ppermute x1 -> x10, starting transfers between devices: 1.48 us -> 13.9 us  [shifted(): return lax.ppermute(value, axis, pairs)]
    dynamic_slice x20 -> x1, local copies, waits for them, and re-layouts: 12.6 us -> 1.01 us  [on_device(): lax.dynamic_slice_in_dim(kv_share, target * share_rows, share_rows, 0)]
  transfers between devices with their start and end apart: 12 -> 15, of which waited for: 11 -> 9; matrix products, arithmetic and copies ran while one was open for 14% -> 10% of each run, Pallas kernels for 0% -> 5%
where the time goes in v1:
time: 310 us; the launch traced here: 307 us
  waiting for transfers between devices  176 us (57%)
  local copies, waits for them, and re-layouts  38.5 us (12%)
  Pallas kernels  22.8 us (7%)
  between operations  17.3 us (6%)
  matrix products  14.4 us (5%)
  starting transfers between devices  14.3 us (5%)
  other arithmetic  13.9 us (4%)
  blocking collectives  9.53 us (3%)
    reduce_scatter x3, waiting for transfers between devices, over_tokens(): lax.psum_scatter(dot(left, right, TN).astype(BF16), 'seq', scatter_dimens...  69.7 us
    ppermute x10, waiting for transfers between devices, shifted(): return lax.ppermute(value, axis, pairs)  62.6 us
    reduce_scatter x1, waiting for transfers between devices, on_device(): lax.psum_scatter(kv_terms, 'seq', scatter_dimension=0, tiled=True)  43.4 us
    unnamed x79, local copies, waits for them, and re-layouts  34.2 us
    pallas_call x9, Pallas kernels, call(): pl.pallas_call(body, out_shape=out_shape, in_specs=[SMEM] * smem_count +...  22.8 us
    dot_general x3, matrix products, dot(): return lax.dot_general(left, right, dims, preferred_element_type=F32)  14.4 us
    ppermute x10, starting transfers between devices, shifted(): return lax.ppermute(value, axis, pairs)  13.9 us
    all_gather x1, blocking collectives, on_device(): all_docs = lax.all_gather(block_docs[0], 'seq', axis=0, tiled=True)  9.53 us
  transfers between devices with their start and end apart: 15, of which 9 were waited for; matrix products, arithmetic and copies ran while one was open for 10% of the time, Pallas kernels for 5%

profile of v1, /device:TPU:0, one launch (start us, length us, event | category | flops | bytes accessed | tf_op | source)
XLA Modules:
  0.0 306.5 jit_solution(7902484313857359486)
XLA Ops:
  7.2 2.3 bitcast_select_fusion.refs_0_
  9.6 2.9 collective-permute-start.1
  12.5 2.2 broadcast_select_fusion
  15.4 15.0 %collective-permute-done.1.refs_1_ = bf16[256,1536]{1,0:T(8,128)(2,1)} collective-permute-done((bf16[256,1536]{1,0:T(8,128)(2,1)}, bf16[256,1536]{1,0:T(8,128)(2,1)}, u32[]{:S(2)}, u32[]{:S(2)}) %collective-permute-start.1) | collective-permute-done | bytes 786464 | tf_op jit(solution)/shard_map/ppermute | solution.py:34
  30.4 3.7 %shard_map.136 = (bf16[256,3072]{1,0:T(8,128)(2,1)S(1)}, f32[256,128]{1,0:T(8,128)S(1)}, bf16[256,512]{1,0:T(8,128)(2,1)}, f32[256,256]{1,0:T(8,128)S(1)}) custom-call(s32[1]{0:T(128)} %bitcast.1.me_ref, bf16[256,1536]{1,0:T(8,128)(2,1)} %bitcast_select_fusion.refs_0_, bf16[256,1536]{1,0:T(8,128)(2,1)} %collective-permute-done.1.refs_1_, ...), custom_call_target="tpu_custom_call" | custom-call | flops 805306368 | bytes 6946820 | tf_op jit(solution)/shard_map/pallas_call | solution.py:41
  36.7 1.8 collective-permute-start.4
  40.1 9.5 %all-reduce = s32[16]{0:T(128)S(1)} all-reduce(s32[16]{0:T(128)S(1)} %bitcast_dynamic-update-slice_fusion), channel_id=2, replica_groups=mesh['seq'=8,'section'=2,'tp'=2] {'seq'}, use_global_device_ids=true, to_apply=%add | all-reduce | flops 16 | bytes 128 | tf_op jit(solution)/shard_map/all_gather | solution.py:286
  54.2 3.3 %collective-permute-done.4.refs_1_ = bf16[256,1536]{1,0:T(8,128)(2,1)} collective-permute-done((bf16[256,1536]{1,0:T(8,128)(2,1)}, bf16[256,1536]{1,0:T(8,128)(2,1)}, u32[]{:S(2)}, u32[]{:S(2)}) %collective-permute-start.4) | collective-permute-done | bytes 786464 | tf_op jit(solution)/shard_map/ppermute | solution.py:34
  57.5 2.4 copy-done.2
  61.1 2.7 shard_map.139
  65.8 6.9 %collective-permute-done.refs_1_ = bf16[256,1536]{1,0:T(8,128)(2,1)} collective-permute-done((bf16[256,1536]{1,0:T(8,128)(2,1)}, bf16[256,1536]{1,0:T(8,128)(2,1)}, u32[]{:S(2)}, u32[]{:S(2)}) %collective-permute-start) | collective-permute-done | bytes 786464 | tf_op jit(solution)/shard_map/ppermute | solution.py:34
  72.7 2.3 copy-done
  75.0 3.3 %shard_map.135 = (bf16[256,3072]{1,0:T(8,128)(2,1)S(1)}, f32[256,128]{1,0:T(8,128)S(1)}, bf16[6,256,128]{2,1,0:T(8,128)(2,1)S(1)}, f32[6,256,128]{2,1,0:T(8,128)S(1)}) custom-call(s32[1]{0:T(128)} %bitcast.1.me_ref, bf16[256,1536]{1,0:T(8,128)(2,1)S(1)} %bitcast.48, bf16[256,1536]{1,0:T(8,128)(2,1)} %collective-permute-done.refs_1_, ...), custom_call_target="tpu_custom_call" | custom-call | flops 1207959552 | bytes 9175044 | tf_op jit(solution)/shard_map/pallas_call | solution.py:41
  84.3 1.8 shard_map.137
  86.2 3.5 %shard_map.140 = (bf16[2048,512]{1,0:T(8,128)(2,1)S(1)}, bf16[256,768]{1,0:T(8,128)(2,1)S(1)}) custom-call(s32[19]{0:T(128)S(1)} %pad_add_fusion.meta, bf16[6,256,128]{2,1,0:T(8,128)(2,1)S(1)} %copy-done.32, f32[6,256,128]{2,1,0:T(8,128)S(1)} %copy-done.27, bf16[6,256,128]{2,1,0:T(8,128)(2,1)S(1)} %copy-done.29, ...), custom_call_target="tpu_custom_call" | custom-call | flops 4026531840 | bytes 7340108 | tf_op jit(solution)/shard_map/pallas_call | solution.py:41
  92.0 5.0 %convolution_convert_fusion = bf16[3072,768]{1,0:T(8,128)(2,1)} fusion(bf16[256,3072]{1,0:T(8,128)(2,1)} %copy-done.8, bf16[256,768]{1,0:T(8,128)(2,1)S(1)} %get-tuple-element.31.left_ref.out_ref), kind=kOutput, calls=%fused_computation.1 | convolution fusion | flops 1210318848 | bytes 6684672 | tf_op jit(solution)/shard_map/dot_general | solution.py:28
  97.1 43.4 %reduce-scatter.5.cloned.1.call-done.grad_ref = bf16[256,512]{1,0:T(8,128)(2,1)} async-done(((bf16[2048,512]{1,0:T(8,128)(2,1)}), bf16[256,512]{1,0:T(8,128)(2,1)}) %reduce-scatter.5.cloned.1.call-update) | async-done | bytes 262160 | tf_op jit(solution)/shard_map/reduce_scatter | solution.py:375
  142.7 4.1 %convolution_convert_fusion.2 = bf16[3072,512]{1,0:T(8,128)(2,1)} fusion(bf16[256,3072]{1,0:T(8,128)(2,1)} %copy-done.6, bf16[256,512]{1,0:T(8,128)(2,1)S(1)} %shard_map.142.left_ref), kind=kOutput, calls=%fused_computation.3 | convolution fusion | flops 806879232 | bytes 4980736 | tf_op jit(solution)/shard_map/dot_general | solution.py:28
  146.9 5.3 %convolution_convert_fusion.1 = bf16[3072,768]{1,0:T(8,128)(2,1)} fusion(bf16[256,3072]{1,0:T(8,128)(2,1)} %copy-done.7, bf16[256,768]{1,0:T(8,128)(2,1)} %copy-done.14), kind=kOutput, calls=%fused_computation.2 | convolution fusion | flops 1210318848 | bytes 6684672 | tf_op jit(solution)/shard_map/dot_general | solution.py:28
  152.2 2.4 copy-done.1
  156.7 2.8 shard_map.141
  161.1 2.4 copy-done.3
  167.3 25.4 %collective-permute-done.6 = f32[256]{0:T(256)S(1)} collective-permute-done((f32[256]{0:T(256)S(1)}, f32[256]{0:T(256)S(1)}, u32[]{:S(2)}, u32[]{:S(2)}) %collective-permute-start.6) | collective-permute-done | bytes 1056 | tf_op jit(solution)/shard_map/ppermute | solution.py:34
  192.8 1.9 fusion.4
  196.1 3.4 %shard_map.143 = (bf16[256,1536]{1,0:T(8,128)(2,1)S(1)}, bf16[256,1536]{1,0:T(8,128)(2,1)}, f32[256,128]{1,0:T(8,128)S(1)}) custom-call(s32[1]{0:T(128)} %bitcast.1.me_ref, bf16[256,512]{1,0:T(8,128)(2,1)S(1)} %shard_map.142.left_ref, bf16[3072,512]{1,0:T(8,128)(2,1)S(1)} %bitcast.42, bf16[256,1536]{1,0:T(8,128)(2,1)} %bitcast_select_fusion.refs_0_, ...), custom_call_target="tpu_custom_call" | custom-call | flops 805306368 | bytes 6684676 | tf_op jit(solution)/shard_map/pallas_call | solution.py:41
  204.2 6.2 %collective-permute-done.3 = bf16[256,1536]{1,0:T(8,128)(2,1)} collective-permute-done((bf16[256,1536]{1,0:T(8,128)(2,1)}, bf16[256,1536]{1,0:T(8,128)(2,1)}, u32[]{:S(2)}, u32[]{:S(2)}) %collective-permute-start.3) | collective-permute-done | bytes 786464 | tf_op jit(solution)/shard_map/ppermute | solution.py:34
  210.4 5.8 %collective-permute-done.8 = f32[256]{0:T(256)S(1)} collective-permute-done((f32[256]{0:T(256)S(1)}, f32[256]{0:T(256)S(1)}, u32[]{:S(2)}, u32[]{:S(2)}) %collective-permute-start.8) | collective-permute-done | bytes 1056 | tf_op jit(solution)/shard_map/ppermute | solution.py:34
  216.2 2.7 fusion.3
  221.4 16.0 %reduce-scatter.11.cloned.1.call-done = bf16[384,512]{1,0:T(8,128)(2,1)} async-done(((bf16[3072,512]{1,0:T(8,128)(2,1)}), bf16[384,512]{1,0:T(8,128)(2,1)}) %reduce-scatter.11.cloned.1.call-update) | async-done | bytes 393232 | tf_op jit(solution)/shard_map/reduce_scatter | solution.py:414
  240.0 53.7 %reduce-scatter.7.cloned.1.call-done = bf16[384,768]{1,0:T(8,128)(2,1)} async-done(((bf16[3072,768]{1,0:T(8,128)(2,1)}), bf16[384,768]{1,0:T(8,128)(2,1)}) %reduce-scatter.7.cloned.1.call-update) | async-done | bytes 589840 | tf_op jit(solution)/shard_map/reduce_scatter | solution.py:414
  293.7 2.2 bitcast_convert_fusion
  297.9 2.1 copy.20
  (113 shorter events, 40.9 us)
Async XLA Ops:
  7.2 74.6 %all-gather.3.cloned.1.call-start = ((), (), s32[]{:S(2)}) async-start(), calls=%async_computation.4 | async-start | bytes 2359296 | tf_op jit(solution)/shard_map/all_gather | solution.py:310
  9.6 20.8 %collective-permute-start.1 = (bf16[256,1536]{1,0:T(8,128)(2,1)}, bf16[256,1536]{1,0:T(8,128)(2,1)}, u32[]{:S(2)}, u32[]{:S(2)}) collective-permute-start(bf16[256,1536]{1,0:T(8,128)(2,1)} %bitcast_select_fusion.refs_0_), channel_id=1, source_target_pairs={{0,1},{1,0},{2,3},{3,2},{4,5},{5,4},{6,7},{7,6},{8,9},{9,8},{10,11... | collective-permute-start | bytes 2359304 | tf_op jit(solution)/shard_map/ppermute | solution.py:34
  30.3 8.4 %copy-start.35 = (u32[32]{0:T(128)S(1)}, u32[32]{0:T(128)}, u32[]{:S(2)}) copy-start(u32[32]{0:T(128)} %constant.72) | copy-start | bytes 388
  30.3 9.7 %copy-start.34 = (s32[1,2]{1,0:T(1,128)S(1)}, s32[1,2]{1,0:T(1,128)}, u32[]{:S(2)}) copy-start(s32[1,2]{1,0:T(1,128)} %param.11) | copy-start | bytes 28
  36.6 103.9 %reduce-scatter.5.cloned.1.call-start = ((), (), s32[]{:S(2)}) async-start(), calls=%async_computation.5 | async-start | bytes 2359296 | tf_op jit(solution)/shard_map/reduce_scatter | solution.py:375
  36.7 20.9 %collective-permute-start.4 = (bf16[256,1536]{1,0:T(8,128)(2,1)}, bf16[256,1536]{1,0:T(8,128)(2,1)}, u32[]{:S(2)}, u32[]{:S(2)}) collective-permute-start(bf16[256,1536]{1,0:T(8,128)(2,1)} %bitcast.50), channel_id=1, source_target_pairs={{0,1},{1,0},{2,3},{3,2},{4,5},{5,4},{6,7},{7,6},{8,9},{9,8},{10,11... | collective-permute-start | bytes 2359304 | tf_op jit(solution)/shard_map/ppermute | solution.py:34
  38.5 34.2 %collective-permute-start = (bf16[256,1536]{1,0:T(8,128)(2,1)}, bf16[256,1536]{1,0:T(8,128)(2,1)}, u32[]{:S(2)}, u32[]{:S(2)}) collective-permute-start(bf16[256,1536]{1,0:T(8,128)(2,1)} %bitcast.47), channel_id=1, source_target_pairs={{0,1},{1,0},{2,3},{3,2},{4,5},{5,4},{6,7},{7,6},{8,9},{9,8},{10,11... | collective-permute-start | bytes 2359304 | tf_op jit(solution)/shard_map/ppermute | solution.py:34
  57.5 2.4 copy-start.2
  61.1 11.6 %copy-start.4 = (bf16[1,256,1536]{2,1,0:T(8,128)(2,1)S(1)}, bf16[1,256,1536]{2,1,0:T(8,128)(2,1)}, u32[]{:S(2)}) copy-start(bf16[1,256,1536]{2,1,0:T(8,128)(2,1)} %param.8) | copy-start | bytes 2359300
  72.7 2.3 copy-start
  81.7 1.6 copy-start.25
  84.3 1.8 copy-start.27
  84.3 1.8 copy-start.29
  84.3 1.8 copy-start.32
  86.1 5.9 %copy-start.12 = (bf16[256,768]{1,0:T(8,128)(2,1)}, bf16[256,768]{1,0:T(8,128)(2,1)S(1)}, u32[]{:S(2)}) copy-start(bf16[256,768]{1,0:T(8,128)(2,1)S(1)} %get-tuple-element.31.left_ref.out_ref) | copy-start | bytes 1179652
  91.8 127.1 %reduce-scatter.9.cloned.1.call-start = ((), (), s32[]{:S(2)}) async-start(), calls=%async_computation.7 | async-start | bytes 5308416 | tf_op jit(solution)/shard_map/reduce_scatter | solution.py:414
  97.1 140.4 %reduce-scatter.11.cloned.1.call-start = ((), (), s32[]{:S(2)}) async-start(), calls=%async_computation.8 | async-start | bytes 3538944 | tf_op jit(solution)/shard_map/reduce_scatter | solution.py:414
  146.8 146.9 %reduce-scatter.7.cloned.1.call-start = ((), (), s32[]{:S(2)}) async-start(), calls=%async_computation.6 | async-start | bytes 5308416 | tf_op jit(solution)/shard_map/reduce_scatter | solution.py:414
  152.2 2.4 copy-start.1
  156.7 4.4 %copy-start.13 = (bf16[256,768]{1,0:T(8,128)(2,1)S(1)}, bf16[256,768]{1,0:T(8,128)(2,1)}, u32[]{:S(2)}) copy-start(bf16[256,768]{1,0:T(8,128)(2,1)} %copy-done.12) | copy-start | bytes 1179652
  159.5 33.3 %collective-permute-start.5 = (bf16[256,1536]{1,0:T(8,128)(2,1)S(1)}, bf16[256,1536]{1,0:T(8,128)(2,1)S(1)}, u32[]{:S(2)}, u32[]{:S(2)}) collective-permute-start(bf16[256,1536]{1,0:T(8,128)(2,1)S(1)} %get-tuple-element.40), channel_id=1, source_target_pairs={{0,1},{1,0},{2,3},{3,2},{4,5},{5,4},{6,7},{7,6},{8,9},{9,8},{10,11... | collective-permute-start | bytes 2359304 | tf_op jit(solution)/shard_map/ppermute | solution.py:34
  161.1 2.4 copy-start.3
  163.5 3.7 %copy-start.23 = (f32[256,128]{1,0:T(8,128)S(1)}, f32[256,128]{1,0:T(8,128)}, u32[]{:S(2)}) copy-start(f32[256,128]{1,0:T(8,128)} %copy-done.22) | copy-start | bytes 393220
  163.5 29.3 %copy-start.10 = (bf16[1,256,1536]{2,1,0:T(8,128)(2,1)S(1)}, bf16[1,256,1536]{2,1,0:T(8,128)(2,1)}, u32[]{:S(2)}) copy-start(bf16[1,256,1536]{2,1,0:T(8,128)(2,1)} %param.10) | copy-start | bytes 2359300
  164.9 27.8 %collective-permute-start.2 = (bf16[256,1536]{1,0:T(8,128)(2,1)S(1)}, bf16[256,1536]{1,0:T(8,128)(2,1)S(1)}, u32[]{:S(2)}, u32[]{:S(2)}) collective-permute-start(bf16[256,1536]{1,0:T(8,128)(2,1)S(1)} %get-tuple-element.33), channel_id=1, source_target_pairs={{0,1},{1,0},{2,3},{3,2},{4,5},{5,4},{6,7},{7,6},{8,9},{9,8},{10,11... | collective-permute-start | bytes 2359304 | tf_op jit(solution)/shard_map/ppermute | solution.py:34
  165.6 27.2 %collective-permute-start.6 = (f32[256]{0:T(256)S(1)}, f32[256]{0:T(256)S(1)}, u32[]{:S(2)}, u32[]{:S(2)}) collective-permute-start(f32[256]{0:T(256)S(1)} %slice_reduce_fusion.2), channel_id=1, source_target_pairs={{0,1},{1,0},{2,3},{3,2},{4,5},{5,4},{6,7},{7,6},{8,9},{9,8},{10,11... | collective-permute-start | bytes 3080 | tf_op jit(solution)/shard_map/ppermute | solution.py:34
  194.7 9.5 %copy-start.21 = (f32[256,128]{1,0:T(8,128)S(1)}, f32[256,128]{1,0:T(8,128)}, u32[]{:S(2)}) copy-start(f32[256,128]{1,0:T(8,128)} %copy-done.20) | copy-start | bytes 393220
  194.7 15.7 %collective-permute-start.3 = (bf16[256,1536]{1,0:T(8,128)(2,1)}, bf16[256,1536]{1,0:T(8,128)(2,1)}, u32[]{:S(2)}, u32[]{:S(2)}) collective-permute-start(bf16[256,1536]{1,0:T(8,128)(2,1)} %get-tuple-element.66), channel_id=1, source_target_pairs={{0,2},{2,0},{1,3},{3,1},{4,6},{6,4},{5,7},{7,5},{8,10},{10,8},{9,1... | collective-permute-start | bytes 2359304 | tf_op jit(solution)/shard_map/ppermute | solution.py:34
  201.0 15.2 %collective-permute-start.7 = (bf16[256,1536]{1,0:T(8,128)(2,1)}, bf16[256,1536]{1,0:T(8,128)(2,1)S(1)}, u32[]{:S(2)}, u32[]{:S(2)}) collective-permute-start(bf16[256,1536]{1,0:T(8,128)(2,1)} %get-tuple-element.46), channel_id=1, source_target_pairs={{0,1},{1,0},{2,3},{3,2},{4,5},{5,4},{6,7},{7,6},{8,9},{9,8},{10,11... | collective-permute-start | bytes 2359304 | tf_op jit(solution)/shard_map/ppermute | solution.py:34
  203.6 12.6 %collective-permute-start.8 = (f32[256]{0:T(256)S(1)}, f32[256]{0:T(256)S(1)}, u32[]{:S(2)}, u32[]{:S(2)}) collective-permute-start(f32[256]{0:T(256)S(1)} %slice_reduce_fusion), channel_id=1, source_target_pairs={{0,1},{1,0},{2,3},{3,2},{4,5},{5,4},{6,7},{7,6},{8,9},{9,8},{10,11... | collective-permute-start | bytes 3080 | tf_op jit(solution)/shard_map/ppermute | solution.py:34
  237.5 58.4 %copy-start.33 = (bf16[384,512]{1,0:T(8,128)(2,1)S(1)}, bf16[384,512]{1,0:T(8,128)(2,1)}, u32[]{:S(2)}) copy-start(bf16[384,512]{1,0:T(8,128)(2,1)} %reduce-scatter.11.cloned.1.call-done) | copy-start | bytes 1179652
  238.5 57.3 %collective-permute-start.9 = (bf16[192,512]{1,0:T(8,128)(2,1)S(1)}, bf16[192,512]{1,0:T(8,128)(2,1)S(1)}, u32[]{:S(2)}, u32[]{:S(2)}) collective-permute-start(bf16[192,512]{1,0:T(8,128)(2,1)S(1)} %constant_dynamic-slice_fusion), channel_id=1, source_target_pairs={{0,2},{2,0},{1,3},{3,1},{4,6},{6,4},{5,7},{7,5},{8,10},{10,8},{9,1... | collective-permute-start | bytes 589832 | tf_op jit(solution)/shard_map/ppermute | solution.py:34
  (19 other events, 17.8 us)
Sparse Core Ops, SparseCore 0:
  36.8 30.6 all-gather.2
  91.9 48.5 reduce-scatter.4
  142.8 53.6 reduce-scatter.8
  198.7 38.6 reduce-scatter.10
  239.6 54.0 reduce-scatter.6

commit v2 on v1

v2 whole, which is shorter than its diff:
```python
import functools
import math

import jax
import jax.numpy as jnp
from jax import lax
from jax.experimental import pallas as pl
from jax.experimental.pallas import tpu as pltpu
from jax.sharding import PartitionSpec as P

HEAD_DIM = 128
BLK = 128
WIN = 1024

score_scale = 40.0
norm_eps = 1e-06
log2_e = math.log2(math.e)

F32 = jnp.float32
BF16 = jnp.bfloat16
NN = (((1,), (0,)), ((), ()))
NT = (((1,), (1,)), ((), ()))
TN = (((0,), (0,)), ((), ()))

VMEM = pl.BlockSpec(memory_space=pltpu.VMEM)
SMEM = pl.BlockSpec(memory_space=pltpu.SMEM)


def dot(left, right, dims):
    return lax.dot_general(left, right, dims, preferred_element_type=F32)


def shifted(value, axis, steps):
    count = lax.axis_size(axis)
    pairs = [(source, (source + steps) % count) for source in range(count)]
    return lax.ppermute(value, axis, pairs)


def call(
    body, out_shape, inputs, smem_count, flops, scratch=(), limit=60, after=(),
    grid=(), in_specs=None, out_specs=None,
):
    moved = sum(v.size * v.dtype.itemsize for v in inputs) + sum(
        o.size * o.dtype.itemsize for o in out_shape
    )
    if in_specs is None:
        in_specs = [SMEM] * smem_count + [VMEM] * (len(inputs) - smem_count)
    if out_specs is None:
        out_specs = [VMEM] * len(out_shape)

    def with_order(*refs):
        body(*refs[: len(inputs)], *refs[len(inputs) + len(after) :])

    return pl.pallas_call(
        with_order,
        out_shape=out_shape,
        grid=grid,
        in_specs=list(in_specs) + [pl.BlockSpec(memory_space=pl.ANY)] * len(after),
        out_specs=out_specs,
        scratch_shapes=list(scratch),
        compiler_params=pltpu.CompilerParams(vmem_limit_bytes=limit * 1024 * 1024),
        cost_estimate=pl.CostEstimate(flops=flops, bytes_accessed=moved, transcendentals=0),
    )(*inputs, *after)


def struct(shape, dtype):
    return jax.ShapeDtypeStruct(shape, dtype)


def offset(me, count, step, width):
    return pl.multiple_of(lax.rem(me + count - step, count) * width, width)


def normalize(pieces, me, normed_ref, factor_ref):
    count = len(pieces)
    width = pieces[0].shape[1]
    total = 0.0
    for piece in pieces:
        wide = piece[...].astype(F32)
        total = total + jnp.sum(wide * wide, axis=1, keepdims=True)
    factor = lax.rsqrt(total / (count * width) + norm_eps)
    factor_ref[...] = jnp.broadcast_to(factor, factor_ref.shape)
    for step, piece in enumerate(pieces):
        normed_ref[:, pl.ds(offset(me, count, step, width), width)] = (
            piece[...].astype(F32) * factor
        ).astype(BF16)


def unit(raw):
    return raw * lax.rsqrt(jnp.sum(raw * raw, axis=1, keepdims=True) + norm_eps)


def unit_back(raw, grad):
    scale = lax.rsqrt(jnp.sum(raw * raw, axis=1, keepdims=True) + norm_eps)
    along = jnp.sum(raw * grad, axis=1, keepdims=True)
    return scale * grad - raw * (scale * scale * scale * along)


def query_body(count, me_ref, *refs):
    pieces, (weight, normed_ref, factor_ref, unit_ref, raw_ref) = refs[:count], refs[count:]

    @pl.when(pl.program_id(0) == 0)
    def first():
        normalize(pieces, me_ref[0], normed_ref, factor_ref)

    both = dot(normed_ref[...], weight[...], NN)
    for head in range(unit_ref.shape[0]):
        raw = both[:, head * HEAD_DIM : (head + 1) * HEAD_DIM]
        raw_ref[head] = raw
        unit_ref[head] = unit(raw).astype(BF16)


def key_body(count, me_ref, *refs):
    pieces, (weight, normed_ref, factor_ref, packed_ref, raw_ref) = refs[:count], refs[count:]
    normalize(pieces, me_ref[0], normed_ref, factor_ref)
    both = dot(normed_ref[...], weight[...], NN)
    half = both.shape[1] // 2
    for head in range(half // HEAD_DIM):
        cols = slice(head * HEAD_DIM, (head + 1) * HEAD_DIM)
        packed_ref[:, cols] = unit(both[:, cols]).astype(BF16)
    packed_ref[:, half:] = both[:, half:].astype(BF16)
    raw_ref[...] = both[:, :half]


def allowed_block(meta, block, rows):
    per = rows // BLK
    shard, self_section = meta[0], meta[1]
    shape = (rows, rows)
    query = lax.broadcasted_iota(jnp.int32, shape, 0)
    key = lax.broadcasted_iota(jnp.int32, shape, 1)
    query_doc = jnp.full(shape, meta[3 + shard * per], jnp.int32)
    key_doc = jnp.full(shape, meta[3 + block * per], jnp.int32)
    for part in range(1, per):
        query_doc = jnp.where(query >= part * BLK, meta[3 + shard * per + part], query_doc)
        key_doc = jnp.where(key >= part * BLK, meta[3 + block * per + part], key_doc)
    query_pos = shard * rows + query
    key_pos = block * rows + key
    is_self = jnp.full(shape, self_section, jnp.int32) == 1
    upper = jnp.where(is_self, query_pos, query_pos // BLK * BLK + BLK - 1)
    lower = jnp.where(is_self, query_pos - WIN, -1)
    return (query_doc == key_doc) & (key_pos <= upper) & (key_pos > lower)


def key_value(kv_ref, span, kv_head, kv_heads):
    first = (kv_heads + kv_head) * HEAD_DIM
    key = kv_ref[span, kv_head * HEAD_DIM : (kv_head + 1) * HEAD_DIM]
    return key, kv_ref[span, first : first + HEAD_DIM]


def forward_body(kv_heads, meta, query_ref, kv_ref, out_ref, log_ref, number_ref, denom_ref):
    heads, rows, _ = query_ref.shape
    group = heads // kv_heads
    stacked = (group * rows, HEAD_DIM)
    number_ref[...] = jnp.zeros_like(number_ref)
    denom_ref[...] = jnp.zeros_like(denom_ref)

    def step(block, carry):
        allowed = allowed_block(meta, block, rows)
        span = pl.ds(pl.multiple_of(block * rows, rows), rows)
        for kv_head in range(kv_heads):
            mine = slice(kv_head * group, (kv_head + 1) * group)
            key, value = key_value(kv_ref, span, kv_head, kv_heads)
            score = dot(query_ref[mine].reshape(stacked), key, NT).reshape(group, rows, rows)
            weight = jnp.where(allowed[None], jnp.exp2(score * (score_scale * log2_e)), 0.0)
            folded = weight[:, :, :HEAD_DIM]
            for first in range(HEAD_DIM, rows, HEAD_DIM):
                folded = folded + weight[:, :, first : first + HEAD_DIM]
            denom_ref[mine] += folded
            product = dot(weight.astype(BF16).reshape(group * rows, rows), value, NN)
            number_ref[mine] += product.reshape(group, rows, HEAD_DIM)
        return carry

    lax.fori_loop(meta[2], meta[0] + 1, step, 0)
    for head in range(heads):
        denom = jnp.sum(denom_ref[head], axis=1, keepdims=True)
        log_ref[head] = jnp.broadcast_to(jnp.log2(denom), (rows, HEAD_DIM))
        out_ref[:, head * HEAD_DIM : (head + 1) * HEAD_DIM] = (number_ref[head] / denom).astype(BF16)


def rows_body(count, me_ref, *refs):
    width = refs[0].shape[1]
    for step, piece in enumerate(refs[:count]):
        refs[-1][:, pl.ds(offset(me_ref[0], count, step, width), width)] = piece[...]


def whole_rows(pieces, me, after):
    rows, width = pieces[0].shape
    (out,) = call(
        functools.partial(rows_body, len(pieces)),
        [struct((rows, width * len(pieces)), BF16)],
        [me, *pieces],
        1,
        0,
        after=after,
    )
    return out


def grad_attn_body(rows_ref, weight, grad_ref):
    both = dot(rows_ref[...], weight[...], NT)
    for head in range(grad_ref.shape[0]):
        grad_ref[head] = both[:, head * HEAD_DIM : (head + 1) * HEAD_DIM].astype(BF16)


def backward_body(
    kv_heads, meta, query_ref, raw_ref, grad_ref, out_ref, log_ref, kv_ref,
    keep_ref, *refs,
):
    *send_refs, queries_ref, running_ref, delta_ref = refs
    heads, rows, _ = query_ref.shape
    group = heads // kv_heads
    stacked = (group * rows, HEAD_DIM)
    running_ref[...] = jnp.zeros_like(running_ref)
    keep_ref[...] = jnp.zeros_like(keep_ref)
    for send_ref in send_refs:
        send_ref[...] = jnp.zeros_like(send_ref)
    for head in range(heads):
        cols = slice(head * HEAD_DIM, (head + 1) * HEAD_DIM)
        product = grad_ref[head].astype(F32) * out_ref[:, cols].astype(F32)
        delta_ref[head] = jnp.broadcast_to(jnp.sum(product, axis=1, keepdims=True), (rows, HEAD_DIM))

    def widened(ref, mine):
        return jnp.concatenate([ref[mine].reshape(stacked)] * (rows // HEAD_DIM), axis=1)

    def step(block, carry):
        allowed = allowed_block(meta, block, rows)
        span = pl.ds(pl.multiple_of(block * rows, rows), rows)
        for kv_head in range(kv_heads):
            mine = slice(kv_head * group, (kv_head + 1) * group)
            key, value = key_value(kv_ref, span, kv_head, kv_heads)
            query = query_ref[mine].reshape(stacked)
            grad = grad_ref[mine].reshape(stacked)
            score = dot(query, key, NT)
            probs = jnp.exp2(score * (score_scale * log2_e) - widened(log_ref, mine))
            probs = jnp.where(allowed[None], probs.reshape(group, rows, rows), 0.0)
            probs = probs.reshape(group * rows, rows)
            grad_probs = dot(grad, value, NT)
            grad_scores = (probs * (grad_probs - widened(delta_ref, mine))).astype(BF16)
            running_ref[mine] += dot(grad_scores, key, NN).reshape(group, rows, HEAD_DIM)
            key_term = (score_scale * dot(grad_scores, query, TN)).astype(BF16)
            value_term = dot(probs.astype(BF16), grad, TN).astype(BF16)
            low = kv_head * HEAD_DIM
            high = (kv_heads + kv_head) * HEAD_DIM

            steps = meta[0] // 2 - block // 2
            same_core = block % 2 == meta[0] % 2

            @pl.when(same_core)
            def own():
                keep_ref[steps, :, low : low + HEAD_DIM] = key_term
                keep_ref[steps, :, high : high + HEAD_DIM] = value_term

            for place, send_ref in enumerate(send_refs):

                def other(send_ref=send_ref):
                    send_ref[:, low : low + HEAD_DIM] = key_term
                    send_ref[:, high : high + HEAD_DIM] = value_term

                pl.when(jnp.logical_not(same_core) & (steps == place))(other)
        return carry

    lax.fori_loop(meta[2], meta[0] + 1, step, 0)
    for head in range(heads):
        queries_ref[:, head * HEAD_DIM : (head + 1) * HEAD_DIM] = unit_back(
            raw_ref[head], score_scale * running_ref[head]
        ).astype(BF16)


CHUNKS = 1


def chunked(rows):
    return CHUNKS if rows % (16 * CHUNKS) == 0 else 1


def split(count, transposed, me, left, weight_ref, pieces, outs, dot_ref):
    own_ref, sent = outs[0], outs[1:]
    rows, width = own_ref.shape
    parts = len(sent) // max(count - 1, 1)
    total = 0.0
    for step in list(range(1, count)) + [0]:
        span = pl.ds(offset(me, count, step, width), width)
        if transposed:
            part = dot(left, weight_ref[span, :], NT).astype(BF16)
        else:
            part = dot(left, weight_ref[:, span], NN).astype(BF16)
        if step == 0:
            own_ref[...] = part
        else:
            tall = rows // parts
            for index in range(parts):
                sent[(step - 1) * parts + index][...] = part[index * tall : (index + 1) * tall]
        if dot_ref is not None:
            total = total + jnp.sum(
                part.astype(F32) * pieces[step][...].astype(F32), axis=1, keepdims=True
            )
    if dot_ref is not None:
        dot_ref[...] = jnp.broadcast_to(total, dot_ref.shape)


def split_shapes(rows, width, count):
    parts = chunked(rows)
    return [struct((rows, width), BF16)] + [struct((rows // parts, width), BF16)] * (
        parts * (count - 1)
    )


def sent_over_tp(outs, rows):
    parts = chunked(rows)
    return [shifted(out, "tp", -(1 + index // parts)) for index, out in enumerate(outs[1:])]


def project_body(count, me_ref, left_ref, weight_ref, *outs):
    split(count, False, me_ref[0], left_ref[...], weight_ref, None, outs, None)


def back_body(count, me_ref, left_ref, weight_ref, *refs):
    pieces, outs, dot_ref = refs[:count], refs[count:-1], refs[-1]
    split(count, True, me_ref[0], left_ref[...], weight_ref, pieces, outs, dot_ref)


def key_back_body(count, terms, me_ref, raw_ref, weight_ref, *refs):
    term_refs, refs = refs[:terms], refs[terms:]
    pieces, outs, dot_ref, grad_ref = refs[:count], refs[count:-2], refs[-2], refs[-1]
    half = raw_ref.shape[1]
    total = term_refs[0][...].astype(F32)
    for term in term_refs[1:]:
        total = total + term[...].astype(F32)
    for first in range(0, half, HEAD_DIM):
        cols = slice(first, first + HEAD_DIM)
        grad_ref[:, cols] = unit_back(raw_ref[:, cols], total[:, cols]).astype(BF16)
    grad_ref[:, half:] = total[:, half:].astype(BF16)
    split(count, True, me_ref[0], grad_ref[...], weight_ref, pieces, outs, dot_ref)


def summed(own_ref, came, at):
    rows = own_ref.shape[0]
    parts = chunked(rows)
    tall = rows // parts
    total = own_ref[at * tall : (at + 1) * tall].astype(F32)
    for ref in came[at::parts]:
        total = total + ref[...].astype(F32)
    return total, slice(at * tall, (at + 1) * tall)


def output_body(hidden_ref, own_ref, *refs):
    came, out_ref = refs[:-1], refs[-1]
    for at in range(chunked(own_ref.shape[0])):
        total, span = summed(own_ref, came, at)
        out_ref[span] = (hidden_ref[span].astype(F32) + total).astype(BF16)


def input_body(count, residual, model, *refs):
    base, refs = (refs[0], refs[1:]) if residual else (None, refs)
    values_ref, factor_ref, own_ref, *refs = refs
    dots, came, out_ref = refs[:count], refs[count:-1], refs[-1]
    for at in range(chunked(own_ref.shape[0])):
        total, span = summed(own_ref, came, at)
        dot_total = dots[0][span, :1]
        for ref in dots[1:]:
            dot_total = dot_total + ref[span, :1]
        factor = factor_ref[span, :1]
        grad = factor * total - values_ref[span].astype(F32) * (
            factor * factor * factor * dot_total / model
        )
        if residual:
            grad = grad + base[span].astype(F32)
        out_ref[span] = grad.astype(BF16)


def flipped_bits(value, count):
    out, left = 0, count
    while left > 1:
        out = out * 2 + value % 2
        value, left = value // 2, left // 2
    return out


def tokens_body(at_ref, left_ref, right_ref, keep_ref, *send_refs):
    both = dot(left_ref[...], right_ref[...], TN).astype(BF16)
    half = both.shape[0] // 2

    @pl.when(at_ref[0] == 0)
    def low():
        keep_ref[0] = both[:half]

    @pl.when(at_ref[0] == 1)
    def high():
        keep_ref[0] = both[half:]

    for place, send_ref in enumerate(send_refs):

        @pl.when((at_ref[0] == 0) & (pl.program_id(0) == place))
        def low_sent(send_ref=send_ref):
            send_ref[...] = both[half:]

        @pl.when((at_ref[0] == 1) & (pl.program_id(0) == place))
        def high_sent(send_ref=send_ref):
            send_ref[...] = both[:half]


def ordered(body, inputs, after, outs, grid, in_specs, out_specs, scalars):
    kept = 1 + len(inputs)

    def with_order(*refs):
        body(*refs[:kept], *refs[kept + len(after) :])

    return pl.pallas_call(
        with_order,
        out_shape=outs,
        grid_spec=pltpu.PrefetchScalarGridSpec(
            num_scalar_prefetch=1,
            grid=grid,
            in_specs=in_specs + [pl.BlockSpec(memory_space=pl.ANY)] * len(after),
            out_specs=out_specs,
        ),
        compiler_params=pltpu.CompilerParams(vmem_limit_bytes=60 * 1024 * 1024),
        cost_estimate=pl.CostEstimate(flops=0, bytes_accessed=1024, transcendentals=0),
    )(scalars, *inputs, *after)


def over_tokens(left, right, after=()):
    rows, model = left.shape
    chips = lax.axis_size("seq") // 2
    step = model // chips
    cols = right.shape[1]
    shard = lax.axis_index("seq").astype(jnp.int32)
    near = jnp.stack(
        [shard % 2]
        + [lax.bitwise_xor(shard // 2, jnp.int32(flipped_bits(i, chips))) for i in range(chips)]
    )
    share = (step // 2, cols)
    keep, *send = ordered(
        tokens_body,
        [left, right],
        after,
        [struct((chips, *share), BF16)] + [struct(share, BF16)] * chips,
        (chips,),
        [
            pl.BlockSpec((rows, step), lambda i, at: (0, at[1 + i])),
            pl.BlockSpec(right.shape, lambda i, at: (0, 0)),
        ],
        [pl.BlockSpec((1, *share), lambda i, at: (i, 0, 0))]
        + [pl.BlockSpec(share, lambda i, at: (0, 0))] * chips,
        near,
    )
    return keep, send


def add_body(count, at_ref, *refs):
    out_ref = refs[-1]
    for index in range(count):
        total = refs[0][index].astype(F32) + refs[1 + index][...].astype(F32)
        for ref in refs[1 + count : -1]:
            total = total + ref[index].astype(F32)
        out_ref[index] = total.astype(out_ref.dtype)


def added(keep, came, terms, first, count, dtype, after):
    rows, cols = keep.shape[1:]
    block = pl.BlockSpec((count, rows, cols), lambda i, at: (first // count, 0, 0))
    flat = pl.BlockSpec((rows, cols), lambda i, at: (0, 0))
    (out,) = ordered(
        functools.partial(add_body, count),
        [keep, *came[first : first + count], *terms],
        after,
        [struct((count, rows, cols), dtype)],
        (1,),
        [block] + [flat] * count + [block] * len(terms),
        [pl.BlockSpec((count, rows, cols), lambda i, at: (0, 0, 0))],
        jnp.zeros((1,), jnp.int32),
    )
    return out


def whole_body(left_ref, right_ref, out_ref):
    out_ref[...] = dot(left_ref[...], right_ref[...], TN).astype(BF16)


def scattered(left, right, after=()):
    rows, model = left.shape
    step = math.gcd(model, 512)
    cols = right.shape[1]
    (partial,) = call(
        whole_body,
        [struct((model, cols), BF16)],
        [left, right],
        0,
        2 * rows * model * cols,
        after=after,
        grid=(model // step,),
        in_specs=[
            pl.BlockSpec((rows, step), lambda i: (0, i)),
            pl.BlockSpec(right.shape, lambda i: (0, 0)),
        ],
        out_specs=[pl.BlockSpec((step, cols), lambda i: (i, 0))],
    )
    return lax.psum_scatter(partial, "seq", scatter_dimension=0, tiled=True), partial


def core_swap(value):
    count = lax.axis_size("seq")
    return lax.ppermute(value, "seq", [(shard, shard ^ 1) for shard in range(count)])


def chip_sum_body(count, keep_ref, *refs):
    for index in range(count):
        total = keep_ref[index].astype(F32) + refs[index][...].astype(F32)
        refs[count + index][...] = total.astype(BF16)


def sums_below(keep, came, after):
    chips, rows, cols = keep.shape
    sums = call(
        functools.partial(chip_sum_body, chips),
        [struct((rows, cols), BF16)] * chips,
        [keep, *came],
        0,
        2 * keep.size,
        after=after,
    )
    terms = [sums[0]]
    for steps in range(1, chips):
        pairs = [(shard, shard - 2 * steps) for shard in range(2 * steps, 2 * chips)]
        terms.append(lax.ppermute(sums[steps], "seq", pairs))
    return terms, sums[0]


class Halving:
    def __init__(self, keep, send):
        self.keep = keep
        self.came = [core_swap(piece) for piece in send]
        self.terms = []
        self.count = keep.shape[0]
        self.distance = 2

    def step(self, after):
        self.count //= 2
        sent = added(self.keep, self.came, self.terms, self.count, self.count, BF16, after)
        pairs = [(shard, shard ^ self.distance) for shard in range(lax.axis_size("seq"))]
        self.terms.append(lax.ppermute(sent, "seq", pairs))
        self.distance *= 2
        return sent

    def last(self, after):
        return added(self.keep, self.came, self.terms, 0, 1, F32, after)[0]


def on_device(
    h_in,
    memory,
    cotangent,
    block_docs,
    w_query,
    w_out,
    self_key_value_weight,
    cache_key_value_weight,
):
    section_id = lax.axis_index("section")
    section_count = lax.axis_size("section")
    shard_id = lax.axis_index("seq")
    tp_id = lax.axis_index("tp")
    tp_count = lax.axis_size("tp")
    self_section = section_id == 0
    hidden = h_in[0]
    grad_local = cotangent[0]
    source = jnp.where(self_section, hidden, memory[0])

    def gathered(own):
        return [own] + [shifted(own, "tp", step) for step in range(1, tp_count)]

    source_pieces = gathered(source)
    hidden_pieces = gathered(hidden)
    grad_pieces = gathered(grad_local)

    rows, width = hidden.shape
    model = width * tp_count
    per = rows // BLK
    query_weight = w_query[0]
    out_weight = w_out[0]
    kv_weight = jnp.where(self_section, self_key_value_weight, cache_key_value_weight)
    kv_cols = self_key_value_weight.shape[2]
    kv_heads = kv_cols // HEAD_DIM
    query_cols = query_weight.shape[1]
    heads = query_cols // HEAD_DIM
    kv_flat = kv_weight.reshape(model, 2 * kv_cols)
    me = tp_id.astype(jnp.int32).reshape(1)

    all_docs = lax.all_gather(block_docs[0], "seq", axis=0, tiled=True)
    first_doc = lax.dynamic_slice_in_dim(all_docs, shard_id * per, 1)[0]
    first_block = jnp.sum((all_docs < first_doc).astype(jnp.int32)) // per
    window_block = jnp.maximum(shard_id * rows - WIN + 1, 0) // rows
    first_block = jnp.where(self_section, jnp.maximum(first_block, window_block), first_block)
    meta = jnp.concatenate(
        [
            jnp.stack([shard_id, self_section.astype(jnp.int32), first_block]).astype(jnp.int32),
            all_docs,
        ]
    )

    source_normed, source_factor, packed, key_raw = call(
        functools.partial(key_body, tp_count),
        [
            struct((rows, model), BF16),
            struct((rows, HEAD_DIM), F32),
            struct((rows, 2 * kv_cols), BF16),
            struct((rows, kv_cols), F32),
        ],
        [me, *source_pieces, kv_flat],
        1,
        2 * rows * model * 2 * kv_cols,
        after=[meta],
    )
    all_kv = lax.all_gather(packed, "seq", axis=0, tiled=True)
    length = all_kv.shape[0]
    chips = length // rows // 2

    together = 2 if heads % 2 == 0 else 1
    whole = pl.BlockSpec((rows, width), lambda i: (0, 0))
    full = pl.BlockSpec((rows, model), lambda i: (0, 0))
    per_head = pl.BlockSpec((together, rows, HEAD_DIM), lambda i: (i, 0, 0))
    normed, row_factor, query_unit, query_raw = call(
        functools.partial(query_body, tp_count),
        [
            struct((rows, model), BF16),
            struct((rows, HEAD_DIM), F32),
            struct((heads, rows, HEAD_DIM), BF16),
            struct((heads, rows, HEAD_DIM), F32),
        ],
        [me, *hidden_pieces, query_weight],
        1,
        2 * rows * model * query_cols,
        after=[packed],
        grid=(heads // together,),
        in_specs=[SMEM]
        + [whole] * tp_count
        + [pl.BlockSpec((model, together * HEAD_DIM), lambda i: (0, i))],
        out_specs=[
            full,
            pl.BlockSpec((rows, HEAD_DIM), lambda i: (0, 0)),
            per_head,
            per_head,
        ],
    )
    attn_flat, log_denom = call(
        functools.partial(forward_body, kv_heads),
        [struct((rows, query_cols), BF16), struct((heads, rows, HEAD_DIM), F32)],
        [meta, query_unit, all_kv],
        1,
        4 * rows * length * query_cols,
        [pltpu.VMEM((heads, rows, HEAD_DIM), F32)] * 2,
    )
    grad_rows = whole_rows(grad_pieces, me, [attn_flat])
    out_share, mark = scattered(grad_rows, attn_flat)
    (grad_attn,) = call(
        grad_attn_body,
        [struct((heads, rows, HEAD_DIM), BF16)],
        [grad_rows, out_weight],
        0,
        2 * rows * model * query_cols,
        after=[mark],
        grid=(heads // together,),
        in_specs=[full]
        + [pl.BlockSpec((together * HEAD_DIM, model), lambda i: (i, 0))],
        out_specs=[per_head],
    )
    halves = [struct((chips, rows, 2 * kv_cols), BF16)] + [
        struct((rows, 2 * kv_cols), BF16)
    ] * chips
    keep, *send, grad_queries = call(
        functools.partial(backward_body, kv_heads),
        halves + [struct((rows, query_cols), BF16)],
        [meta, query_unit, query_raw, grad_attn, attn_flat, log_denom, all_kv],
        1,
        10 * rows * length * query_cols,
        [pltpu.VMEM((heads, rows, HEAD_DIM), F32)] * 2,
        after=[mark],
    )
    kv_came = [core_swap(piece) for piece in send]
    query_share, mark = scattered(normed, grad_queries)
    kv_sums, mark = sums_below(keep, kv_came, [mark])

    def dots(value):
        return [value] + [shifted(value, "tp", step) for step in range(1, tp_count)]

    wide = struct((rows, width), BF16)
    broad = struct((rows, HEAD_DIM), F32)
    shapes = split_shapes(rows, width, tp_count)
    projected = call(
        functools.partial(project_body, tp_count),
        shapes,
        [me, attn_flat, out_weight],
        1,
        2 * rows * model * query_cols,
        after=[mark],
    )
    projected_came = sent_over_tp(projected, rows)
    *rows_parts, row_dot = call(
        functools.partial(back_body, tp_count),
        shapes + [broad],
        [me, grad_queries, query_weight, *hidden_pieces],
        1,
        2 * rows * model * query_cols,
        after=[projected[0]],
    )
    rows_came = sent_over_tp(rows_parts, rows)
    row_dots = dots(row_dot)
    *source_parts, source_dot, kv_grad = call(
        functools.partial(key_back_body, tp_count, chips),
        shapes + [broad, struct((rows, 2 * kv_cols), BF16)],
        [me, key_raw, kv_flat, *kv_sums, *source_pieces],
        1,
        4 * rows * model * kv_cols,
        after=[row_dot],
    )
    source_came = sent_over_tp(source_parts, rows)
    source_dots = dots(source_dot)
    kv_keep, kv_send = over_tokens(source_normed, kv_grad)
    kv_sum = Halving(kv_keep, kv_send)
    (h_out,) = call(
        output_body, [wide], [hidden, projected[0], *projected_came], 0, 0, after=[kv_keep]
    )
    passed = shifted(h_out, "section", 1)
    mark = h_out
    while kv_sum.count > 2:
        mark = kv_sum.step([mark])
    (grad_input,) = call(
        functools.partial(input_body, tp_count, True, model),
        [wide],
        [grad_local, hidden, row_factor, rows_parts[0], *row_dots, *rows_came],
        0,
        0,
        after=[mark],
    )
    mark = kv_sum.step([grad_input])
    (grad_memory,) = call(
        functools.partial(input_body, tp_count, False, model),
        [wide],
        [source, source_factor, source_parts[0], *source_dots, *source_came],
        0,
        0,
        after=[mark],
    )
    kv_share = kv_sum.last([grad_memory])

    share_rows = kv_share.shape[0] // section_count
    own = lax.dynamic_slice_in_dim(kv_share, section_id * share_rows, share_rows, 0)
    self_grad = jnp.where(self_section, own, 0.0)
    cache_grad = jnp.where(self_section, 0.0, own)
    for step in range(1, section_count):
        target = lax.rem(section_id + step, section_count)
        piece = lax.dynamic_slice_in_dim(kv_share, target * share_rows, share_rows, 0)
        came = shifted(piece.astype(BF16), "section", step).astype(F32)
        from_self = section_id == step
        self_grad = self_grad + jnp.where(from_self, came, 0.0)
        cache_grad = cache_grad + jnp.where(from_self, 0.0, came)
    return (
        passed[None],
        grad_input[None],
        grad_memory[None],
        query_share.astype(F32)[None],
        out_share.astype(F32).T[None],
        self_grad.reshape(share_rows, 2, kv_cols),
        cache_grad.reshape(share_rows, 2, kv_cols),
    )


def solution(mesh):
    return jax.shard_map(
        on_device,
        mesh=mesh,
        in_specs=(
            P("section", "seq", "tp"),
            P("section", "seq", "tp"),
            P("section", "seq", "tp"),
            P("section", "seq"),
            P("section", None, "tp"),
            P("section", "tp", None),
            P(None, None, "tp"),
            P(None, None, "tp"),
        ),
        out_specs=(
            P("section", "seq", "tp"),
            P("section", "seq", "tp"),
            P("section", "seq", "tp"),
            P("section", "seq", "tp"),
            P("section", "tp", "seq"),
            P(("seq", "section"), None, "tp"),
            P(("seq", "section"), None, "tp"),
        ),
        check_vma=False,
    )
```

time: 310 us -> 271 us (0.87)
  waiting for transfers between devices: 176 us -> 113 us
  Pallas kernels: 22.8 us -> 81.2 us
  local copies, waits for them, and re-layouts: 38.5 us -> 22 us
  matrix products: 14.4 us -> 0 us
  other arithmetic: 13.9 us -> 9.93 us
    reduce_scatter x4 -> x2, waiting for transfers between devices: 113 us -> 0.01 us  [scattered(): lax.psum_scatter(partial, 'seq', scatter_dimension=0, tiled=True)]
    pallas_call x9 -> x19, Pallas kernels: 22.8 us -> 81.2 us  [the longest x15 68.3 us: call(): pl.pallas_call(with_order, out_shape=out_shape, grid=grid, in_specs=list(...]
    ppermute x0 -> x13, waiting for transfers between devices: none -> 53.2 us  [the longest x3 34.6 us: sums_below(): terms.append(lax.ppermute(sums[steps], 'seq', pairs))]
    unnamed x79 -> x73, local copies, waits for them, and re-layouts: 34.2 us -> 18.4 us
    dot_general x3 -> x0, matrix products: 14.4 us -> none  [dot(): return lax.dot_general(left, right, dims, preferred_element_type=F32)]
    ppermute x0 -> x13, starting transfers between devices: none -> 5.51 us  [the longest x3 4.05 us: sums_below(): terms.append(lax.ppermute(sums[steps], 'seq', pairs))]
    broadcast_in_dim x4 -> x2, other arithmetic: 7.86 us -> 3.3 us  [the longest x1 2.15 us: on_device(): query_share.astype(F32)[None]]
  transfers between devices with their start and end apart: 15 -> 26, of which waited for: 9 -> 13; matrix products, arithmetic and copies ran while one was open for 10% -> 6% of each run, Pallas kernels for 5% -> 25%
where the time goes in v2:
time: 271 us; the launch traced here: 270 us
  waiting for transfers between devices  113 us (42%)
  Pallas kernels  81.2 us (30%)
  local copies, waits for them, and re-layouts  22 us (8%)
  starting transfers between devices  17.4 us (6%)
  between operations  17.3 us (6%)
  other arithmetic  9.93 us (4%)
  blocking collectives  9.17 us (3%)
    pallas_call x15, Pallas kernels, call(): pl.pallas_call(with_order, out_shape=out_shape, grid=grid, in_specs=list(...  68.3 us
    ppermute x10, waiting for transfers between devices, shifted(): return lax.ppermute(value, axis, pairs)  59.6 us
    ppermute x3, waiting for transfers between devices, sums_below(): terms.append(lax.ppermute(sums[steps], 'seq', pairs))  34.6 us
    unnamed x73, local copies, waits for them, and re-layouts  18.4 us
    ppermute x2, waiting for transfers between devices, step(): self.terms.append(lax.ppermute(sent, 'seq', pairs))  16.8 us
    pallas_call x4, Pallas kernels, ordered(): pl.pallas_call(with_order, out_shape=outs, grid_spec=pltpu.PrefetchScalar...  13 us
    ppermute x10, starting transfers between devices, shifted(): return lax.ppermute(value, axis, pairs)  11.8 us
    all_gather x1, blocking collectives, on_device(): all_docs = lax.all_gather(block_docs[0], 'seq', axis=0, tiled=True)  9.17 us
  transfers between devices with their start and end apart: 26, of which 13 were waited for; matrix products, arithmetic and copies ran while one was open for 6% of the time, Pallas kernels for 25%

profile of v2, /device:TPU:0, one launch (start us, length us, event | category | flops | bytes accessed | tf_op | source)
XLA Modules:
  0.0 269.9 jit_solution(10713413176022513770)
XLA Ops:
  8.7 3.0 %collective-permute-start.1 = (bf16[256,1536]{1,0:T(8,128)(2,1)S(1)}, bf16[256,1536]{1,0:T(8,128)(2,1)S(1)}, u32[]{:S(2)}, u32[]{:S(2)}) collective-permute-start(bf16[256,1536]{1,0:T(8,128)(2,1)S(1)} %bitcast_select_fusion.refs_1_.refs_7_.refs_0_), channel_id=1, source_target_pairs={{0,1},{1,0},{2,3},{3,2},{4,5},{5,4},{6,7},{7,6},{8,9},{9,8},{10,11... | collective-permute-start | bytes 2359304 | tf_op jit(solution)/shard_map/ppermute | solution.py:36
  14.3 9.2 %all-reduce = s32[16]{0:T(128)S(1)} all-reduce(s32[16]{0:T(128)S(1)} %bitcast_dynamic-update-slice_fusion), channel_id=2, replica_groups=mesh['seq'=8,'section'=2,'tp'=2] {'seq'}, use_global_device_ids=true, to_apply=%add | all-reduce | flops 16 | bytes 128 | tf_op jit(solution)/shard_map/all_gather | solution.py:589
  28.0 2.2 broadcast_select_fusion
  30.2 2.3 copy.16
  34.0 4.6 %shard_map.135 = (bf16[256,3072]{1,0:T(8,128)(2,1)}, f32[256,128]{1,0:T(8,128)}, bf16[256,512]{1,0:T(8,128)(2,1)}, f32[256,256]{1,0:T(8,128)}) custom-call(s32[1]{0:T(128)} %bitcast.1.refs_0_, bf16[256,1536]{1,0:T(8,128)(2,1)} %copy-done.1, bf16[256,1536]{1,0:T(8,128)(2,1)} %copy-done.2, bf16[3072,512]{1,0:T(8,128)(2,1)} %bitcast.41, ...), custom_call_target="tpu_custom_call" | custom-call | flops 805306368 | bytes 6946820 | tf_op jit(solution)/shard_map/pallas_call | solution.py:54
  40.8 18.5 %collective-permute-done.refs_2_.refs_4_ = bf16[256,1536]{1,0:T(8,128)(2,1)S(1)} collective-permute-done((bf16[256,1536]{1,0:T(8,128)(2,1)S(1)}, bf16[256,1536]{1,0:T(8,128)(2,1)S(1)}, u32[]{:S(2)}, u32[]{:S(2)}) %collective-permute-start) | collective-permute-done | bytes 786464 | tf_op jit(solution)/shard_map/ppermute | solution.py:36
  60.2 6.2 %shard_map.136 = (bf16[256,3072]{1,0:T(8,128)(2,1)}, f32[256,128]{1,0:T(8,128)}, bf16[6,256,128]{2,1,0:T(8,128)(2,1)}, f32[6,256,128]{2,1,0:T(8,128)}) custom-call(s32[1]{0:T(128)} %bitcast.1.refs_0_, bf16[256,1536]{1,0:T(8,128)(2,1)} %bitcast.43, bf16[256,1536]{1,0:T(8,128)(2,1)} %copy-done.6, bf16[3072,768]{1,0:T(8,128)(2,1)} %bitcast.50, ...), custom_call_target="tpu_custom_call" | custom-call | flops 1207959552 | bytes 9175044 | tf_op jit(solution)/shard_map/pallas_call | solution.py:54
  66.4 3.9 %shard_map.137 = (bf16[256,768]{1,0:T(8,128)(2,1)}, f32[6,256,128]{2,1,0:T(8,128)}) custom-call(s32[19]{0:T(128)} %pad_add_fusion.refs_4_.refs_0_, bf16[6,256,128]{2,1,0:T(8,128)(2,1)} %get-tuple-element.42.refs_1_, bf16[2048,512]{1,0:T(8,128)(2,1)} %all-gather.3.cloned.1.call-done.refs_2_.refs_6_), custom_call_target="tpu_custom_call" | custom-call | flops 1610612736 | bytes 3670092 | tf_op jit(solution)/shard_map/pallas_call | solution.py:54
  70.3 3.4 %collective-permute-done.2.refs_2_ = bf16[256,1536]{1,0:T(8,128)(2,1)S(1)} collective-permute-done((bf16[256,1536]{1,0:T(8,128)(2,1)S(1)}, bf16[256,1536]{1,0:T(8,128)(2,1)S(1)}, u32[]{:S(2)}, u32[]{:S(2)}) %collective-permute-start.2) | collective-permute-done | bytes 786464 | tf_op jit(solution)/shard_map/ppermute | solution.py:36
  74.6 2.7 %shard_map.138.refs_0_ = bf16[256,3072]{1,0:T(8,128)(2,1)} custom-call(s32[1]{0:T(128)} %bitcast.1.refs_0_, bf16[256,1536]{1,0:T(8,128)(2,1)} %bitcast.56, bf16[256,1536]{1,0:T(8,128)(2,1)} %copy-done.9, bf16[256,768]{1,0:T(8,128)(2,1)} %get-tuple-element.43.refs_3_.refs_1_.refs_4_), custom_call_target="tpu_custom_call" | custom-call | bytes 3145732 | tf_op jit(solution)/shard_map/pallas_call | solution.py:54
  77.3 6.4 %shard_map.139.refs_2_.refs_7_ = bf16[3072,768]{1,0:T(8,128)(2,1)} custom-call(bf16[256,3072]{1,0:T(8,128)(2,1)} %shard_map.138.refs_0_, bf16[256,768]{1,0:T(8,128)(2,1)} %get-tuple-element.43.refs_3_.refs_1_.refs_4_), custom_call_target="tpu_custom_call" | custom-call | flops 1207959552 | bytes 6684672 | tf_op jit(solution)/shard_map/pallas_call | solution.py:54
  83.7 5.2 %shard_map.140.refs_3_ = bf16[6,256,128]{2,1,0:T(8,128)(2,1)} custom-call(bf16[256,3072]{1,0:T(8,128)(2,1)} %shard_map.138.refs_0_, bf16[768,3072]{1,0:T(8,128)(2,1)} %bitcast.48, bf16[3072,768]{1,0:T(8,128)(2,1)} %shard_map.139.refs_2_.refs_7_), custom_call_target="tpu_custom_call" | custom-call | flops 1207959552 | bytes 6684672 | tf_op jit(solution)/shard_map/pallas_call | solution.py:54
  88.9 5.9 %shard_map.141 = (bf16[4,256,512]{2,1,0:T(8,128)(2,1)}, bf16[256,512]{1,0:T(8,128)(2,1)}, bf16[256,512]{1,0:T(8,128)(2,1)}, bf16[256,512]{1,0:T(8,128)(2,1)}, bf...) custom-call(s32[19]{0:T(128)} %pad_add_fusion.refs_4_.refs_0_, bf16[6,256,128]{2,1,0:T(8,128)(2,1)} %get-tuple-element.42.refs_1_, ...), custom_call_target="tpu_custom_call" | custom-call | flops 4026531840 | bytes 7340108 | tf_op jit(solution)/shard_map/pallas_call | solution.py:54
  94.8 6.3 %shard_map.142.refs_5_ = bf16[3072,768]{1,0:T(8,128)(2,1)} custom-call(bf16[256,3072]{1,0:T(8,128)(2,1)} %get-tuple-element.51.refs_0_, bf16[256,768]{1,0:T(8,128)(2,1)} %get-tuple-element.52.refs_1_), custom_call_target="tpu_custom_call" | custom-call | flops 1207959552 | bytes 6684672 | tf_op jit(solution)/shard_map/pallas_call | solution.py:54
  105.6 2.6 shard_map.143
  108.2 4.9 %shard_map.144 = (bf16[256,1536]{1,0:T(8,128)(2,1)}, bf16[256,1536]{1,0:T(8,128)(2,1)}) custom-call(s32[1]{0:T(128)} %bitcast.1.refs_0_, bf16[256,768]{1,0:T(8,128)(2,1)} %get-tuple-element.43.refs_3_.refs_1_.refs_4_, bf16[768,3072]{1,0:T(8,128)(2,1)} %bitcast.49, bf16[256,512]{1,0:T(8,128)(2,1)} %get-tuple-element.53.refs_3_), custom_call_target="tpu_custom_call" | custom-call | flops 1207959552 | bytes 6684676 | tf_op jit(solution)/shard_map/pallas_call | solution.py:54
  118.8 5.4 %shard_map.145 = (bf16[256,1536]{1,0:T(8,128)(2,1)}, bf16[256,1536]{1,0:T(8,128)(2,1)}, f32[256,128]{1,0:T(8,128)}) custom-call(s32[1]{0:T(128)} %bitcast.1.refs_0_, bf16[256,768]{1,0:T(8,128)(2,1)} %get-tuple-element.52.refs_1_, bf16[3072,768]{1,0:T(8,128)(2,1)} %bitcast.51, bf16[256,1536]{1,0:T(8,128)(2,1)} %bitcast.44, bf16[256,1536]{1,0:T(8,128)(2,1)} %copy-done.6, ...), custom_call_target="tpu_custom_call" | custom-call | flops 1207959552 | bytes 8388612 | tf_op jit(solution)/shard_map/pallas_call | solution.py:54
  124.2 10.6 %collective-permute-done.8.refs_4_ = bf16[256,512]{1,0:T(8,128)(2,1)S(1)} collective-permute-done((bf16[256,512]{1,0:T(8,128)(2,1)S(1)}, bf16[256,512]{1,0:T(8,128)(2,1)S(1)}, u32[]{:S(2)}, u32[]{:S(2)}) %collective-permute-start.8) | collective-permute-done | bytes 262176 | tf_op jit(solution)/shard_map/ppermute | solution.py:525
  134.8 24.1 %collective-permute-done.9.refs_5_ = bf16[256,512]{1,0:T(8,128)(2,1)S(1)} collective-permute-done((bf16[256,512]{1,0:T(8,128)(2,1)S(1)}, bf16[256,512]{1,0:T(8,128)(2,1)S(1)}, u32[]{:S(2)}, u32[]{:S(2)}) %collective-permute-start.9) | collective-permute-done | bytes 262176 | tf_op jit(solution)/shard_map/ppermute | solution.py:525
  159.7 4.8 %shard_map.146 = (bf16[256,1536]{1,0:T(8,128)(2,1)}, bf16[256,1536]{1,0:T(8,128)(2,1)}, f32[256,128]{1,0:T(8,128)}, bf16[256,512]{1,0:T(8,128)(2,1)}) custom-call(s32[1]{0:T(128)} %bitcast.1.refs_0_, f32[256,256]{1,0:T(8,128)} %get-tuple-element.57.refs_1_, bf16[3072,512]{1,0:T(8,128)(2,1)} %bitcast.42, bf16[256,512]{1,0:T(8,128)(2,1)} %get-tuple-element.53.refs_3_, ...), custom_call_target="tpu_custom_call" | custom-call | flops 805306368 | bytes 7995396 | tf_op jit(solution)/shard_map/pallas_call | solution.py:54
  164.5 6.0 %shard_map.147 = (bf16[4,384,512]{2,1,0:T(8,128)(2,1)}, bf16[384,512]{1,0:T(8,128)(2,1)}, bf16[384,512]{1,0:T(8,128)(2,1)}, bf16[384,512]{1,0:T(8,128)(2,1)}, bf16[384,512]{1,0:T(8,128)(2,1)}) custom-call(s32[5]{0:T(128)} %stack.39.refs_0_, bf16[256,3072]{1,0:T(8,128)(2,1)} %get-tuple-element.56.refs_1_, bf16[256,512]{1,0:T(8,128)(2,1)} %get-tuple-element.62.refs_2_), custom_call_target="tpu_custom_call" | custom-call | bytes 1024 | tf_op jit(solution)/shard_map/pallas_call | solution.py:408
  172.9 2.8 %shard_map.148.refs_4_ = bf16[256,1536]{1,0:T(8,128)(2,1)} custom-call(bf16[256,1536]{1,0:T(8,128)(2,1)} %bitcast.45, bf16[256,1536]{1,0:T(8,128)(2,1)} %get-tuple-element.54.refs_5_.refs_1_, bf16[256,1536]{1,0:T(8,128)(2,1)} %copy-done.7, bf16[4,384,512]{2,1,0:T(8,128)(2,1)} %get-tuple-element.63.refs_3_.refs_1_), custom_call_target="tpu_custom_call" | custom-call | bytes 3145728 | tf_op jit(solution)/shard_map/pallas_call | solution.py:54
  177.2 2.4 shard_map.149.refs_7_
  181.6 28.8 %collective-permute-done.12.refs_5_ = f32[256,128]{1,0:T(8,128)S(1)} collective-permute-done((f32[256,128]{1,0:T(8,128)S(1)}, f32[256,128]{1,0:T(8,128)S(1)}, u32[]{:S(2)}, u32[]{:S(2)}) %collective-permute-start.12) | collective-permute-done | bytes 131104 | tf_op jit(solution)/shard_map/ppermute | solution.py:36
  211.9 3.4 %shard_map.150.refs_4_ = bf16[256,1536]{1,0:T(8,128)(2,1)} custom-call(bf16[256,1536]{1,0:T(8,128)(2,1)} %bitcast.57, bf16[256,1536]{1,0:T(8,128)(2,1)} %bitcast.46, f32[256,128]{1,0:T(8,128)} %get-tuple-element.64.refs_2_, bf16[256,1536]{1,0:T(8,128)(2,1)} %get-tuple-element.65.refs_3_, f32[256,128]{1,0:T(8,128)} %get-tuple-element.61.refs_9_.refs_4_, ...), custom_call_target="tpu_custom_call" | custom-call | bytes 4325376 | tf_op jit(solution)/shard_map/pallas_call | solution.py:54
  218.0 2.1 shard_map.151.refs_6_
  221.3 3.9 %collective-permute-done.16.refs_4_ = f32[256,128]{1,0:T(8,128)S(1)} collective-permute-done((f32[256,128]{1,0:T(8,128)S(1)}, f32[256,128]{1,0:T(8,128)S(1)}, u32[]{:S(2)}, u32[]{:S(2)}) %collective-permute-start.16) | collective-permute-done | bytes 131104 | tf_op jit(solution)/shard_map/ppermute | solution.py:36
  225.8 3.1 %shard_map.152.refs_5_ = bf16[256,1536]{1,0:T(8,128)(2,1)} custom-call(bf16[256,1536]{1,0:T(8,128)(2,1)} %copy-done.1, f32[256,128]{1,0:T(8,128)} %get-tuple-element.69.refs_1_, bf16[256,1536]{1,0:T(8,128)(2,1)} %get-tuple-element.70.refs_2_, f32[256,128]{1,0:T(8,128)} %get-tuple-element.71.refs_3_, f32[256,128]{1,0:T(8,128)} %copy-done.24, ...), custom_call_target="tpu_custom_call" | custom-call | bytes 3538944 | tf_op jit(solution)/shard_map/pallas_call | solution.py:54
  228.9 15.0 %collective-permute-done.21.refs_4_ = bf16[1,384,512]{2,1,0:T(8,128)(2,1)S(1)} collective-permute-done((bf16[1,384,512]{2,1,0:T(8,128)(2,1)}, bf16[1,384,512]{2,1,0:T(8,128)(2,1)S(1)}, u32[]{:S(2)}, u32[]{:S(2)}) %collective-permute-start.21) | collective-permute-done | bytes 393248 | tf_op jit(solution)/shard_map/ppermute | solution.py:541
  244.6 2.4 shard_map.153
  249.6 5.1 %collective-permute-done.22 = bf16[192,512]{1,0:T(8,128)(2,1)S(1)} collective-permute-done((bf16[192,512]{1,0:T(8,128)(2,1)S(1)}, bf16[192,512]{1,0:T(8,128)(2,1)S(1)}, u32[]{:S(2)}, u32[]{:S(2)}) %collective-permute-start.22) | collective-permute-done | bytes 196640 | tf_op jit(solution)/shard_map/ppermute | solution.py:36
  260.4 2.2 bitcast_convert_fusion
  (127 shorter events, 43.3 us)
Async XLA Ops:
  7.2 59.2 %all-gather.3.cloned.1.call-start = ((), (), s32[]{:S(2)}) async-start(), calls=%async_computation.2 | async-start | bytes 2359296 | tf_op jit(solution)/shard_map/all_gather | solution.py:614
  8.7 21.6 %copy-start.1 = (bf16[256,1536]{1,0:T(8,128)(2,1)}, bf16[256,1536]{1,0:T(8,128)(2,1)S(1)}, u32[]{:S(2)}) copy-start(bf16[256,1536]{1,0:T(8,128)(2,1)S(1)} %bitcast_select_fusion.refs_1_.refs_7_.refs_0_) | copy-start | bytes 2359300
  8.7 24.5 %collective-permute-start.1 = (bf16[256,1536]{1,0:T(8,128)(2,1)S(1)}, bf16[256,1536]{1,0:T(8,128)(2,1)S(1)}, u32[]{:S(2)}, u32[]{:S(2)}) collective-permute-start(bf16[256,1536]{1,0:T(8,128)(2,1)S(1)} %bitcast_select_fusion.refs_1_.refs_7_.refs_0_), channel_id=1, source_target_pairs={{0,1},{1,0},{2,3},{3,2},{4,5},{5,4},{6,7},{7,6},{8,9},{9,8},{10,11... | collective-permute-start | bytes 2359304 | tf_op jit(solution)/shard_map/ppermute | solution.py:36
  38.7 219.2 %reduce-scatter.5.cloned.1.call-start = ((), (), s32[]{:S(2)}) async-start(), calls=%async_computation.4 | async-start | bytes 5308416 | tf_op jit(solution)/shard_map/reduce_scatter | solution.py:498
  38.7 20.5 %collective-permute-start = (bf16[256,1536]{1,0:T(8,128)(2,1)S(1)}, bf16[256,1536]{1,0:T(8,128)(2,1)S(1)}, u32[]{:S(2)}, u32[]{:S(2)}) collective-permute-start(bf16[256,1536]{1,0:T(8,128)(2,1)S(1)} %bitcast.47), channel_id=1, source_target_pairs={{0,1},{1,0},{2,3},{3,2},{4,5},{5,4},{6,7},{7,6},{8,9},{9,8},{10,11... | collective-permute-start | bytes 2359304 | tf_op jit(solution)/shard_map/ppermute | solution.py:36
  39.4 34.3 %collective-permute-start.2 = (bf16[256,1536]{1,0:T(8,128)(2,1)S(1)}, bf16[256,1536]{1,0:T(8,128)(2,1)S(1)}, u32[]{:S(2)}, u32[]{:S(2)}) collective-permute-start(bf16[256,1536]{1,0:T(8,128)(2,1)S(1)} %bitcast.58), channel_id=1, source_target_pairs={{0,1},{1,0},{2,3},{3,2},{4,5},{5,4},{6,7},{7,6},{8,9},{9,8},{10,11... | collective-permute-start | bytes 2359304 | tf_op jit(solution)/shard_map/ppermute | solution.py:36
  83.7 176.7 %reduce-scatter.3.cloned.1.call-start = ((), (), s32[]{:S(2)}) async-start(), calls=%async_computation.3 | async-start | bytes 5308416 | tf_op jit(solution)/shard_map/reduce_scatter | solution.py:498
  102.1 1.5 collective-permute-start.3
  102.2 1.8 collective-permute-start.4
  102.6 1.9 collective-permute-start.5
  102.7 2.2 collective-permute-start.6
  108.2 7.1 %copy-start.27 = (bf16[256,512]{1,0:T(8,128)(2,1)S(1)}, bf16[256,512]{1,0:T(8,128)(2,1)}, u32[]{:S(2)}) copy-start(bf16[256,512]{1,0:T(8,128)(2,1)} %get-tuple-element.59) | copy-start | bytes 786436
  108.2 8.4 %copy-start.26 = (bf16[256,512]{1,0:T(8,128)(2,1)S(1)}, bf16[256,512]{1,0:T(8,128)(2,1)}, u32[]{:S(2)}) copy-start(bf16[256,512]{1,0:T(8,128)(2,1)} %get-tuple-element.60) | copy-start | bytes 786436
  113.1 58.9 %collective-permute-start.7 = (bf16[256,1536]{1,0:T(8,128)(2,1)}, bf16[256,1536]{1,0:T(8,128)(2,1)S(1)}, u32[]{:S(2)}, u32[]{:S(2)}) collective-permute-start(bf16[256,1536]{1,0:T(8,128)(2,1)} %get-tuple-element.55), channel_id=1, source_target_pairs={{0,1},{1,0},{2,3},{3,2},{4,5},{5,4},{6,7},{7,6},{8,9},{9,8},{10,11... | collective-permute-start | bytes 2359304 | tf_op jit(solution)/shard_map/ppermute | solution.py:36
  114.0 20.8 %collective-permute-start.8 = (bf16[256,512]{1,0:T(8,128)(2,1)S(1)}, bf16[256,512]{1,0:T(8,128)(2,1)S(1)}, u32[]{:S(2)}, u32[]{:S(2)}) collective-permute-start(bf16[256,512]{1,0:T(8,128)(2,1)S(1)} %copy-done.28), channel_id=1, source_target_pairs={{8,0},{12,4},{16,8},{20,12},{24,16},{28,20},{9,1},{13,5},{17,9},{2... | collective-permute-start | bytes 786440 | tf_op jit(solution)/shard_map/ppermute | solution.py:525
  115.3 43.6 %collective-permute-start.9 = (bf16[256,512]{1,0:T(8,128)(2,1)S(1)}, bf16[256,512]{1,0:T(8,128)(2,1)S(1)}, u32[]{:S(2)}, u32[]{:S(2)}) collective-permute-start(bf16[256,512]{1,0:T(8,128)(2,1)S(1)} %copy-done.27), channel_id=1, source_target_pairs={{16,0},{20,4},{24,8},{28,12},{17,1},{21,5},{25,9},{29,13},{18,2},{... | collective-permute-start | bytes 786440 | tf_op jit(solution)/shard_map/ppermute | solution.py:525
  116.6 42.3 %collective-permute-start.10 = (bf16[256,512]{1,0:T(8,128)(2,1)S(1)}, bf16[256,512]{1,0:T(8,128)(2,1)S(1)}, u32[]{:S(2)}, u32[]{:S(2)}) collective-permute-start(bf16[256,512]{1,0:T(8,128)(2,1)S(1)} %copy-done.26), channel_id=1, source_target_pairs={{24,0},{28,4},{25,1},{29,5},{26,2},{30,6},{27,3},{31,7}} | collective-permute-start | bytes 786440 | tf_op jit(solution)/shard_map/ppermute | solution.py:525
  134.8 24.1 %copy-start.16 = (bf16[256,512]{1,0:T(8,128)(2,1)}, bf16[256,512]{1,0:T(8,128)(2,1)S(1)}, u32[]{:S(2)}) copy-start(bf16[256,512]{1,0:T(8,128)(2,1)S(1)} %collective-permute-done.8.refs_4_) | copy-start | bytes 786436
  170.5 5.2 %collective-permute-start.14 = (bf16[384,512]{1,0:T(8,128)(2,1)}, bf16[384,512]{1,0:T(8,128)(2,1)S(1)}, u32[]{:S(2)}, u32[]{:S(2)}) collective-permute-start(bf16[384,512]{1,0:T(8,128)(2,1)} %get-tuple-element.67), channel_id=1, source_target_pairs={{0,4},{4,0},{8,12},{12,8},{16,20},{20,16},{24,28},{28,24},{1,5},{5... | collective-permute-start | bytes 1179656 | tf_op jit(solution)/shard_map/ppermute | solution.py:503
  170.5 5.2 %collective-permute-start.15 = (bf16[384,512]{1,0:T(8,128)(2,1)}, bf16[384,512]{1,0:T(8,128)(2,1)S(1)}, u32[]{:S(2)}, u32[]{:S(2)}) collective-permute-start(bf16[384,512]{1,0:T(8,128)(2,1)} %get-tuple-element.68), channel_id=1, source_target_pairs={{0,4},{4,0},{8,12},{12,8},{16,20},{20,16},{24,28},{28,24},{1,5},{5... | collective-permute-start | bytes 1179656 | tf_op jit(solution)/shard_map/ppermute | solution.py:503
  171.0 39.5 %collective-permute-start.13 = (bf16[256,1536]{1,0:T(8,128)(2,1)}, bf16[256,1536]{1,0:T(8,128)(2,1)S(1)}, u32[]{:S(2)}, u32[]{:S(2)}) collective-permute-start(bf16[256,1536]{1,0:T(8,128)(2,1)} %get-tuple-element.66), channel_id=1, source_target_pairs={{0,1},{1,0},{2,3},{3,2},{4,5},{5,4},{6,7},{7,6},{8,9},{9,8},{10,11... | collective-permute-start | bytes 2359304 | tf_op jit(solution)/shard_map/ppermute | solution.py:36
  175.7 34.7 %copy-start.3 = (bf16[256,1536]{1,0:T(8,128)(2,1)S(1)}, bf16[256,1536]{1,0:T(8,128)(2,1)}, u32[]{:S(2)}) copy-start(bf16[256,1536]{1,0:T(8,128)(2,1)} %shard_map.148.refs_4_) | copy-start | bytes 2359300
  179.6 37.6 %collective-permute-start.19 = (bf16[2,384,512]{2,1,0:T(8,128)(2,1)}, bf16[2,384,512]{2,1,0:T(8,128)(2,1)S(1)}, u32[]{:S(2)}, u32[]{:S(2)}) collective-permute-start(bf16[2,384,512]{2,1,0:T(8,128)(2,1)} %shard_map.149.refs_7_), channel_id=1, source_target_pairs={{0,8},{4,12},{8,0},{12,4},{16,24},{20,28},{24,16},{28,20},{1,9},{5... | collective-permute-start | bytes 2359304 | tf_op jit(solution)/shard_map/ppermute | solution.py:541
  179.6 45.5 %collective-permute-start.17 = (bf16[256,1536]{1,0:T(8,128)(2,1)}, bf16[256,1536]{1,0:T(8,128)(2,1)}, u32[]{:S(2)}, u32[]{:S(2)}) collective-permute-start(bf16[256,1536]{1,0:T(8,128)(2,1)} %get-tuple-element.72), channel_id=1, source_target_pairs={{0,1},{1,0},{2,3},{3,2},{4,5},{5,4},{6,7},{7,6},{8,9},{9,8},{10,11... | collective-permute-start | bytes 2359304 | tf_op jit(solution)/shard_map/ppermute | solution.py:36
  180.6 34.7 %collective-permute-start.18 = (bf16[384,512]{1,0:T(8,128)(2,1)}, bf16[384,512]{1,0:T(8,128)(2,1)S(1)}, u32[]{:S(2)}, u32[]{:S(2)}) collective-permute-start(bf16[384,512]{1,0:T(8,128)(2,1)} %get-tuple-element.73), channel_id=1, source_target_pairs={{0,4},{4,0},{8,12},{12,8},{16,20},{20,16},{24,28},{28,24},{1,5},{5... | collective-permute-start | bytes 1179656 | tf_op jit(solution)/shard_map/ppermute | solution.py:503
  180.6 29.8 %collective-permute-start.12 = (f32[256,128]{1,0:T(8,128)S(1)}, f32[256,128]{1,0:T(8,128)S(1)}, u32[]{:S(2)}, u32[]{:S(2)}) collective-permute-start(f32[256,128]{1,0:T(8,128)S(1)} %copy-done.10), channel_id=1, source_target_pairs={{0,1},{1,0},{2,3},{3,2},{4,5},{5,4},{6,7},{7,6},{8,9},{9,8},{10,11... | collective-permute-start | bytes 393224 | tf_op jit(solution)/shard_map/ppermute | solution.py:36
  210.4 39.2 %collective-permute-start.11 = (bf16[256,1536]{1,0:T(8,128)(2,1)S(1)}, bf16[256,1536]{1,0:T(8,128)(2,1)S(1)}, u32[]{:S(2)}, u32[]{:S(2)}) collective-permute-start(bf16[256,1536]{1,0:T(8,128)(2,1)S(1)} %copy-done.3), channel_id=1, source_target_pairs={{0,2},{2,0},{1,3},{3,1},{4,6},{6,4},{5,7},{7,5},{8,10},{10,8},{9,1... | collective-permute-start | bytes 2359304 | tf_op jit(solution)/shard_map/ppermute | solution.py:36
  211.1 17.8 %collective-permute-start.20 = (bf16[384,512]{1,0:T(8,128)(2,1)}, bf16[384,512]{1,0:T(8,128)(2,1)S(1)}, u32[]{:S(2)}, u32[]{:S(2)}) collective-permute-start(bf16[384,512]{1,0:T(8,128)(2,1)} %get-tuple-element.74), channel_id=1, source_target_pairs={{0,4},{4,0},{8,12},{12,8},{16,20},{20,16},{24,28},{28,24},{1,5},{5... | collective-permute-start | bytes 1179656 | tf_op jit(solution)/shard_map/ppermute | solution.py:503
  220.2 23.7 %collective-permute-start.21 = (bf16[1,384,512]{2,1,0:T(8,128)(2,1)}, bf16[1,384,512]{2,1,0:T(8,128)(2,1)S(1)}, u32[]{:S(2)}, u32[]{:S(2)}) collective-permute-start(bf16[1,384,512]{2,1,0:T(8,128)(2,1)} %shard_map.151.refs_6_), channel_id=1, source_target_pairs={{0,16},{4,20},{8,24},{12,28},{16,0},{20,4},{24,8},{28,12},{1,17},{... | collective-permute-start | bytes 1179656 | tf_op jit(solution)/shard_map/ppermute | solution.py:541
  220.2 5.0 %collective-permute-start.16 = (f32[256,128]{1,0:T(8,128)S(1)}, f32[256,128]{1,0:T(8,128)S(1)}, u32[]{:S(2)}, u32[]{:S(2)}) collective-permute-start(f32[256,128]{1,0:T(8,128)S(1)} %copy-done.23), channel_id=1, source_target_pairs={{0,1},{1,0},{2,3},{3,2},{4,5},{5,4},{6,7},{7,6},{8,9},{9,8},{10,11... | collective-permute-start | bytes 393224 | tf_op jit(solution)/shard_map/ppermute | solution.py:36
  228.9 15.0 %copy-start.11 = (bf16[384,512]{1,0:T(8,128)(2,1)}, bf16[384,512]{1,0:T(8,128)(2,1)S(1)}, u32[]{:S(2)}) copy-start(bf16[384,512]{1,0:T(8,128)(2,1)S(1)} %collective-permute-done.20.refs_2_) | copy-start | bytes 1179652
  248.1 6.7 %collective-permute-start.22 = (bf16[192,512]{1,0:T(8,128)(2,1)S(1)}, bf16[192,512]{1,0:T(8,128)(2,1)S(1)}, u32[]{:S(2)}, u32[]{:S(2)}) collective-permute-start(bf16[192,512]{1,0:T(8,128)(2,1)S(1)} %fusion.2), channel_id=1, source_target_pairs={{0,2},{2,0},{1,3},{3,1},{4,6},{6,4},{5,7},{7,5},{8,10},{10,8},{9,1... | collective-permute-start | bytes 589832 | tf_op jit(solution)/shard_map/ppermute | solution.py:36
  (27 other events, 49.3 us)
Sparse Core Ops, SparseCore 0:
  38.8 26.6 all-gather.2
  83.8 64.3 reduce-scatter.4
  150.5 88.6 reduce-scatter.2

commit v3 on v2

--- a/solution.py
+++ b/solution.py
@@ -177,27 +177,13 @@
         out_ref[:, head * HEAD_DIM : (head + 1) * HEAD_DIM] = (number_ref[head] / denom).astype(BF16)
 
 
-def rows_body(count, me_ref, *refs):
-    width = refs[0].shape[1]
-    for step, piece in enumerate(refs[:count]):
-        refs[-1][:, pl.ds(offset(me_ref[0], count, step, width), width)] = piece[...]
-
-
-def whole_rows(pieces, me, after):
-    rows, width = pieces[0].shape
-    (out,) = call(
-        functools.partial(rows_body, len(pieces)),
-        [struct((rows, width * len(pieces)), BF16)],
-        [me, *pieces],
-        1,
-        0,
-        after=after,
-    )
-    return out
-
-
-def grad_attn_body(rows_ref, weight, grad_ref):
-    both = dot(rows_ref[...], weight[...], NT)
+def grad_attn_body(count, me_ref, *refs):
+    pieces, (weight, grad_ref) = refs[:count], refs[count:]
+    width = pieces[0].shape[1]
+    both = 0.0
+    for step, piece in enumerate(pieces):
+        span = pl.ds(offset(me_ref[0], count, step, width), width)
+        both = both + dot(piece[...], weight[:, span], NT)
     for head in range(grad_ref.shape[0]):
         grad_ref[head] = both[:, head * HEAD_DIM : (head + 1) * HEAD_DIM].astype(BF16)
 
@@ -266,17 +252,8 @@
         ).astype(BF16)
 
 
-CHUNKS = 1
-
-
-def chunked(rows):
-    return CHUNKS if rows % (16 * CHUNKS) == 0 else 1
-
-
 def split(count, transposed, me, left, weight_ref, pieces, outs, dot_ref):
-    own_ref, sent = outs[0], outs[1:]
-    rows, width = own_ref.shape
-    parts = len(sent) // max(count - 1, 1)
+    rows, width = outs[0].shape
     total = 0.0
     for step in list(range(1, count)) + [0]:
         span = pl.ds(offset(me, count, step, width), width)
@@ -284,30 +261,30 @@
             part = dot(left, weight_ref[span, :], NT).astype(BF16)
         else:
             part = dot(left, weight_ref[:, span], NN).astype(BF16)
-        if step == 0:
-            own_ref[...] = part
-        else:
-            tall = rows // parts
-            for index in range(parts):
-                sent[(step - 1) * parts + index][...] = part[index * tall : (index + 1) * tall]
+        outs[step][:, :width] = part
         if dot_ref is not None:
             total = total + jnp.sum(
                 part.astype(F32) * pieces[step][...].astype(F32), axis=1, keepdims=True
             )
     if dot_ref is not None:
         dot_ref[...] = jnp.broadcast_to(total, dot_ref.shape)
-
-
-def split_shapes(rows, width, count):
-    parts = chunked(rows)
-    return [struct((rows, width), BF16)] + [struct((rows // parts, width), BF16)] * (
-        parts * (count - 1)
-    )
-
-
-def sent_over_tp(outs, rows):
-    parts = chunked(rows)
-    return [shifted(out, "tp", -(1 + index // parts)) for index, out in enumerate(outs[1:])]
+        lane = lax.broadcasted_iota(jnp.int32, dot_ref.shape, 1)
+        rest, column = total, jnp.zeros(dot_ref.shape, F32)
+        for place in range(3):
+            term = rest.astype(BF16).astype(F32)
+            column = jnp.where(lane == place, term, column)
+            rest = rest - term
+        for out in outs[1:]:
+            out[:, width:] = column.astype(BF16)
+
+
+def split_shapes(rows, width, count, dotted):
+    extra = HEAD_DIM if dotted else 0
+    return [struct((rows, width), BF16)] + [struct((rows, width + extra), BF16)] * (count - 1)
+
+
+def sent_over_tp(outs):
+    return [shifted(out, "tp", -1 - index) for index, out in enumerate(outs)]
 
 
 def project_body(count, me_ref, left_ref, weight_ref, *outs):
@@ -319,53 +296,38 @@
     split(count, True, me_ref[0], left_ref[...], weight_ref, pieces, outs, dot_ref)
 
 
-def key_back_body(count, terms, me_ref, raw_ref, weight_ref, *refs):
-    term_refs, refs = refs[:terms], refs[terms:]
-    pieces, outs, dot_ref, grad_ref = refs[:count], refs[count:-2], refs[-2], refs[-1]
+def key_grad_body(raw_ref, *refs):
+    term_refs, grad_ref = refs[:-1], refs[-1]
     half = raw_ref.shape[1]
-    total = term_refs[0][...].astype(F32)
-    for term in term_refs[1:]:
-        total = total + term[...].astype(F32)
+    total = sum(term[...].astype(F32) for term in term_refs)
     for first in range(0, half, HEAD_DIM):
         cols = slice(first, first + HEAD_DIM)
         grad_ref[:, cols] = unit_back(raw_ref[:, cols], total[:, cols]).astype(BF16)
     grad_ref[:, half:] = total[:, half:].astype(BF16)
-    split(count, True, me_ref[0], grad_ref[...], weight_ref, pieces, outs, dot_ref)
-
-
-def summed(own_ref, came, at):
-    rows = own_ref.shape[0]
-    parts = chunked(rows)
-    tall = rows // parts
-    total = own_ref[at * tall : (at + 1) * tall].astype(F32)
-    for ref in came[at::parts]:
-        total = total + ref[...].astype(F32)
-    return total, slice(at * tall, (at + 1) * tall)
 
 
 def output_body(hidden_ref, own_ref, *refs):
-    came, out_ref = refs[:-1], refs[-1]
-    for at in range(chunked(own_ref.shape[0])):
-        total, span = summed(own_ref, came, at)
-        out_ref[span] = (hidden_ref[span].astype(F32) + total).astype(BF16)
-
-
-def input_body(count, residual, model, *refs):
+    total = hidden_ref[...].astype(F32) + sum(ref[...].astype(F32) for ref in (own_ref, *refs[:-1]))
+    refs[-1][...] = total.astype(BF16)
+
+
+def input_body(residual, model, *refs):
     base, refs = (refs[0], refs[1:]) if residual else (None, refs)
-    values_ref, factor_ref, own_ref, *refs = refs
-    dots, came, out_ref = refs[:count], refs[count:-1], refs[-1]
-    for at in range(chunked(own_ref.shape[0])):
-        total, span = summed(own_ref, came, at)
-        dot_total = dots[0][span, :1]
-        for ref in dots[1:]:
-            dot_total = dot_total + ref[span, :1]
-        factor = factor_ref[span, :1]
-        grad = factor * total - values_ref[span].astype(F32) * (
-            factor * factor * factor * dot_total / model
-        )
-        if residual:
-            grad = grad + base[span].astype(F32)
-        out_ref[span] = grad.astype(BF16)
+    values_ref, factor_ref, dot_ref, own_ref, *came, out_ref = refs
+    width = own_ref.shape[1]
+    total = own_ref[...].astype(F32)
+    dot_total = dot_ref[:, :1]
+    for ref in came:
+        total = total + ref[:, :width].astype(F32)
+        column = ref[:, width:].astype(F32)
+        dot_total = dot_total + (column[:, :1] + column[:, 1:2] + column[:, 2:3])
+    factor = factor_ref[:, :1]
+    grad = factor * total - values_ref[...].astype(F32) * (
+        factor * factor * factor * dot_total / model
+    )
+    if residual:
+        grad = grad + base[...].astype(F32)
+    out_ref[...] = grad.astype(BF16)
 
 
 def flipped_bits(value, count):
@@ -388,38 +350,48 @@
     def high():
         keep_ref[0] = both[half:]
 
-    for place, send_ref in enumerate(send_refs):
-
-        @pl.when((at_ref[0] == 0) & (pl.program_id(0) == place))
+    tall = send_refs[0].shape[0]
+    place = pl.program_id(0)
+    for group, send_ref in enumerate(send_refs):
+
+        @pl.when((at_ref[0] == 0) & (place // tall == group))
         def low_sent(send_ref=send_ref):
-            send_ref[...] = both[half:]
-
-        @pl.when((at_ref[0] == 1) & (pl.program_id(0) == place))
+            send_ref[place % tall] = both[half:]
+
+        @pl.when((at_ref[0] == 1) & (place // tall == group))
         def high_sent(send_ref=send_ref):
-            send_ref[...] = both[:half]
-
-
-def ordered(body, inputs, after, outs, grid, in_specs, out_specs, scalars):
+            send_ref[place % tall] = both[:half]
+
+
+def ordered(
+    body, inputs, after, outs, grid, in_specs, out_specs, scalars, relay=(), scratch=()
+):
     kept = 1 + len(inputs)
+    first = kept + len(after)
+    anywhere = pl.BlockSpec(memory_space=pl.ANY)
 
     def with_order(*refs):
-        body(*refs[:kept], *refs[kept + len(after) :])
+        begin = first + len(relay)
+        last = begin + len(outs)
+        body(*refs[:kept], *refs[begin:last], *refs[last + len(relay) :])
 
     return pl.pallas_call(
         with_order,
-        out_shape=outs,
+        out_shape=outs + [struct(value.shape, value.dtype) for value in relay],
         grid_spec=pltpu.PrefetchScalarGridSpec(
             num_scalar_prefetch=1,
             grid=grid,
-            in_specs=in_specs + [pl.BlockSpec(memory_space=pl.ANY)] * len(after),
-            out_specs=out_specs,
+            in_specs=in_specs + [anywhere] * (len(after) + len(relay)),
+            out_specs=out_specs + [anywhere] * len(relay),
+            scratch_shapes=list(scratch),
         ),
-        compiler_params=pltpu.CompilerParams(vmem_limit_bytes=60 * 1024 * 1024),
+        input_output_aliases={first + i: len(outs) + i for i in range(len(relay))},
+        compiler_params=pltpu.CompilerParams(vmem_limit_bytes=16 * 1024 * 1024),
         cost_estimate=pl.CostEstimate(flops=0, bytes_accessed=1024, transcendentals=0),
-    )(scalars, *inputs, *after)
-
-
-def over_tokens(left, right, after=()):
+    )(scalars, *inputs, *after, *relay)
+
+
+def over_tokens(left, right, after=(), relay=(), natural=False):
     rows, model = left.shape
     chips = lax.axis_size("seq") // 2
     step = model // chips
@@ -427,75 +399,53 @@
     shard = lax.axis_index("seq").astype(jnp.int32)
     near = jnp.stack(
         [shard % 2]
-        + [lax.bitwise_xor(shard // 2, jnp.int32(flipped_bits(i, chips))) for i in range(chips)]
+        + [
+            jnp.int32(i) if natural else lax.bitwise_xor(shard // 2, jnp.int32(flipped_bits(i, chips)))
+            for i in range(chips)
+        ]
     )
     share = (step // 2, cols)
-    keep, *send = ordered(
+    group = (chips // 2, *share)
+    keep, low, high, *relayed = ordered(
         tokens_body,
         [left, right],
         after,
-        [struct((chips, *share), BF16)] + [struct(share, BF16)] * chips,
+        [struct((chips, *share), BF16), struct(group, BF16), struct(group, BF16)],
         (chips,),
         [
             pl.BlockSpec((rows, step), lambda i, at: (0, at[1 + i])),
             pl.BlockSpec(right.shape, lambda i, at: (0, 0)),
         ],
         [pl.BlockSpec((1, *share), lambda i, at: (i, 0, 0))]
-        + [pl.BlockSpec(share, lambda i, at: (0, 0))] * chips,
+        + [pl.BlockSpec(group, lambda i, at: (0, 0, 0))] * 2,
         near,
-    )
-    return keep, send
-
-
-def add_body(count, at_ref, *refs):
+        relay,
+    )
+    return keep, low, high, relayed
+
+
+def add_body(at_ref, *refs):
     out_ref = refs[-1]
-    for index in range(count):
-        total = refs[0][index].astype(F32) + refs[1 + index][...].astype(F32)
-        for ref in refs[1 + count : -1]:
-            total = total + ref[index].astype(F32)
+    for index in range(out_ref.shape[0]):
+        total = sum(ref[index].astype(F32) for ref in refs[:-1])
         out_ref[index] = total.astype(out_ref.dtype)
 
 
-def added(keep, came, terms, first, count, dtype, after):
+def added(keep, came, terms, first, count, dtype, after, relay=()):
     rows, cols = keep.shape[1:]
     block = pl.BlockSpec((count, rows, cols), lambda i, at: (first // count, 0, 0))
-    flat = pl.BlockSpec((rows, cols), lambda i, at: (0, 0))
-    (out,) = ordered(
-        functools.partial(add_body, count),
-        [keep, *came[first : first + count], *terms],
+    start = pl.BlockSpec((count, rows, cols), lambda i, at: (0, 0, 0))
+    return ordered(
+        add_body,
+        [keep, came, *terms],
         after,
         [struct((count, rows, cols), dtype)],
         (1,),
-        [block] + [flat] * count + [block] * len(terms),
-        [pl.BlockSpec((count, rows, cols), lambda i, at: (0, 0, 0))],
+        [block, start if came.shape[0] == count and first > 0 else block] + [block] * len(terms),
+        [start],
         jnp.zeros((1,), jnp.int32),
-    )
-    return out
-
-
-def whole_body(left_ref, right_ref, out_ref):
-    out_ref[...] = dot(left_ref[...], right_ref[...], TN).astype(BF16)
-
-
-def scattered(left, right, after=()):
-    rows, model = left.shape
-    step = math.gcd(model, 512)
-    cols = right.shape[1]
-    (partial,) = call(
-        whole_body,
-        [struct((model, cols), BF16)],
-        [left, right],
-        0,
-        2 * rows * model * cols,
-        after=after,
-        grid=(model // step,),
-        in_specs=[
-            pl.BlockSpec((rows, step), lambda i: (0, i)),
-            pl.BlockSpec(right.shape, lambda i: (0, 0)),
-        ],
-        out_specs=[pl.BlockSpec((step, cols), lambda i: (i, 0))],
-    )
-    return lax.psum_scatter(partial, "seq", scatter_dimension=0, tiled=True), partial
+        relay,
+    )
 
 
 def core_swap(value):
@@ -503,47 +453,173 @@
     return lax.ppermute(value, "seq", [(shard, shard ^ 1) for shard in range(count)])
 
 
+def whole_body(left_ref, right_ref, out_ref):
+    out_ref[...] = dot(left_ref[...], right_ref[...], TN).astype(BF16)
+
+
+def pieces_body(count, at_ref, *refs):
+    pieces, (right_ref, out_ref) = refs[:count], refs[count:]
+    for step, piece in enumerate(pieces):
+
+        @pl.when(pl.program_id(0) == step)
+        def multiply(piece=piece):
+            out_ref[...] = dot(piece[...], right_ref[...], TN).astype(BF16)
+
+
+def scattered(pieces, right, after=()):
+    rows, width = pieces[0].shape
+    count = len(pieces)
+    block = width // 2 if count == 1 else width
+    parts = width // block
+    cols = right.shape[1]
+    tp_id = lax.axis_index("tp").astype(jnp.int32)
+    places = jnp.stack([lax.rem(tp_id + count - step, count) if count > 1 else tp_id * 0 for step in range(count)])
+
+    def picked(which):
+        def index(step, part, at):
+            held = jnp.where(step < which, 0, parts - 1)
+            return 0, jnp.where(step == which, part, held)
+
+        return pl.BlockSpec((rows, block), index)
+
+    (partial,) = ordered(
+        functools.partial(pieces_body, count),
+        [*pieces, right],
+        after,
+        [struct((width * count, cols), BF16)],
+        (count, parts),
+        [picked(which) for which in range(count)]
+        + [pl.BlockSpec(right.shape, lambda step, part, at: (0, 0))],
+        [pl.BlockSpec((block, cols), lambda step, part, at: (at[step] * parts + part, 0))],
+        places,
+    )
+    return lax.psum_scatter(partial, "seq", scatter_dimension=0, tiled=True), partial
+
+
 def chip_sum_body(count, keep_ref, *refs):
+    came, refs = refs[:count], refs[count:]
+    whole_ref, low_ref, high_ref, out_ref = *refs[:3], refs[3 + count]
     for index in range(count):
-        total = keep_ref[index].astype(F32) + refs[index][...].astype(F32)
-        refs[count + index][...] = total.astype(BF16)
-
-
-def sums_below(keep, came, after):
+        total = keep_ref[index].astype(F32) + came[index][...].astype(F32)
+        refs[3 + index][...] = total.astype(BF16)
+    half = count // 2
+    for index in range(count):
+        other = low_ref[index] if index < half else high_ref[index - half]
+        total = whole_ref[index].astype(F32) + other.astype(F32)
+        out_ref[index] = total.astype(BF16)
+
+
+def sums_below(keep, came, query, after):
     chips, rows, cols = keep.shape
-    sums = call(
+    *sums, query_sum = call(
         functools.partial(chip_sum_body, chips),
-        [struct((rows, cols), BF16)] * chips,
-        [keep, *came],
+        [struct((rows, cols), BF16)] * chips + [struct(query[0].shape, BF16)],
+        [keep, *came, *query],
         0,
         2 * keep.size,
         after=after,
+        limit=24,
     )
     terms = [sums[0]]
     for steps in range(1, chips):
         pairs = [(shard, shard - 2 * steps) for shard in range(2 * steps, 2 * chips)]
         terms.append(lax.ppermute(sums[steps], "seq", pairs))
-    return terms, sums[0]
+    return terms, sums[0], query_sum
 
 
 class Halving:
-    def __init__(self, keep, send):
+    def __init__(self, keep, low, high):
         self.keep = keep
-        self.came = [core_swap(piece) for piece in send]
+        self.high, self.low = core_swap(high), core_swap(low)
         self.terms = []
         self.count = keep.shape[0]
         self.distance = 2
 
-    def step(self, after):
+    def step(self, after, relay=()):
         self.count //= 2
-        sent = added(self.keep, self.came, self.terms, self.count, self.count, BF16, after)
+        came = self.low if self.terms else self.high
+        sent, *relayed = added(
+            self.keep, came, self.terms, self.count, self.count, BF16, after, relay
+        )
         pairs = [(shard, shard ^ self.distance) for shard in range(lax.axis_size("seq"))]
         self.terms.append(lax.ppermute(sent, "seq", pairs))
         self.distance *= 2
-        return sent
-
-    def last(self, after):
-        return added(self.keep, self.came, self.terms, 0, 1, F32, after)[0]
+        return sent, relayed
+
+    def finish(self, after):
+        rows, cols = self.keep.shape[1:]
+        sections = lax.axis_size("section")
+        section = lax.axis_index("section")
+        share = rows // sections
+        piece = struct((share, cols), BF16)
+        block = pl.BlockSpec((2, rows, cols), lambda i, at: (0, 0, 0))
+        flat = pl.BlockSpec((share, cols), lambda i, at: (0, 0))
+        targets = [lax.rem(section + step, sections) for step in range(sections)]
+        outs = ordered(
+            last_body,
+            [self.keep, self.low, *self.terms],
+            after,
+            [piece] * (2 * sections),
+            (1,),
+            [block] * (2 + len(self.terms)),
+            [flat] * (2 * sections),
+            jnp.stack(targets).astype(jnp.int32),
+            scratch=[pltpu.VMEM((2, rows, cols), F32)],
+        )
+        count = lax.axis_size("seq")
+        parts = list(outs[:1])
+        for step in range(sections):
+            pairs = [
+                (shard * sections + one, (shard ^ self.distance) * sections + (one + step) % sections)
+                for shard in range(count)
+                for one in range(sections)
+            ]
+            parts.append(lax.ppermute(outs[sections + step], ("seq", "section"), pairs))
+            if step > 0:
+                parts.append(shifted(outs[step], "section", step))
+        return parts
+
+
+def last_body(at_ref, *refs):
+    sections = at_ref.shape[0]
+    terms, outs, total_ref = refs[: -2 * sections - 1], refs[-2 * sections - 1 : -1], refs[-1]
+    share = outs[0].shape[0]
+    for place in range(2):
+        total_ref[place] = sum(ref[place].astype(F32) for ref in terms)
+        for step in range(sections):
+            span = pl.ds(pl.multiple_of(at_ref[step] * share, share), share)
+            outs[place * sections + step][...] = total_ref[place, span, :].astype(BF16)
+
+
+def section_body(sections, section_ref, *refs):
+    parts, (self_ref, cache_ref) = refs[:-2], refs[-2:]
+    section = section_ref[0]
+    groups = [[parts[0], parts[1]]] + [
+        [parts[2 * step], parts[2 * step + 1]] for step in range(1, sections)
+    ]
+    own = jnp.zeros(parts[0].shape, F32)
+    other = jnp.zeros(parts[0].shape, F32)
+    for step, group in enumerate(groups):
+        total = group[0][...].astype(F32) + group[1][...].astype(F32)
+        from_self = jnp.full(total.shape, section, jnp.int32) == step
+        own = own + jnp.where(from_self, total, 0.0)
+        other = other + jnp.where(from_self, 0.0, total)
+    half = own.shape[1] // 2
+    for kind in range(2):
+        self_ref[:, kind, :] = own[:, kind * half : (kind + 1) * half]
+        cache_ref[:, kind, :] = other[:, kind * half : (kind + 1) * half]
+
+
+def flip_body(value_ref, out_ref):
+    out_ref[...] = value_ref[...].astype(F32).T
+
+
+def same_body(value_ref, out_ref):
+    out_ref[...] = value_ref[...]
+
+
+def wide_body(value_ref, out_ref):
+    out_ref[...] = value_ref[...].astype(F32)
 
 
 def on_device(
@@ -609,6 +685,7 @@
         [me, *source_pieces, kv_flat],
         1,
         2 * rows * model * 2 * kv_cols,
+        limit=40,
         after=[meta],
     )
     all_kv = lax.all_gather(packed, "seq", axis=0, tiled=True)
@@ -650,17 +727,17 @@
         4 * rows * length * query_cols,
         [pltpu.VMEM((heads, rows, HEAD_DIM), F32)] * 2,
     )
-    grad_rows = whole_rows(grad_pieces, me, [attn_flat])
-    out_share, mark = scattered(grad_rows, attn_flat)
+    out_share, mark = scattered(grad_pieces, attn_flat)
     (grad_attn,) = call(
-        grad_attn_body,
+        functools.partial(grad_attn_body, tp_count),
         [struct((heads, rows, HEAD_DIM), BF16)],
-        [grad_rows, out_weight],
-        0,
+        [me, *grad_pieces, out_weight],
+        1,
         2 * rows * model * query_cols,
         after=[mark],
         grid=(heads // together,),
-        in_specs=[full]
+        in_specs=[SMEM]
+        + [whole] * tp_count
         + [pl.BlockSpec((together * HEAD_DIM, model), lambda i: (i, 0))],
         out_specs=[per_head],
     )
@@ -677,91 +754,113 @@
         after=[mark],
     )
     kv_came = [core_swap(piece) for piece in send]
-    query_share, mark = scattered(normed, grad_queries)
-    kv_sums, mark = sums_below(keep, kv_came, [mark])
-
-    def dots(value):
-        return [value] + [shifted(value, "tp", step) for step in range(1, tp_count)]
+    query_keep, query_low, query_high, _ = over_tokens(normed, grad_queries, natural=True)
+    kv_sums, mark, query_sum = sums_below(
+        keep, kv_came, [query_keep, core_swap(query_low), core_swap(query_high)], []
+    )
+    query_share = lax.psum_scatter(
+        query_sum.reshape(-1, query_cols),
+        "seq",
+        scatter_dimension=0,
+        tiled=True,
+        axis_index_groups=[[2 * one + core for one in range(chips)] for core in range(2)],
+    )
 
     wide = struct((rows, width), BF16)
     broad = struct((rows, HEAD_DIM), F32)
-    shapes = split_shapes(rows, width, tp_count)
-    projected = call(
+    projected, *projected_sent = call(
         functools.partial(project_body, tp_count),
-        shapes,
+        split_shapes(rows, width, tp_count, False),
         [me, attn_flat, out_weight],
         1,
         2 * rows * model * query_cols,
         after=[mark],
     )
-    projected_came = sent_over_tp(projected, rows)
-    *rows_parts, row_dot = call(
+    rows_part, *rows_sent, row_dot = call(
         functools.partial(back_body, tp_count),
-        shapes + [broad],
+        split_shapes(rows, width, tp_count, True) + [broad],
         [me, grad_queries, query_weight, *hidden_pieces],
         1,
         2 * rows * model * query_cols,
-        after=[projected[0]],
-    )
-    rows_came = sent_over_tp(rows_parts, rows)
-    row_dots = dots(row_dot)
-    *source_parts, source_dot, kv_grad = call(
-        functools.partial(key_back_body, tp_count, chips),
-        shapes + [broad, struct((rows, 2 * kv_cols), BF16)],
-        [me, key_raw, kv_flat, *kv_sums, *source_pieces],
+        after=[projected],
+    )
+    (kv_grad,) = call(
+        key_grad_body,
+        [struct((rows, 2 * kv_cols), BF16)],
+        [key_raw, *kv_sums],
+        0,
+        0,
+        after=[row_dot],
+        limit=16,
+    )
+    kv_keep, kv_low, kv_high, relayed = over_tokens(
+        source_normed, kv_grad, (), [*rows_sent, *projected_sent]
+    )
+    others = tp_count - 1
+    projected_came = sent_over_tp(relayed[others:])
+    rows_came = sent_over_tp(relayed[:others])
+    kv_sum = Halving(kv_keep, kv_low, kv_high)
+    source_part, *source_sent, source_dot = call(
+        functools.partial(back_body, tp_count),
+        split_shapes(rows, width, tp_count, True) + [broad],
+        [me, kv_grad, kv_flat, *source_pieces],
         1,
         4 * rows * model * kv_cols,
-        after=[row_dot],
-    )
-    source_came = sent_over_tp(source_parts, rows)
-    source_dots = dots(source_dot)
-    kv_keep, kv_send = over_tokens(source_normed, kv_grad)
-    kv_sum = Halving(kv_keep, kv_send)
-    (h_out,) = call(
-        output_body, [wide], [hidden, projected[0], *projected_came], 0, 0, after=[kv_keep]
-    )
-    passed = shifted(h_out, "section", 1)
+        after=[kv_keep],
+    )
+    mark, source_sent = kv_sum.step([source_dot], source_sent)
+    source_came = sent_over_tp(source_sent)
+    (h_out,) = call(output_body, [wide], [hidden, projected, *projected_came], 0, 0, after=[mark])
+    passed_came = shifted(h_out, "section", 1)
     mark = h_out
     while kv_sum.count > 2:
-        mark = kv_sum.step([mark])
+        mark, _ = kv_sum.step([mark])
+    kv_parts = kv_sum.finish([mark])
     (grad_input,) = call(
-        functools.partial(input_body, tp_count, True, model),
+        functools.partial(input_body, True, model),
         [wide],
-        [grad_local, hidden, row_factor, rows_parts[0], *row_dots, *rows_came],
-        0,
-        0,
-        after=[mark],
-    )
-    mark = kv_sum.step([grad_input])
+        [grad_local, hidden, row_factor, row_dot, rows_part, *rows_came],
+        0,
+        0,
+        after=[kv_parts[0]],
+    )
     (grad_memory,) = call(
-        functools.partial(input_body, tp_count, False, model),
+        functools.partial(input_body, False, model),
         [wide],
-        [source, source_factor, source_parts[0], *source_dots, *source_came],
-        0,
-        0,
-        after=[mark],
-    )
-    kv_share = kv_sum.last([grad_memory])
-
-    share_rows = kv_share.shape[0] // section_count
-    own = lax.dynamic_slice_in_dim(kv_share, section_id * share_rows, share_rows, 0)
-    self_grad = jnp.where(self_section, own, 0.0)
-    cache_grad = jnp.where(self_section, 0.0, own)
-    for step in range(1, section_count):
-        target = lax.rem(section_id + step, section_count)
-        piece = lax.dynamic_slice_in_dim(kv_share, target * share_rows, share_rows, 0)
-        came = shifted(piece.astype(BF16), "section", step).astype(F32)
-        from_self = section_id == step
-        self_grad = self_grad + jnp.where(from_self, came, 0.0)
-        cache_grad = cache_grad + jnp.where(from_self, 0.0, came)
+        [source, source_factor, source_dot, source_part, *source_came],
+        0,
+        0,
+        after=[grad_input],
+    )
+    (passed,) = call(same_body, [wide], [passed_came], 0, 0, after=[grad_memory])
+    (out_grad,) = call(
+        flip_body,
+        [struct((query_cols, out_share.shape[0]), F32)],
+        [out_share],
+        0,
+        0,
+        after=[passed],
+    )
+    (query_grad,) = call(
+        wide_body, [struct(query_share.shape, F32)], [query_share], 0, 0, after=[out_grad]
+    )
+    share_rows = kv_parts[0].shape[0]
+    self_grad, cache_grad = call(
+        functools.partial(section_body, section_count),
+        [struct((share_rows, 2, kv_cols), F32)] * 2,
+        [section_id.astype(jnp.int32).reshape(1), *kv_parts],
+        1,
+        0,
+        after=[query_grad],
+    )
     return (
         passed[None],
         grad_input[None],
         grad_memory[None],
-        query_share.astype(F32)[None],
-        out_share.astype(F32).T[None],
-        self_grad.reshape(share_rows, 2, kv_cols),
-        cache_grad.reshape(share_rows, 2, kv_cols),
+        query_grad[None],
+        out_grad[None],
+        self_grad,
+        cache_grad,
     )
 
 

time: 271 us -> 252 us (0.930)
  local copies, waits for them, and re-layouts: 22 us -> 13.5 us
  Pallas kernels: 81.2 us -> 74.6 us
  starting transfers between devices: 17.4 us -> 22.2 us
  waiting for transfers between devices: 113 us -> 109 us
  other arithmetic: 9.93 us -> 6.06 us
    ppermute x10 -> x8, waiting for transfers between devices: 59.6 us -> 30 us  [shifted(): return lax.ppermute(value, axis, pairs)]
    ppermute x2 -> x1, waiting for transfers between devices: 16.8 us -> 32.4 us  [step(): self.terms.append(lax.ppermute(sent, 'seq', pairs))]
    pallas_call x15 -> x17, Pallas kernels: 68.3 us -> 62.2 us  [call(): pl.pallas_call(with_order, out_shape=out_shape, grid=grid, in_specs=list(...]
    unnamed x73 -> x55, local copies, waits for them, and re-layouts: 18.4 us -> 13.3 us
    ppermute x0 -> x2, starting transfers between devices: none -> 3.84 us  [finish(): parts.append(lax.ppermute(outs[sections + step], ('seq', 'section'), pairs))]
    ppermute x0 -> x2, waiting for transfers between devices: none -> 3.52 us  [finish(): parts.append(lax.ppermute(outs[sections + step], ('seq', 'section'), pairs))]
    broadcast_in_dim x2 -> x0, other arithmetic: 3.3 us -> none  [the longest x1 2.15 us: on_device(): query_share.astype(F32)[None]]
    all_gather x1, waiting for transfers between devices: 0.01 us -> 2.97 us  [on_device(): all_kv = lax.all_gather(packed, 'seq', axis=0, tiled=True)]
  transfers between devices with their start and end apart: 26 -> 25, of which waited for: 13 -> 13; matrix products, arithmetic and copies ran while one was open for 6% -> 2% of each run, Pallas kernels for 25% -> 26%
where the time goes in v3:
time: 252 us; the launch traced here: 251 us
  waiting for transfers between devices  109 us (43%)
  Pallas kernels  74.6 us (30%)
  starting transfers between devices  22.2 us (9%)
  between operations  17.3 us (7%)
  local copies, waits for them, and re-layouts  13.5 us (5%)
  blocking collectives  9.17 us (4%)
  other arithmetic  6.06 us (2%)
    pallas_call x17, Pallas kernels, call(): pl.pallas_call(with_order, out_shape=out_shape, grid=grid, in_specs=list(...  62.2 us
    ppermute x3, waiting for transfers between devices, sums_below(): terms.append(lax.ppermute(sums[steps], 'seq', pairs))  35 us
    ppermute x1, waiting for transfers between devices, step(): self.terms.append(lax.ppermute(sent, 'seq', pairs))  32.4 us
    ppermute x8, waiting for transfers between devices, shifted(): return lax.ppermute(value, axis, pairs)  30 us
    unnamed x55, local copies, waits for them, and re-layouts  13.3 us
    pallas_call x5, Pallas kernels, ordered(): pl.pallas_call(with_order, out_shape=outs + [struct(value.shape, value.dt...  12.4 us
    ppermute x8, starting transfers between devices, shifted(): return lax.ppermute(value, axis, pairs)  11.7 us
    all_gather x1, blocking collectives, on_device(): all_docs = lax.all_gather(block_docs[0], 'seq', axis=0, tiled=True)  9.17 us
  transfers between devices with their start and end apart: 25, of which 13 were waited for; matrix products, arithmetic and copies ran while one was open for 2% of the time, Pallas kernels for 26%

profile of v3, /device:TPU:0, one launch (start us, length us, event | category | flops | bytes accessed | tf_op | source)
XLA Modules:
  0.0 251.3 jit_solution(2200018155410487685)
XLA Ops:
  7.2 2.3 bitcast_select_fusion.refs_1_.refs_3_.refs_0_
  9.6 2.9 %collective-permute-start.1 = (bf16[256,1536]{1,0:T(8,128)(2,1)}, bf16[256,1536]{1,0:T(8,128)(2,1)S(1)}, u32[]{:S(2)}, u32[]{:S(2)}) collective-permute-start(bf16[256,1536]{1,0:T(8,128)(2,1)} %bitcast_select_fusion.refs_1_.refs_3_.refs_0_), channel_id=1, source_target_pairs={{0,1},{1,0},{2,3},{3,2},{4,5},{5,4},{6,7},{7,6},{8,9},{9,8},{10,11... | collective-permute-start | bytes 2359304 | tf_op jit(solution)/shard_map/ppermute | solution.py:36
  13.9 9.2 %all-reduce = s32[16]{0:T(128)S(1)} all-reduce(s32[16]{0:T(128)S(1)} %bitcast_dynamic-update-slice_fusion), channel_id=2, replica_groups=mesh['seq'=8,'section'=2,'tp'=2] {'seq'}, use_global_device_ids=true, to_apply=%add | all-reduce | flops 16 | bytes 128 | tf_op jit(solution)/shard_map/all_gather | solution.py:665
  27.5 2.2 broadcast_select_fusion
  30.5 4.1 %shard_map.135 = (bf16[256,3072]{1,0:T(8,128)(2,1)S(1)}, f32[256,128]{1,0:T(8,128)S(1)}, bf16[256,512]{1,0:T(8,128)(2,1)}, f32[256,256]{1,0:T(8,128)S(1)}) custom-call(s32[1]{0:T(128)} %bitcast.1.refs_0_, bf16[256,1536]{1,0:T(8,128)(2,1)} %bitcast_select_fusion.refs_1_.refs_3_.refs_0_, bf16[256,1536]{1,0:T(8,128)(2,1)S(1)} %collective-permute-done.1.refs_2_.refs_4_, ...), custom_call_target="tpu_custom_call" | custom-call | flops 805306368 | bytes 6946820 | tf_op jit(solution)/shard_map/pallas_call | solution.py:54
  37.5 18.7 %collective-permute-done.refs_2_.refs_4_ = bf16[256,1536]{1,0:T(8,128)(2,1)} collective-permute-done((bf16[256,1536]{1,0:T(8,128)(2,1)}, bf16[256,1536]{1,0:T(8,128)(2,1)}, u32[]{:S(2)}, u32[]{:S(2)}) %collective-permute-start) | collective-permute-done | bytes 786464 | tf_op jit(solution)/shard_map/ppermute | solution.py:36
  56.2 6.3 %shard_map.136 = (bf16[256,3072]{1,0:T(8,128)(2,1)}, f32[256,128]{1,0:T(8,128)}, bf16[6,256,128]{2,1,0:T(8,128)(2,1)}, f32[6,256,128]{2,1,0:T(8,128)}) custom-call(s32[1]{0:T(128)} %bitcast.1.refs_0_, bf16[256,1536]{1,0:T(8,128)(2,1)} %bitcast.43, bf16[256,1536]{1,0:T(8,128)(2,1)} %collective-permute-done.refs_2_.refs_4_, bf16[3072,768]{1,0:T(8,128)(2,1)} %bitcast.49, ...), custom_call_target="tpu_custom_call" | custom-call | flops 1207959552 | bytes 9175044 | tf_op jit(solution)/shard_map/pallas_call | solution.py:54
  62.5 3.0 %all-gather.3.cloned.1.call-done.refs_2_.refs_6_ = bf16[2048,512]{1,0:T(8,128)(2,1)} async-done(((bf16[256,512]{1,0:T(8,128)(2,1)}), bf16[2048,512]{1,0:T(8,128)(2,1)}) %all-gather.3.cloned.1.call-update) | async-done | bytes 2097168 | tf_op jit(solution)/shard_map/all_gather | solution.py:691
  65.5 3.9 %shard_map.137 = (bf16[256,768]{1,0:T(8,128)(2,1)}, f32[6,256,128]{2,1,0:T(8,128)}) custom-call(s32[19]{0:T(128)} %copy-done.19, bf16[6,256,128]{2,1,0:T(8,128)(2,1)} %get-tuple-element.53.refs_1_, bf16[2048,512]{1,0:T(8,128)(2,1)} %all-gather.3.cloned.1.call-done.refs_2_.refs_6_), custom_call_target="tpu_custom_call" | custom-call | flops 1610612736 | bytes 3670092 | tf_op jit(solution)/shard_map/pallas_call | solution.py:54
  72.2 2.3 shard_map.138.refs_4_.refs_7_
  74.5 2.2 copy-done
  76.9 5.2 %shard_map.139.refs_3_ = bf16[6,256,128]{2,1,0:T(8,128)(2,1)} custom-call(s32[1]{0:T(128)} %bitcast.1.refs_0_, bf16[256,1536]{1,0:T(8,128)(2,1)} %bitcast.38, bf16[256,1536]{1,0:T(8,128)(2,1)} %copy-done.6, bf16[768,3072]{1,0:T(8,128)(2,1)} %bitcast.47, bf16[3072,768]{1,0:T(8,128)(2,1)} %copy-done), custom_call_target="tpu_custom_call" | custom-call | flops 1207959552 | bytes 6684676 | tf_op jit(solution)/shard_map/pallas_call | solution.py:54
  82.1 6.2 %shard_map.140 = (bf16[4,256,512]{2,1,0:T(8,128)(2,1)}, bf16[256,512]{1,0:T(8,128)(2,1)}, bf16[256,512]{1,0:T(8,128)(2,1)}, bf16[256,512]{1,0:T(8,128)(2,1)}, bf...) custom-call(s32[19]{0:T(128)} %copy-done.19, bf16[6,256,128]{2,1,0:T(8,128)(2,1)} %get-tuple-element.53.refs_1_, ...), custom_call_target="tpu_custom_call" | custom-call | flops 4026531840 | bytes 7340108 | tf_op jit(solution)/shard_map/pallas_call | solution.py:54
  89.3 3.4 %shard_map.141 = (bf16[4,384,768]{2,1,0:T(8,128)(2,1)S(1)}, bf16[2,384,768]{2,1,0:T(8,128)(2,1)S(1)}, bf16[2,384,768]{2,1,0:T(8,128)(2,1)S(1)}) custom-call(s32[5]{0:T(128)S(1)} %stack.60.refs_0_, bf16[256,3072]{1,0:T(8,128)(2,1)S(1)} %copy-done.9, bf16[256,768]{1,0:T(8,128)(2,1)S(1)} %copy-done.10), custom_call_target="tpu_custom_call" | custom-call | bytes 1024 | tf_op jit(solution)/shard_map/pallas_call | solution.py:378
  94.7 2.5 %collective-permute-done.3.refs_1_ = bf16[256,512]{1,0:T(8,128)(2,1)S(1)} collective-permute-done((bf16[256,512]{1,0:T(8,128)(2,1)}, bf16[256,512]{1,0:T(8,128)(2,1)S(1)}, u32[]{:S(2)}, u32[]{:S(2)}) %collective-permute-start.3) | collective-permute-done | bytes 262176 | tf_op jit(solution)/shard_map/ppermute | solution.py:453
  99.7 2.3 shard_map.142
  106.7 4.8 %shard_map.143 = (bf16[256,1536]{1,0:T(8,128)(2,1)}, bf16[256,1536]{1,0:T(8,128)(2,1)}) custom-call(s32[1]{0:T(128)} %bitcast.1.refs_0_, bf16[256,768]{1,0:T(8,128)(2,1)} %get-tuple-element.54.refs_3_.refs_4_.refs_1_, bf16[768,3072]{1,0:T(8,128)(2,1)} %bitcast.48, bf16[256,512]{1,0:T(8,128)(2,1)} %copy-done.12), custom_call_target="tpu_custom_call" | custom-call | flops 1207959552 | bytes 6684676 | tf_op jit(solution)/shard_map/pallas_call | solution.py:54
  111.5 5.7 %shard_map.144 = (bf16[256,1536]{1,0:T(8,128)(2,1)}, bf16[256,1664]{1,0:T(8,128)(2,1)}, f32[256,128]{1,0:T(8,128)}) custom-call(s32[1]{0:T(128)} %bitcast.1.refs_0_, bf16[256,768]{1,0:T(8,128)(2,1)} %get-tuple-element.63.refs_2_.refs_1_, bf16[3072,768]{1,0:T(8,128)(2,1)} %bitcast.50, bf16[256,1536]{1,0:T(8,128)(2,1)} %bitcast.44, ...), custom_call_target="tpu_custom_call" | custom-call | flops 1207959552 | bytes 8454148 | tf_op jit(solution)/shard_map/pallas_call | solution.py:54
  117.2 8.3 %collective-permute-done.9.refs_2_ = bf16[256,512]{1,0:T(8,128)(2,1)S(1)} collective-permute-done((bf16[256,512]{1,0:T(8,128)(2,1)}, bf16[256,512]{1,0:T(8,128)(2,1)S(1)}, u32[]{:S(2)}, u32[]{:S(2)}) %collective-permute-start.9) | collective-permute-done | bytes 262176 | tf_op jit(solution)/shard_map/ppermute | solution.py:526
  125.5 26.7 %collective-permute-done.10.refs_3_ = bf16[256,512]{1,0:T(8,128)(2,1)S(1)} collective-permute-done((bf16[256,512]{1,0:T(8,128)(2,1)S(1)}, bf16[256,512]{1,0:T(8,128)(2,1)S(1)}, u32[]{:S(2)}, u32[]{:S(2)}) %collective-permute-start.10) | collective-permute-done | bytes 262176 | tf_op jit(solution)/shard_map/ppermute | solution.py:526
  153.4 3.9 %shard_map.146 = (bf16[4,384,512]{2,1,0:T(8,128)(2,1)S(1)}, bf16[2,384,512]{2,1,0:T(8,128)(2,1)}, bf16[2,384,512]{2,1,0:T(8,128)(2,1)}, bf16[256,1664]{1,0:T(8,128)(2,1)}, bf16[256,1536]{1,0:T(8,128)(2,1)}) custom-call(s32[5]{0:T(128)S(1)} %stack.65.refs_0_, ...), custom_call_target="tpu_custom_call", output_to_operand_aliasing={{3}: (3, {}), {4}: (4, {})} | custom-call | bytes 1024 | tf_op jit(solution)/shard_map/pallas_call | solution.py:378
  160.8 5.2 %shard_map.147 = (bf16[256,1536]{1,0:T(8,128)(2,1)}, bf16[256,1664]{1,0:T(8,128)(2,1)}, f32[256,128]{1,0:T(8,128)}) custom-call(s32[1]{0:T(128)} %bitcast.1.refs_0_, bf16[256,512]{1,0:T(8,128)(2,1)} %copy-done.8, bf16[3072,512]{1,0:T(8,128)(2,1)} %bitcast.37, bf16[256,1536]{1,0:T(8,128)(2,1)} %bitcast_select_fusion.refs_1_.refs_3_.refs_0_, ...), custom_call_target="tpu_custom_call" | custom-call | flops 805306368 | bytes 6750212 | tf_op jit(solution)/shard_map/pallas_call | solution.py:54
  169.5 9.7 %collective-permute-done.12.refs_2_ = bf16[256,1536]{1,0:T(8,128)(2,1)} collective-permute-done((bf16[256,1536]{1,0:T(8,128)(2,1)}, bf16[256,1536]{1,0:T(8,128)(2,1)}, u32[]{:S(2)}, u32[]{:S(2)}) %collective-permute-start.12) | collective-permute-done | bytes 786464 | tf_op jit(solution)/shard_map/ppermute | solution.py:36
  179.2 2.8 %shard_map.149.refs_4_ = bf16[256,1536]{1,0:T(8,128)(2,1)} custom-call(bf16[256,1536]{1,0:T(8,128)(2,1)} %bitcast.45, bf16[256,1536]{1,0:T(8,128)(2,1)} %get-tuple-element.68.refs_5_.refs_1_, bf16[256,1536]{1,0:T(8,128)(2,1)} %collective-permute-done.12.refs_2_, bf16[2,384,512]{2,1,0:T(8,128)(2,1)} %get-tuple-element.82.refs_3_), custom_call_target="tpu_custom_call" | custom-call | bytes 3145728 | tf_op jit(solution)/shard_map/pallas_call | solution.py:54
  182.0 2.6 %collective-permute-start.14 = (bf16[256,1536]{1,0:T(8,128)(2,1)}, bf16[256,1536]{1,0:T(8,128)(2,1)}, u32[]{:S(2)}, u32[]{:S(2)}) collective-permute-start(bf16[256,1536]{1,0:T(8,128)(2,1)} %shard_map.149.refs_4_), channel_id=1, source_target_pairs={{0,2},{2,0},{1,3},{3,1},{4,6},{6,4},{5,7},{7,5},{8,10},{10,8},{9,1... | collective-permute-start | bytes 2359304 | tf_op jit(solution)/shard_map/ppermute | solution.py:36
  184.7 32.4 %collective-permute-done.18.refs_3_ = bf16[2,384,512]{2,1,0:T(8,128)(2,1)S(1)} collective-permute-done((bf16[2,384,512]{2,1,0:T(8,128)(2,1)}, bf16[2,384,512]{2,1,0:T(8,128)(2,1)S(1)}, u32[]{:S(2)}, u32[]{:S(2)}) %collective-permute-start.18) | collective-permute-done | bytes 786464 | tf_op jit(solution)/shard_map/ppermute | solution.py:545
  221.2 3.3 %collective-permute-start.20 = (bf16[192,512]{1,0:T(8,128)(2,1)S(1)}, bf16[192,512]{1,0:T(8,128)(2,1)S(1)}, u32[]{:S(2)}, u32[]{:S(2)}) collective-permute-start(bf16[192,512]{1,0:T(8,128)(2,1)S(1)} %get-tuple-element.93), channel_id=1, source_target_pairs={{0,18},{2,16},{4,22},{6,20},{8,26},{10,24},{12,30},{14,28},{16,2},... | collective-permute-start | bytes 589832 | tf_op jit(solution)/shard_map/ppermute | solution.py:577
  225.1 3.4 %shard_map.151.refs_5_ = bf16[256,1536]{1,0:T(8,128)(2,1)} custom-call(bf16[256,1536]{1,0:T(8,128)(2,1)} %bitcast.39, bf16[256,1536]{1,0:T(8,128)(2,1)} %bitcast.46, f32[256,128]{1,0:T(8,128)} %get-tuple-element.86.refs_2_, f32[256,128]{1,0:T(8,128)} %get-tuple-element.74.refs_5_.refs_3_, bf16[256,1536]{1,0:T(8,128)(2,1)} %get-tuple-element.87.refs_4_, ...), custom_call_target="tpu_custom_call" | custom-call | bytes 4259840 | tf_op jit(solution)/shard_map/pallas_call | solution.py:54
  228.5 3.1 %shard_map.152.refs_1_ = bf16[256,1536]{1,0:T(8,128)(2,1)} custom-call(bf16[256,1536]{1,0:T(8,128)(2,1)} %bitcast_select_fusion.refs_1_.refs_3_.refs_0_, f32[256,128]{1,0:T(8,128)} %copy-done.18, f32[256,128]{1,0:T(8,128)} %get-tuple-element.80.refs_3_.refs_2_, bf16[256,1536]{1,0:T(8,128)(2,1)} %get-tuple-element.84.refs_3_, ...), custom_call_target="tpu_custom_call" | custom-call | bytes 3473408 | tf_op jit(solution)/shard_map/pallas_call | solution.py:54
  233.6 2.3 shard_map.154.refs_1_
  238.1 3.5 %collective-permute-done.20.refs_3_ = bf16[192,512]{1,0:T(8,128)(2,1)S(1)} collective-permute-done((bf16[192,512]{1,0:T(8,128)(2,1)S(1)}, bf16[192,512]{1,0:T(8,128)(2,1)S(1)}, u32[]{:S(2)}, u32[]{:S(2)}) %collective-permute-start.20) | collective-permute-done | bytes 196640 | tf_op jit(solution)/shard_map/ppermute | solution.py:577
  242.4 2.4 shard_map.156
  (107 shorter events, 37.1 us)
Async XLA Ops:
  7.2 5.4 %copy-start.24 = (u32[32]{0:T(128)S(1)}, u32[32]{0:T(128)}, u32[]{:S(2)}) copy-start(u32[32]{0:T(128)} %constant.102) | copy-start | bytes 388
  7.2 6.6 %copy-start.23 = (s32[1,2]{1,0:T(1,128)S(1)}, s32[1,2]{1,0:T(1,128)}, u32[]{:S(2)}) copy-start(s32[1,2]{1,0:T(1,128)} %param.11) | copy-start | bytes 28
  7.2 58.3 %all-gather.3.cloned.1.call-start = ((), (), s32[]{:S(2)}) async-start(), calls=%async_computation.2 | async-start | bytes 2359296 | tf_op jit(solution)/shard_map/all_gather | solution.py:691
  9.6 20.9 %collective-permute-start.1 = (bf16[256,1536]{1,0:T(8,128)(2,1)}, bf16[256,1536]{1,0:T(8,128)(2,1)S(1)}, u32[]{:S(2)}, u32[]{:S(2)}) collective-permute-start(bf16[256,1536]{1,0:T(8,128)(2,1)} %bitcast_select_fusion.refs_1_.refs_3_.refs_0_), channel_id=1, source_target_pairs={{0,1},{1,0},{2,3},{3,2},{4,5},{5,4},{6,7},{7,6},{8,9},{9,8},{10,11... | collective-permute-start | bytes 2359304 | tf_op jit(solution)/shard_map/ppermute | solution.py:36
  30.5 6.0 %copy-start.4 = (bf16[1,256,1536]{2,1,0:T(8,128)(2,1)S(1)}, bf16[1,256,1536]{2,1,0:T(8,128)(2,1)}, u32[]{:S(2)}) copy-start(bf16[1,256,1536]{2,1,0:T(8,128)(2,1)} %param.10) | copy-start | bytes 2359300
  35.3 198.3 %reduce-scatter.5.cloned.1.call-start = ((), (), s32[]{:S(2)}) async-start(), calls=%async_computation.4 | async-start | bytes 5308416 | tf_op jit(solution)/shard_map/reduce_scatter | solution.py:496
  35.4 20.9 %collective-permute-start = (bf16[256,1536]{1,0:T(8,128)(2,1)}, bf16[256,1536]{1,0:T(8,128)(2,1)}, u32[]{:S(2)}, u32[]{:S(2)}) collective-permute-start(bf16[256,1536]{1,0:T(8,128)(2,1)} %bitcast.42), channel_id=1, source_target_pairs={{0,1},{1,0},{2,3},{3,2},{4,5},{5,4},{6,7},{7,6},{8,9},{9,8},{10,11... | collective-permute-start | bytes 2359304 | tf_op jit(solution)/shard_map/ppermute | solution.py:36
  36.6 34.4 %collective-permute-start.2 = (bf16[256,1536]{1,0:T(8,128)(2,1)S(1)}, bf16[256,1536]{1,0:T(8,128)(2,1)S(1)}, u32[]{:S(2)}, u32[]{:S(2)}) collective-permute-start(bf16[256,1536]{1,0:T(8,128)(2,1)S(1)} %bitcast.40), channel_id=1, source_target_pairs={{0,1},{1,0},{2,3},{3,2},{4,5},{5,4},{6,7},{7,6},{8,9},{9,8},{10,11... | collective-permute-start | bytes 2359304 | tf_op jit(solution)/shard_map/ppermute | solution.py:36
  76.7 159.2 %reduce-scatter.3.cloned.1.call-start = ((), (), s32[]{:S(2)}) async-start(), calls=%async_computation.3 | async-start | bytes 2949120 | tf_op jit(solution)/shard_map/reduce_scatter | solution.py:761
  82.1 6.2 %copy-start.9 = (bf16[256,3072]{1,0:T(8,128)(2,1)S(1)}, bf16[256,3072]{1,0:T(8,128)(2,1)}, u32[]{:S(2)}) copy-start(bf16[256,3072]{1,0:T(8,128)(2,1)} %get-tuple-element.62.refs_1_) | copy-start | bytes 4718596
  89.3 10.4 %copy-start.14 = (bf16[4,256,512]{2,1,0:T(8,128)(2,1)S(1)}, bf16[4,256,512]{2,1,0:T(8,128)(2,1)}, u32[]{:S(2)}) copy-start(bf16[4,256,512]{2,1,0:T(8,128)(2,1)} %get-tuple-element.57.refs_0_) | copy-start | bytes 3145732
  92.7 6.9 %collective-permute-start.7 = (bf16[2,384,768]{2,1,0:T(8,128)(2,1)S(1)}, bf16[2,384,768]{2,1,0:T(8,128)(2,1)S(1)}, u32[]{:S(2)}, u32[]{:S(2)}) collective-permute-start(bf16[2,384,768]{2,1,0:T(8,128)(2,1)S(1)} %get-tuple-element.65), channel_id=1, source_target_pairs={{0,4},{4,0},{8,12},{12,8},{16,20},{20,16},{24,28},{28,24},{1,5},{5... | collective-permute-start | bytes 3538952 | tf_op jit(solution)/shard_map/ppermute | solution.py:453
  93.7 6.0 %collective-permute-start.8 = (bf16[2,384,768]{2,1,0:T(8,128)(2,1)S(1)}, bf16[2,384,768]{2,1,0:T(8,128)(2,1)S(1)}, u32[]{:S(2)}, u32[]{:S(2)}) collective-permute-start(bf16[2,384,768]{2,1,0:T(8,128)(2,1)S(1)} %get-tuple-element.66), channel_id=1, source_target_pairs={{0,4},{4,0},{8,12},{12,8},{16,20},{20,16},{24,28},{28,24},{1,5},{5... | collective-permute-start | bytes 3538952 | tf_op jit(solution)/shard_map/ppermute | solution.py:453
  93.8 3.5 %collective-permute-start.3 = (bf16[256,512]{1,0:T(8,128)(2,1)}, bf16[256,512]{1,0:T(8,128)(2,1)S(1)}, u32[]{:S(2)}, u32[]{:S(2)}) collective-permute-start(bf16[256,512]{1,0:T(8,128)(2,1)} %get-tuple-element.58), channel_id=1, source_target_pairs={{0,4},{4,0},{8,12},{12,8},{16,20},{20,16},{24,28},{28,24},{1,5},{5... | collective-permute-start | bytes 786440 | tf_op jit(solution)/shard_map/ppermute | solution.py:453
  94.2 3.8 %collective-permute-start.4 = (bf16[256,512]{1,0:T(8,128)(2,1)}, bf16[256,512]{1,0:T(8,128)(2,1)S(1)}, u32[]{:S(2)}, u32[]{:S(2)}) collective-permute-start(bf16[256,512]{1,0:T(8,128)(2,1)} %get-tuple-element.59), channel_id=1, source_target_pairs={{0,4},{4,0},{8,12},{12,8},{16,20},{20,16},{24,28},{28,24},{1,5},{5... | collective-permute-start | bytes 786440 | tf_op jit(solution)/shard_map/ppermute | solution.py:453
  94.3 4.6 %collective-permute-start.5 = (bf16[256,512]{1,0:T(8,128)(2,1)}, bf16[256,512]{1,0:T(8,128)(2,1)S(1)}, u32[]{:S(2)}, u32[]{:S(2)}) collective-permute-start(bf16[256,512]{1,0:T(8,128)(2,1)} %get-tuple-element.60), channel_id=1, source_target_pairs={{0,4},{4,0},{8,12},{12,8},{16,20},{20,16},{24,28},{28,24},{1,5},{5... | collective-permute-start | bytes 786440 | tf_op jit(solution)/shard_map/ppermute | solution.py:453
  97.2 2.4 collective-permute-start.6
  102.7 22.8 %collective-permute-start.9 = (bf16[256,512]{1,0:T(8,128)(2,1)}, bf16[256,512]{1,0:T(8,128)(2,1)S(1)}, u32[]{:S(2)}, u32[]{:S(2)}) collective-permute-start(bf16[256,512]{1,0:T(8,128)(2,1)} %get-tuple-element.71), channel_id=1, source_target_pairs={{8,0},{12,4},{16,8},{20,12},{24,16},{28,20},{9,1},{13,5},{17,9},{2... | collective-permute-start | bytes 786440 | tf_op jit(solution)/shard_map/ppermute | solution.py:526
  104.0 48.2 %collective-permute-start.10 = (bf16[256,512]{1,0:T(8,128)(2,1)S(1)}, bf16[256,512]{1,0:T(8,128)(2,1)S(1)}, u32[]{:S(2)}, u32[]{:S(2)}) collective-permute-start(bf16[256,512]{1,0:T(8,128)(2,1)S(1)} %get-tuple-element.72), channel_id=1, source_target_pairs={{16,0},{20,4},{24,8},{28,12},{17,1},{21,5},{25,9},{29,13},{18,2},{... | collective-permute-start | bytes 786440 | tf_op jit(solution)/shard_map/ppermute | solution.py:526
  105.3 46.9 %collective-permute-start.11 = (bf16[256,512]{1,0:T(8,128)(2,1)S(1)}, bf16[256,512]{1,0:T(8,128)(2,1)S(1)}, u32[]{:S(2)}, u32[]{:S(2)}) collective-permute-start(bf16[256,512]{1,0:T(8,128)(2,1)S(1)} %get-tuple-element.73), channel_id=1, source_target_pairs={{24,0},{28,4},{25,1},{29,5},{26,2},{30,6},{27,3},{31,7}} | collective-permute-start | bytes 786440 | tf_op jit(solution)/shard_map/ppermute | solution.py:526
  111.5 40.7 %copy-start.13 = (bf16[256,512]{1,0:T(8,128)(2,1)S(1)}, bf16[256,512]{1,0:T(8,128)(2,1)}, u32[]{:S(2)}) copy-start(bf16[256,512]{1,0:T(8,128)(2,1)} %copy-done.12) | copy-start | bytes 786436
  153.4 7.4 %copy-start.8 = (bf16[256,512]{1,0:T(8,128)(2,1)}, bf16[256,512]{1,0:T(8,128)(2,1)S(1)}, u32[]{:S(2)}) copy-start(bf16[256,512]{1,0:T(8,128)(2,1)S(1)} %shard_map.145.refs_2_.refs_1_) | copy-start | bytes 786436
  158.5 7.5 %collective-permute-start.13 = (bf16[2,384,512]{2,1,0:T(8,128)(2,1)}, bf16[2,384,512]{2,1,0:T(8,128)(2,1)S(1)}, u32[]{:S(2)}, u32[]{:S(2)}) collective-permute-start(bf16[2,384,512]{2,1,0:T(8,128)(2,1)} %get-tuple-element.79), channel_id=1, source_target_pairs={{0,4},{4,0},{8,12},{12,8},{16,20},{20,16},{24,28},{28,24},{1,5},{5... | collective-permute-start | bytes 2359304 | tf_op jit(solution)/shard_map/ppermute | solution.py:453
  158.5 20.7 %collective-permute-start.12 = (bf16[256,1536]{1,0:T(8,128)(2,1)}, bf16[256,1536]{1,0:T(8,128)(2,1)}, u32[]{:S(2)}, u32[]{:S(2)}) collective-permute-start(bf16[256,1536]{1,0:T(8,128)(2,1)} %get-tuple-element.77), channel_id=1, source_target_pairs={{0,1},{1,0},{2,3},{3,2},{4,5},{5,4},{6,7},{7,6},{8,9},{9,8},{10,11... | collective-permute-start | bytes 2359304 | tf_op jit(solution)/shard_map/ppermute | solution.py:36
  160.0 24.7 %collective-permute-start.17 = (bf16[2,384,512]{2,1,0:T(8,128)(2,1)}, bf16[2,384,512]{2,1,0:T(8,128)(2,1)S(1)}, u32[]{:S(2)}, u32[]{:S(2)}) collective-permute-start(bf16[2,384,512]{2,1,0:T(8,128)(2,1)} %get-tuple-element.89), channel_id=1, source_target_pairs={{0,4},{4,0},{8,12},{12,8},{16,20},{20,16},{24,28},{28,24},{1,5},{5... | collective-permute-start | bytes 2359304 | tf_op jit(solution)/shard_map/ppermute | solution.py:453
  160.2 64.3 %collective-permute-start.16 = (bf16[256,1664]{1,0:T(8,128)(2,1)}, bf16[256,1664]{1,0:T(8,128)(2,1)}, u32[]{:S(2)}, u32[]{:S(2)}) collective-permute-start(bf16[256,1664]{1,0:T(8,128)(2,1)} %get-tuple-element.88), channel_id=1, source_target_pairs={{0,1},{1,0},{2,3},{3,2},{4,5},{5,4},{6,7},{7,6},{8,9},{9,8},{10,11... | collective-permute-start | bytes 2555912 | tf_op jit(solution)/shard_map/ppermute | solution.py:36
  168.0 49.2 %collective-permute-start.18 = (bf16[2,384,512]{2,1,0:T(8,128)(2,1)}, bf16[2,384,512]{2,1,0:T(8,128)(2,1)S(1)}, u32[]{:S(2)}, u32[]{:S(2)}) collective-permute-start(bf16[2,384,512]{2,1,0:T(8,128)(2,1)} %get-tuple-element.82.refs_3_), channel_id=1, source_target_pairs={{0,8},{4,12},{8,0},{12,4},{16,24},{20,28},{24,16},{28,20},{1,9},{5... | collective-permute-start | bytes 2359304 | tf_op jit(solution)/shard_map/ppermute | solution.py:545
  168.0 60.5 %collective-permute-start.15 = (bf16[256,1664]{1,0:T(8,128)(2,1)}, bf16[256,1664]{1,0:T(8,128)(2,1)}, u32[]{:S(2)}, u32[]{:S(2)}) collective-permute-start(bf16[256,1664]{1,0:T(8,128)(2,1)} %get-tuple-element.85), channel_id=1, source_target_pairs={{0,1},{1,0},{2,3},{3,2},{4,5},{5,4},{6,7},{7,6},{8,9},{9,8},{10,11... | collective-permute-start | bytes 2555912 | tf_op jit(solution)/shard_map/ppermute | solution.py:36
  182.0 49.6 %collective-permute-start.14 = (bf16[256,1536]{1,0:T(8,128)(2,1)}, bf16[256,1536]{1,0:T(8,128)(2,1)}, u32[]{:S(2)}, u32[]{:S(2)}) collective-permute-start(bf16[256,1536]{1,0:T(8,128)(2,1)} %shard_map.149.refs_4_), channel_id=1, source_target_pairs={{0,2},{2,0},{1,3},{3,1},{4,6},{6,4},{5,7},{7,5},{8,10},{10,8},{9,1... | collective-permute-start | bytes 2359304 | tf_op jit(solution)/shard_map/ppermute | solution.py:36
  220.7 17.4 %collective-permute-start.19 = (bf16[192,512]{1,0:T(8,128)(2,1)}, bf16[192,512]{1,0:T(8,128)(2,1)S(1)}, u32[]{:S(2)}, u32[]{:S(2)}) collective-permute-start(bf16[192,512]{1,0:T(8,128)(2,1)} %get-tuple-element.92), channel_id=1, source_target_pairs={{0,16},{2,18},{4,20},{6,22},{8,24},{10,26},{12,28},{14,30},{16,0},... | collective-permute-start | bytes 589832 | tf_op jit(solution)/shard_map/ppermute | solution.py:577
  221.2 20.4 %collective-permute-start.20 = (bf16[192,512]{1,0:T(8,128)(2,1)S(1)}, bf16[192,512]{1,0:T(8,128)(2,1)S(1)}, u32[]{:S(2)}, u32[]{:S(2)}) collective-permute-start(bf16[192,512]{1,0:T(8,128)(2,1)S(1)} %get-tuple-element.93), channel_id=1, source_target_pairs={{0,18},{2,16},{4,22},{6,20},{8,26},{10,24},{12,30},{14,28},{16,2},... | collective-permute-start | bytes 589832 | tf_op jit(solution)/shard_map/ppermute | solution.py:577
  224.5 17.1 %collective-permute-start.21 = (bf16[192,512]{1,0:T(8,128)(2,1)S(1)}, bf16[192,512]{1,0:T(8,128)(2,1)S(1)}, u32[]{:S(2)}, u32[]{:S(2)}) collective-permute-start(bf16[192,512]{1,0:T(8,128)(2,1)S(1)} %get-tuple-element.94), channel_id=1, source_target_pairs={{0,2},{2,0},{1,3},{3,1},{4,6},{6,4},{5,7},{7,5},{8,10},{10,8},{9,1... | collective-permute-start | bytes 589832 | tf_op jit(solution)/shard_map/ppermute | solution.py:36
  (18 other events, 36.8 us)
Sparse Core Ops, SparseCore 0:
  35.4 29.9 all-gather.2
  76.8 72.0 reduce-scatter.4
  151.2 69.1 reduce-scatter.2

commit v4 on v3

--- a/solution.py
+++ b/solution.py
@@ -306,7 +306,7 @@
     grad_ref[:, half:] = total[:, half:].astype(BF16)
 
 
-def output_body(hidden_ref, own_ref, *refs):
+def output_body(at_ref, hidden_ref, own_ref, *refs):
     total = hidden_ref[...].astype(F32) + sum(ref[...].astype(F32) for ref in (own_ref, *refs[:-1]))
     refs[-1][...] = total.astype(BF16)
 
@@ -800,49 +800,61 @@
     projected_came = sent_over_tp(relayed[others:])
     rows_came = sent_over_tp(relayed[:others])
     kv_sum = Halving(kv_keep, kv_low, kv_high)
+    mark, _ = kv_sum.step([kv_keep])
     source_part, *source_sent, source_dot = call(
         functools.partial(back_body, tp_count),
         split_shapes(rows, width, tp_count, True) + [broad],
         [me, kv_grad, kv_flat, *source_pieces],
         1,
         4 * rows * model * kv_cols,
-        after=[kv_keep],
-    )
-    mark, source_sent = kv_sum.step([source_dot], source_sent)
+        after=[mark],
+    )
+    tile = pl.BlockSpec((rows, width), lambda i, at: (0, 0))
+    h_out, *source_sent = ordered(
+        output_body,
+        [hidden, projected, *projected_came],
+        [source_dot],
+        [wide],
+        (1,),
+        [tile] * (2 + others),
+        [tile],
+        jnp.zeros((1,), jnp.int32),
+        source_sent,
+    )
     source_came = sent_over_tp(source_sent)
-    (h_out,) = call(output_body, [wide], [hidden, projected, *projected_came], 0, 0, after=[mark])
     passed_came = shifted(h_out, "section", 1)
     mark = h_out
-    while kv_sum.count > 2:
-        mark, _ = kv_sum.step([mark])
-    kv_parts = kv_sum.finish([mark])
+    (out_grad,) = call(
+        flip_body,
+        [struct((query_cols, out_share.shape[0]), F32)],
+        [out_share],
+        0,
+        0,
+        after=[h_out],
+    )
     (grad_input,) = call(
         functools.partial(input_body, True, model),
         [wide],
         [grad_local, hidden, row_factor, row_dot, rows_part, *rows_came],
         0,
         0,
-        after=[kv_parts[0]],
-    )
+        after=[out_grad],
+    )
+    mark = grad_input
+    while kv_sum.count > 2:
+        mark, _ = kv_sum.step([mark])
+    kv_parts = kv_sum.finish([mark])
     (grad_memory,) = call(
         functools.partial(input_body, False, model),
         [wide],
         [source, source_factor, source_dot, source_part, *source_came],
         0,
         0,
-        after=[grad_input],
+        after=[kv_parts[0]],
     )
     (passed,) = call(same_body, [wide], [passed_came], 0, 0, after=[grad_memory])
-    (out_grad,) = call(
-        flip_body,
-        [struct((query_cols, out_share.shape[0]), F32)],
-        [out_share],
-        0,
-        0,
-        after=[passed],
-    )
     (query_grad,) = call(
-        wide_body, [struct(query_share.shape, F32)], [query_share], 0, 0, after=[out_grad]
+        wide_body, [struct(query_share.shape, F32)], [query_share], 0, 0, after=[passed]
     )
     share_rows = kv_parts[0].shape[0]
     self_grad, cache_grad = call(

time: 252 us -> 245 us (0.972)
  waiting for transfers between devices: 109 us -> 99.8 us
  Pallas kernels: 74.6 us -> 71.3 us
  starting transfers between devices: 22.2 us -> 25.2 us
  local copies, waits for them, and re-layouts: 13.5 us -> 16.3 us
    ppermute x1, waiting for transfers between devices: 32.4 us -> 12.5 us  [step(): self.terms.append(lax.ppermute(sent, 'seq', pairs))]
    ppermute x8, waiting for transfers between devices: 30 us -> 39.2 us  [shifted(): return lax.ppermute(value, axis, pairs)]
    pallas_call x17 -> x16, Pallas kernels: 62.2 us -> 57 us  [call(): pl.pallas_call(with_order, out_shape=out_shape, grid=grid, in_specs=list(...]
    ppermute x2, starting transfers between devices: 3.84 us -> 6.68 us  [finish(): parts.append(lax.ppermute(outs[sections + step], ('seq', 'section'), pairs))]
    unnamed x55 -> x67, local copies, waits for them, and re-layouts: 13.3 us -> 16.1 us
    pallas_call x5 -> x6, Pallas kernels: 12.4 us -> 14.3 us  [ordered(): pl.pallas_call(with_order, out_shape=outs + [struct(value.shape, value.dt...]
  transfers between devices with their start and end apart: 25 -> 25, of which waited for: 13 -> 14; matrix products, arithmetic and copies ran while one was open for 2% -> 2% of each run, Pallas kernels for 26% -> 26%
where the time goes in v4:
time: 245 us; the launch traced here: 244 us
  waiting for transfers between devices  99.8 us (41%)
  Pallas kernels  71.3 us (29%)
  starting transfers between devices  25.2 us (10%)
  between operations  17.4 us (7%)
  local copies, waits for them, and re-layouts  16.3 us (7%)
  blocking collectives  9.17 us (4%)
  other arithmetic  5.19 us (2%)
    pallas_call x16, Pallas kernels, call(): pl.pallas_call(with_order, out_shape=out_shape, grid=grid, in_specs=list(...  57 us
    ppermute x8, waiting for transfers between devices, shifted(): return lax.ppermute(value, axis, pairs)  39.2 us
    ppermute x3, waiting for transfers between devices, sums_below(): terms.append(lax.ppermute(sums[steps], 'seq', pairs))  35.1 us
    unnamed x67, local copies, waits for them, and re-layouts  16.1 us
    pallas_call x6, Pallas kernels, ordered(): pl.pallas_call(with_order, out_shape=outs + [struct(value.shape, value.dt...  14.3 us
    ppermute x1, waiting for transfers between devices, step(): self.terms.append(lax.ppermute(sent, 'seq', pairs))  12.5 us
    ppermute x8, starting transfers between devices, shifted(): return lax.ppermute(value, axis, pairs)  11.4 us
    all_gather x1, blocking collectives, on_device(): all_docs = lax.all_gather(block_docs[0], 'seq', axis=0, tiled=True)  9.17 us
  transfers between devices with their start and end apart: 25, of which 14 were waited for; matrix products, arithmetic and copies ran while one was open for 2% of the time, Pallas kernels for 26%

profile of v4, /device:TPU:0, one launch (start us, length us, event | category | flops | bytes accessed | tf_op | source)
XLA Modules:
  0.0 244.3 jit_solution(17510175850107489234)
XLA Ops:
  8.7 3.0 %collective-permute-start.1 = (bf16[256,1536]{1,0:T(8,128)(2,1)S(1)}, bf16[256,1536]{1,0:T(8,128)(2,1)S(1)}, u32[]{:S(2)}, u32[]{:S(2)}) collective-permute-start(bf16[256,1536]{1,0:T(8,128)(2,1)S(1)} %bitcast_select_fusion.refs_1_.refs_3_.refs_0_), channel_id=1, source_target_pairs={{0,1},{1,0},{2,3},{3,2},{4,5},{5,4},{6,7},{7,6},{8,9},{9,8},{10,11... | collective-permute-start | bytes 2359304 | tf_op jit(solution)/shard_map/ppermute | solution.py:36
  13.1 9.2 %all-reduce = s32[16]{0:T(128)S(1)} all-reduce(s32[16]{0:T(128)S(1)} %bitcast_dynamic-update-slice_fusion), channel_id=2, replica_groups=mesh['seq'=8,'section'=2,'tp'=2] {'seq'}, use_global_device_ids=true, to_apply=%add | all-reduce | flops 16 | bytes 128 | tf_op jit(solution)/shard_map/all_gather | solution.py:665
  26.7 2.2 broadcast_select_fusion
  29.8 2.3 shard_map.135
  36.2 18.5 %collective-permute-done.refs_2_.refs_4_ = bf16[256,1536]{1,0:T(8,128)(2,1)} collective-permute-done((bf16[256,1536]{1,0:T(8,128)(2,1)S(1)}, bf16[256,1536]{1,0:T(8,128)(2,1)}, u32[]{:S(2)}, u32[]{:S(2)}) %collective-permute-start) | collective-permute-done | bytes 786464 | tf_op jit(solution)/shard_map/ppermute | solution.py:36
  54.6 6.3 %shard_map.136 = (bf16[256,3072]{1,0:T(8,128)(2,1)}, f32[256,128]{1,0:T(8,128)}, bf16[6,256,128]{2,1,0:T(8,128)(2,1)}, f32[6,256,128]{2,1,0:T(8,128)}) custom-call(s32[1]{0:T(128)} %bitcast.1.refs_0_, bf16[256,1536]{1,0:T(8,128)(2,1)} %bitcast.38, bf16[256,1536]{1,0:T(8,128)(2,1)} %collective-permute-done.refs_2_.refs_4_, bf16[3072,768]{1,0:T(8,128)(2,1)} %bitcast.50, ...), custom_call_target="tpu_custom_call" | custom-call | flops 1207959552 | bytes 9175044 | tf_op jit(solution)/shard_map/pallas_call | solution.py:54
  60.9 3.3 %all-gather.3.cloned.1.call-done.refs_2_.refs_6_ = bf16[2048,512]{1,0:T(8,128)(2,1)} async-done(((bf16[256,512]{1,0:T(8,128)(2,1)}), bf16[2048,512]{1,0:T(8,128)(2,1)}) %all-gather.3.cloned.1.call-update) | async-done | bytes 2097168 | tf_op jit(solution)/shard_map/all_gather | solution.py:691
  64.2 3.9 %shard_map.137 = (bf16[256,768]{1,0:T(8,128)(2,1)}, f32[6,256,128]{2,1,0:T(8,128)}) custom-call(s32[19]{0:T(128)} %copy-done.24, bf16[6,256,128]{2,1,0:T(8,128)(2,1)} %get-tuple-element.53.refs_1_, bf16[2048,512]{1,0:T(8,128)(2,1)} %all-gather.3.cloned.1.call-done.refs_2_.refs_6_), custom_call_target="tpu_custom_call" | custom-call | flops 1610612736 | bytes 3670092 | tf_op jit(solution)/shard_map/pallas_call | solution.py:54
  70.4 2.3 shard_map.138.refs_4_.refs_7_
  72.7 2.2 copy-done
  75.0 5.2 %shard_map.139.refs_3_ = bf16[6,256,128]{2,1,0:T(8,128)(2,1)} custom-call(s32[1]{0:T(128)} %bitcast.1.refs_0_, bf16[256,1536]{1,0:T(8,128)(2,1)} %bitcast.43, bf16[256,1536]{1,0:T(8,128)(2,1)} %copy-done.8, bf16[768,3072]{1,0:T(8,128)(2,1)} %bitcast.48, bf16[3072,768]{1,0:T(8,128)(2,1)} %copy-done), custom_call_target="tpu_custom_call" | custom-call | flops 1207959552 | bytes 6684676 | tf_op jit(solution)/shard_map/pallas_call | solution.py:54
  80.2 6.1 %shard_map.140 = (bf16[4,256,512]{2,1,0:T(8,128)(2,1)}, bf16[256,512]{1,0:T(8,128)(2,1)}, bf16[256,512]{1,0:T(8,128)(2,1)}, bf16[256,512]{1,0:T(8,128)(2,1)}, bf...) custom-call(s32[19]{0:T(128)} %copy-done.24, bf16[6,256,128]{2,1,0:T(8,128)(2,1)} %get-tuple-element.53.refs_1_, ...), custom_call_target="tpu_custom_call" | custom-call | flops 4026531840 | bytes 7340108 | tf_op jit(solution)/shard_map/pallas_call | solution.py:54
  87.3 3.4 %shard_map.141 = (bf16[4,384,768]{2,1,0:T(8,128)(2,1)S(1)}, bf16[2,384,768]{2,1,0:T(8,128)(2,1)S(1)}, bf16[2,384,768]{2,1,0:T(8,128)(2,1)S(1)}) custom-call(s32[5]{0:T(128)S(1)} %stack.60.refs_0_, bf16[256,3072]{1,0:T(8,128)(2,1)S(1)} %copy-done.14, bf16[256,768]{1,0:T(8,128)(2,1)S(1)} %copy-done.15), custom_call_target="tpu_custom_call" | custom-call | bytes 1024 | tf_op jit(solution)/shard_map/pallas_call | solution.py:378
  93.4 2.6 %collective-permute-done.3.refs_1_ = bf16[256,512]{1,0:T(8,128)(2,1)S(1)} collective-permute-done((bf16[256,512]{1,0:T(8,128)(2,1)}, bf16[256,512]{1,0:T(8,128)(2,1)S(1)}, u32[]{:S(2)}, u32[]{:S(2)}) %collective-permute-start.3) | collective-permute-done | bytes 262176 | tf_op jit(solution)/shard_map/ppermute | solution.py:453
  105.3 4.8 %shard_map.143 = (bf16[256,1536]{1,0:T(8,128)(2,1)}, bf16[256,1536]{1,0:T(8,128)(2,1)}) custom-call(s32[1]{0:T(128)} %bitcast.1.refs_0_, bf16[256,768]{1,0:T(8,128)(2,1)} %get-tuple-element.54.refs_3_.refs_4_.refs_1_, bf16[768,3072]{1,0:T(8,128)(2,1)} %bitcast.49, bf16[256,512]{1,0:T(8,128)(2,1)} %copy-done.17), custom_call_target="tpu_custom_call" | custom-call | flops 1207959552 | bytes 6684676 | tf_op jit(solution)/shard_map/pallas_call | solution.py:54
  110.1 5.7 %shard_map.144 = (bf16[256,1536]{1,0:T(8,128)(2,1)}, bf16[256,1664]{1,0:T(8,128)(2,1)}, f32[256,128]{1,0:T(8,128)}) custom-call(s32[1]{0:T(128)} %bitcast.1.refs_0_, bf16[256,768]{1,0:T(8,128)(2,1)} %get-tuple-element.63.refs_2_.refs_1_, bf16[3072,768]{1,0:T(8,128)(2,1)} %bitcast.51, bf16[256,1536]{1,0:T(8,128)(2,1)} %bitcast.39, ...), custom_call_target="tpu_custom_call" | custom-call | flops 1207959552 | bytes 8454148 | tf_op jit(solution)/shard_map/pallas_call | solution.py:54
  115.9 7.6 %collective-permute-done.9.refs_2_ = bf16[256,512]{1,0:T(8,128)(2,1)S(1)} collective-permute-done((bf16[256,512]{1,0:T(8,128)(2,1)S(1)}, bf16[256,512]{1,0:T(8,128)(2,1)S(1)}, u32[]{:S(2)}, u32[]{:S(2)}) %collective-permute-start.9) | collective-permute-done | bytes 262176 | tf_op jit(solution)/shard_map/ppermute | solution.py:526
  123.5 27.5 %collective-permute-done.10.refs_3_ = bf16[256,512]{1,0:T(8,128)(2,1)S(1)} collective-permute-done((bf16[256,512]{1,0:T(8,128)(2,1)S(1)}, bf16[256,512]{1,0:T(8,128)(2,1)S(1)}, u32[]{:S(2)}, u32[]{:S(2)}) %collective-permute-start.10) | collective-permute-done | bytes 262176 | tf_op jit(solution)/shard_map/ppermute | solution.py:526
  152.2 3.7 %shard_map.146 = (bf16[4,384,512]{2,1,0:T(8,128)(2,1)S(1)}, bf16[2,384,512]{2,1,0:T(8,128)(2,1)}, bf16[2,384,512]{2,1,0:T(8,128)(2,1)S(1)}, bf16[256,1664]{1,0:T(8,128)(2,1)}, bf16[256,1536]{1,0:T(8,128)(2,1)}) custom-call(s32[5]{0:T(128)S(1)} %stack.65.refs_0_, bf16[256,3072]{1,0:T(8,128)(2,1)S(1)} %copy-done.13, ...), custom_call_target="tpu_custom_call", output_to_operand_aliasing={{3}: (3, {}), {4}: (4, {})} | custom-call | bytes 1024 | tf_op jit(solution)/shard_map/pallas_call | solution.py:378
  159.2 4.8 %shard_map.148 = (bf16[256,1536]{1,0:T(8,128)(2,1)}, bf16[256,1664]{1,0:T(8,128)(2,1)}, f32[256,128]{1,0:T(8,128)}) custom-call(s32[1]{0:T(128)} %bitcast.1.refs_0_, bf16[256,512]{1,0:T(8,128)(2,1)} %copy-done.11, bf16[3072,512]{1,0:T(8,128)(2,1)} %bitcast.37, bf16[256,1536]{1,0:T(8,128)(2,1)} %copy-done.4, bf16[256,1536]{1,0:T(8,128)(2,1)} %copy-done.6, ...), custom_call_target="tpu_custom_call" | custom-call | flops 805306368 | bytes 6750212 | tf_op jit(solution)/shard_map/pallas_call | solution.py:54
  164.1 12.5 %collective-permute-done.12.refs_3_ = bf16[256,1536]{1,0:T(8,128)(2,1)} collective-permute-done((bf16[256,1536]{1,0:T(8,128)(2,1)}, bf16[256,1536]{1,0:T(8,128)(2,1)}, u32[]{:S(2)}, u32[]{:S(2)}) %collective-permute-start.12) | collective-permute-done | bytes 786464 | tf_op jit(solution)/shard_map/ppermute | solution.py:36
  178.6 2.3 shard_map.149
  182.4 2.8 %collective-permute-start.14 = (bf16[256,1536]{1,0:T(8,128)(2,1)}, bf16[256,1536]{1,0:T(8,128)(2,1)}, u32[]{:S(2)}, u32[]{:S(2)}) collective-permute-start(bf16[256,1536]{1,0:T(8,128)(2,1)} %get-tuple-element.82.refs_1_), channel_id=1, source_target_pairs={{0,2},{2,0},{1,3},{3,1},{4,6},{6,4},{5,7},{7,5},{8,10},{10,8},{9,1... | collective-permute-start | bytes 2359304 | tf_op jit(solution)/shard_map/ppermute | solution.py:36
  185.2 2.3 shard_map.150.refs_6_
  187.5 7.2 %collective-permute-done.18.refs_5_ = bf16[256,1664]{1,0:T(8,128)(2,1)} collective-permute-done((bf16[256,1664]{1,0:T(8,128)(2,1)}, bf16[256,1664]{1,0:T(8,128)(2,1)}, u32[]{:S(2)}, u32[]{:S(2)}) %collective-permute-start.18) | collective-permute-done | bytes 852000 | tf_op jit(solution)/shard_map/ppermute | solution.py:36
  194.8 3.4 %shard_map.151.refs_4_ = bf16[256,1536]{1,0:T(8,128)(2,1)} custom-call(bf16[256,1536]{1,0:T(8,128)(2,1)} %bitcast.44, bf16[256,1536]{1,0:T(8,128)(2,1)} %bitcast.40, f32[256,128]{1,0:T(8,128)} %get-tuple-element.87.refs_2_, f32[256,128]{1,0:T(8,128)} %get-tuple-element.74.refs_5_.refs_3_, bf16[256,1536]{1,0:T(8,128)(2,1)} %get-tuple-element.88.refs_4_, ...), custom_call_target="tpu_custom_call" | custom-call | bytes 4259840 | tf_op jit(solution)/shard_map/pallas_call | solution.py:54
  198.2 12.5 %collective-permute-done.17.refs_3_ = bf16[2,384,512]{2,1,0:T(8,128)(2,1)} collective-permute-done((bf16[2,384,512]{2,1,0:T(8,128)(2,1)S(1)}, bf16[2,384,512]{2,1,0:T(8,128)(2,1)}, u32[]{:S(2)}, u32[]{:S(2)}) %collective-permute-start.17) | collective-permute-done | bytes 786464 | tf_op jit(solution)/shard_map/ppermute | solution.py:545
  211.9 2.4 shard_map.152
  215.0 6.7 %collective-permute-start.20 = (bf16[192,512]{1,0:T(8,128)(2,1)S(1)}, bf16[192,512]{1,0:T(8,128)(2,1)S(1)}, u32[]{:S(2)}, u32[]{:S(2)}) collective-permute-start(bf16[192,512]{1,0:T(8,128)(2,1)S(1)} %get-tuple-element.93), channel_id=1, source_target_pairs={{0,18},{2,16},{4,22},{6,20},{8,26},{10,24},{12,30},{14,28},{16,2},... | collective-permute-start | bytes 589832 | tf_op jit(solution)/shard_map/ppermute | solution.py:577
  222.6 3.1 %shard_map.153.refs_1_ = bf16[256,1536]{1,0:T(8,128)(2,1)} custom-call(bf16[256,1536]{1,0:T(8,128)(2,1)} %copy-done.4, f32[256,128]{1,0:T(8,128)} %copy-done.23, f32[256,128]{1,0:T(8,128)} %get-tuple-element.80.refs_4_.refs_2_, bf16[256,1536]{1,0:T(8,128)(2,1)} %get-tuple-element.84.refs_3_, bf16[256,1664]{1,0:T(8,128)(2,1)} %copy-done.25, ...), custom_call_target="tpu_custom_call" | custom-call | bytes 3473408 | tf_op jit(solution)/shard_map/pallas_call | solution.py:54
  229.9 4.7 %collective-permute-done.20.refs_3_ = bf16[192,512]{1,0:T(8,128)(2,1)S(1)} collective-permute-done((bf16[192,512]{1,0:T(8,128)(2,1)S(1)}, bf16[192,512]{1,0:T(8,128)(2,1)S(1)}, u32[]{:S(2)}, u32[]{:S(2)}) %collective-permute-start.20) | collective-permute-done | bytes 196640 | tf_op jit(solution)/shard_map/ppermute | solution.py:577
  235.4 2.4 shard_map.156
  (119 shorter events, 40.1 us)
Async XLA Ops:
  7.2 57.0 %all-gather.3.cloned.1.call-start = ((), (), s32[]{:S(2)}) async-start(), calls=%async_computation.2 | async-start | bytes 2359296 | tf_op jit(solution)/shard_map/all_gather | solution.py:691
  8.7 21.0 %copy-start.4 = (bf16[256,1536]{1,0:T(8,128)(2,1)}, bf16[256,1536]{1,0:T(8,128)(2,1)S(1)}, u32[]{:S(2)}) copy-start(bf16[256,1536]{1,0:T(8,128)(2,1)S(1)} %bitcast_select_fusion.refs_1_.refs_3_.refs_0_) | copy-start | bytes 2359300
  8.7 21.0 %collective-permute-start.1 = (bf16[256,1536]{1,0:T(8,128)(2,1)S(1)}, bf16[256,1536]{1,0:T(8,128)(2,1)S(1)}, u32[]{:S(2)}, u32[]{:S(2)}) collective-permute-start(bf16[256,1536]{1,0:T(8,128)(2,1)S(1)} %bitcast_select_fusion.refs_1_.refs_3_.refs_0_), channel_id=1, source_target_pairs={{0,1},{1,0},{2,3},{3,2},{4,5},{5,4},{6,7},{7,6},{8,9},{9,8},{10,11... | collective-permute-start | bytes 2359304 | tf_op jit(solution)/shard_map/ppermute | solution.py:36
  33.9 151.3 %reduce-scatter.3.cloned.1.call-start = ((), (), s32[]{:S(2)}) async-start(), calls=%async_computation.3 | async-start | bytes 5308416 | tf_op jit(solution)/shard_map/reduce_scatter | solution.py:496
  34.0 20.7 %collective-permute-start = (bf16[256,1536]{1,0:T(8,128)(2,1)S(1)}, bf16[256,1536]{1,0:T(8,128)(2,1)}, u32[]{:S(2)}, u32[]{:S(2)}) collective-permute-start(bf16[256,1536]{1,0:T(8,128)(2,1)S(1)} %bitcast.41), channel_id=1, source_target_pairs={{0,1},{1,0},{2,3},{3,2},{4,5},{5,4},{6,7},{7,6},{8,9},{9,8},{10,11... | collective-permute-start | bytes 2359304 | tf_op jit(solution)/shard_map/ppermute | solution.py:36
  35.3 33.8 %collective-permute-start.2 = (bf16[256,1536]{1,0:T(8,128)(2,1)S(1)}, bf16[256,1536]{1,0:T(8,128)(2,1)S(1)}, u32[]{:S(2)}, u32[]{:S(2)}) collective-permute-start(bf16[256,1536]{1,0:T(8,128)(2,1)S(1)} %bitcast.45), channel_id=1, source_target_pairs={{0,1},{1,0},{2,3},{3,2},{4,5},{5,4},{6,7},{7,6},{8,9},{9,8},{10,11... | collective-permute-start | bytes 2359304 | tf_op jit(solution)/shard_map/ppermute | solution.py:36
  74.9 152.9 %reduce-scatter.5.cloned.1.call-start = ((), (), s32[]{:S(2)}) async-start(), calls=%async_computation.4 | async-start | bytes 2949120 | tf_op jit(solution)/shard_map/reduce_scatter | solution.py:761
  80.2 6.1 %copy-start.14 = (bf16[256,3072]{1,0:T(8,128)(2,1)S(1)}, bf16[256,3072]{1,0:T(8,128)(2,1)}, u32[]{:S(2)}) copy-start(bf16[256,3072]{1,0:T(8,128)(2,1)} %get-tuple-element.62.refs_1_) | copy-start | bytes 4718596
  87.3 11.1 %copy-start.19 = (bf16[4,256,512]{2,1,0:T(8,128)(2,1)S(1)}, bf16[4,256,512]{2,1,0:T(8,128)(2,1)}, u32[]{:S(2)}) copy-start(bf16[4,256,512]{2,1,0:T(8,128)(2,1)} %get-tuple-element.57.refs_0_) | copy-start | bytes 3145732
  90.8 7.7 %collective-permute-start.7 = (bf16[2,384,768]{2,1,0:T(8,128)(2,1)S(1)}, bf16[2,384,768]{2,1,0:T(8,128)(2,1)S(1)}, u32[]{:S(2)}, u32[]{:S(2)}) collective-permute-start(bf16[2,384,768]{2,1,0:T(8,128)(2,1)S(1)} %get-tuple-element.65), channel_id=1, source_target_pairs={{0,4},{4,0},{8,12},{12,8},{16,20},{20,16},{24,28},{28,24},{1,5},{5... | collective-permute-start | bytes 3538952 | tf_op jit(solution)/shard_map/ppermute | solution.py:453
  92.4 6.1 %collective-permute-start.8 = (bf16[2,384,768]{2,1,0:T(8,128)(2,1)S(1)}, bf16[2,384,768]{2,1,0:T(8,128)(2,1)S(1)}, u32[]{:S(2)}, u32[]{:S(2)}) collective-permute-start(bf16[2,384,768]{2,1,0:T(8,128)(2,1)S(1)} %get-tuple-element.66), channel_id=1, source_target_pairs={{0,4},{4,0},{8,12},{12,8},{16,20},{20,16},{24,28},{28,24},{1,5},{5... | collective-permute-start | bytes 3538952 | tf_op jit(solution)/shard_map/ppermute | solution.py:453
  92.4 3.6 %collective-permute-start.3 = (bf16[256,512]{1,0:T(8,128)(2,1)}, bf16[256,512]{1,0:T(8,128)(2,1)S(1)}, u32[]{:S(2)}, u32[]{:S(2)}) collective-permute-start(bf16[256,512]{1,0:T(8,128)(2,1)} %get-tuple-element.58), channel_id=1, source_target_pairs={{0,4},{4,0},{8,12},{12,8},{16,20},{20,16},{24,28},{28,24},{1,5},{5... | collective-permute-start | bytes 786440 | tf_op jit(solution)/shard_map/ppermute | solution.py:453
  92.9 3.9 %collective-permute-start.4 = (bf16[256,512]{1,0:T(8,128)(2,1)}, bf16[256,512]{1,0:T(8,128)(2,1)S(1)}, u32[]{:S(2)}, u32[]{:S(2)}) collective-permute-start(bf16[256,512]{1,0:T(8,128)(2,1)} %get-tuple-element.59), channel_id=1, source_target_pairs={{0,4},{4,0},{8,12},{12,8},{16,20},{20,16},{24,28},{28,24},{1,5},{5... | collective-permute-start | bytes 786440 | tf_op jit(solution)/shard_map/ppermute | solution.py:453
  93.0 4.6 %collective-permute-start.5 = (bf16[256,512]{1,0:T(8,128)(2,1)}, bf16[256,512]{1,0:T(8,128)(2,1)S(1)}, u32[]{:S(2)}, u32[]{:S(2)}) collective-permute-start(bf16[256,512]{1,0:T(8,128)(2,1)} %get-tuple-element.60), channel_id=1, source_target_pairs={{0,4},{4,0},{8,12},{12,8},{16,20},{20,16},{24,28},{28,24},{1,5},{5... | collective-permute-start | bytes 786440 | tf_op jit(solution)/shard_map/ppermute | solution.py:453
  96.0 2.4 collective-permute-start.6
  101.3 22.2 %collective-permute-start.9 = (bf16[256,512]{1,0:T(8,128)(2,1)S(1)}, bf16[256,512]{1,0:T(8,128)(2,1)S(1)}, u32[]{:S(2)}, u32[]{:S(2)}) collective-permute-start(bf16[256,512]{1,0:T(8,128)(2,1)S(1)} %get-tuple-element.71), channel_id=1, source_target_pairs={{8,0},{12,4},{16,8},{20,12},{24,16},{28,20},{9,1},{13,5},{17,9},{2... | collective-permute-start | bytes 786440 | tf_op jit(solution)/shard_map/ppermute | solution.py:526
  102.6 48.3 %collective-permute-start.10 = (bf16[256,512]{1,0:T(8,128)(2,1)S(1)}, bf16[256,512]{1,0:T(8,128)(2,1)S(1)}, u32[]{:S(2)}, u32[]{:S(2)}) collective-permute-start(bf16[256,512]{1,0:T(8,128)(2,1)S(1)} %get-tuple-element.72), channel_id=1, source_target_pairs={{16,0},{20,4},{24,8},{28,12},{17,1},{21,5},{25,9},{29,13},{18,2},{... | collective-permute-start | bytes 786440 | tf_op jit(solution)/shard_map/ppermute | solution.py:526
  103.9 47.0 %collective-permute-start.11 = (bf16[256,512]{1,0:T(8,128)(2,1)S(1)}, bf16[256,512]{1,0:T(8,128)(2,1)S(1)}, u32[]{:S(2)}, u32[]{:S(2)}) collective-permute-start(bf16[256,512]{1,0:T(8,128)(2,1)S(1)} %get-tuple-element.73), channel_id=1, source_target_pairs={{24,0},{28,4},{25,1},{29,5},{26,2},{30,6},{27,3},{31,7}} | collective-permute-start | bytes 786440 | tf_op jit(solution)/shard_map/ppermute | solution.py:526
  110.1 40.8 %copy-start.18 = (bf16[256,512]{1,0:T(8,128)(2,1)S(1)}, bf16[256,512]{1,0:T(8,128)(2,1)}, u32[]{:S(2)}) copy-start(bf16[256,512]{1,0:T(8,128)(2,1)} %copy-done.17) | copy-start | bytes 786436
  115.9 36.3 %copy-start.13 = (bf16[256,3072]{1,0:T(8,128)(2,1)S(1)}, bf16[256,3072]{1,0:T(8,128)(2,1)}, u32[]{:S(2)}) copy-start(bf16[256,3072]{1,0:T(8,128)(2,1)} %copy-done.12) | copy-start | bytes 4718596
  152.2 6.2 %copy-start.11 = (bf16[256,512]{1,0:T(8,128)(2,1)}, bf16[256,512]{1,0:T(8,128)(2,1)S(1)}, u32[]{:S(2)}) copy-start(bf16[256,512]{1,0:T(8,128)(2,1)S(1)} %shard_map.145.refs_2_.refs_1_) | copy-start | bytes 786436
  155.9 2.3 collective-permute-start.13
  155.9 20.7 %collective-permute-start.12 = (bf16[256,1536]{1,0:T(8,128)(2,1)}, bf16[256,1536]{1,0:T(8,128)(2,1)}, u32[]{:S(2)}, u32[]{:S(2)}) collective-permute-start(bf16[256,1536]{1,0:T(8,128)(2,1)} %get-tuple-element.77), channel_id=1, source_target_pairs={{0,1},{1,0},{2,3},{3,2},{4,5},{5,4},{6,7},{7,6},{8,9},{9,8},{10,11... | collective-permute-start | bytes 2359304 | tf_op jit(solution)/shard_map/ppermute | solution.py:36
  157.4 37.4 %collective-permute-start.18 = (bf16[256,1664]{1,0:T(8,128)(2,1)}, bf16[256,1664]{1,0:T(8,128)(2,1)}, u32[]{:S(2)}, u32[]{:S(2)}) collective-permute-start(bf16[256,1664]{1,0:T(8,128)(2,1)} %get-tuple-element.89), channel_id=1, source_target_pairs={{0,1},{1,0},{2,3},{3,2},{4,5},{5,4},{6,7},{7,6},{8,9},{9,8},{10,11... | collective-permute-start | bytes 2555912 | tf_op jit(solution)/shard_map/ppermute | solution.py:36
  157.9 40.3 %collective-permute-start.16 = (bf16[2,384,512]{2,1,0:T(8,128)(2,1)}, bf16[2,384,512]{2,1,0:T(8,128)(2,1)}, u32[]{:S(2)}, u32[]{:S(2)}) collective-permute-start(bf16[2,384,512]{2,1,0:T(8,128)(2,1)} %get-tuple-element.86), channel_id=1, source_target_pairs={{0,4},{4,0},{8,12},{12,8},{16,20},{20,16},{24,28},{28,24},{1,5},{5... | collective-permute-start | bytes 2359304 | tf_op jit(solution)/shard_map/ppermute | solution.py:453
  158.4 18.2 %copy-start.3 = (bf16[1,256,1536]{2,1,0:T(8,128)(2,1)S(1)}, bf16[1,256,1536]{2,1,0:T(8,128)(2,1)}, u32[]{:S(2)}) copy-start(bf16[1,256,1536]{2,1,0:T(8,128)(2,1)} %param.8) | copy-start | bytes 2359300
  158.4 52.4 %collective-permute-start.17 = (bf16[2,384,512]{2,1,0:T(8,128)(2,1)S(1)}, bf16[2,384,512]{2,1,0:T(8,128)(2,1)}, u32[]{:S(2)}, u32[]{:S(2)}) collective-permute-start(bf16[2,384,512]{2,1,0:T(8,128)(2,1)S(1)} %shard_map.147.refs_5_), channel_id=1, source_target_pairs={{0,8},{4,12},{8,0},{12,4},{16,24},{20,28},{24,16},{28,20},{1,9},{5... | collective-permute-start | bytes 2359304 | tf_op jit(solution)/shard_map/ppermute | solution.py:545
  180.9 40.9 %collective-permute-start.15 = (bf16[256,1664]{1,0:T(8,128)(2,1)}, bf16[256,1664]{1,0:T(8,128)(2,1)S(1)}, u32[]{:S(2)}, u32[]{:S(2)}) collective-permute-start(bf16[256,1664]{1,0:T(8,128)(2,1)} %get-tuple-element.85), channel_id=1, source_target_pairs={{0,1},{1,0},{2,3},{3,2},{4,5},{5,4},{6,7},{7,6},{8,9},{9,8},{10,11... | collective-permute-start | bytes 2555912 | tf_op jit(solution)/shard_map/ppermute | solution.py:36
  182.4 43.3 %collective-permute-start.14 = (bf16[256,1536]{1,0:T(8,128)(2,1)}, bf16[256,1536]{1,0:T(8,128)(2,1)}, u32[]{:S(2)}, u32[]{:S(2)}) collective-permute-start(bf16[256,1536]{1,0:T(8,128)(2,1)} %get-tuple-element.82.refs_1_), channel_id=1, source_target_pairs={{0,2},{2,0},{1,3},{3,1},{4,6},{6,4},{5,7},{7,5},{8,10},{10,8},{9,1... | collective-permute-start | bytes 2359304 | tf_op jit(solution)/shard_map/ppermute | solution.py:36
  215.0 14.9 %collective-permute-start.19 = (bf16[192,512]{1,0:T(8,128)(2,1)S(1)}, bf16[192,512]{1,0:T(8,128)(2,1)S(1)}, u32[]{:S(2)}, u32[]{:S(2)}) collective-permute-start(bf16[192,512]{1,0:T(8,128)(2,1)S(1)} %get-tuple-element.92), channel_id=1, source_target_pairs={{0,16},{2,18},{4,20},{6,22},{8,24},{10,26},{12,28},{14,30},{16,0},... | collective-permute-start | bytes 589832 | tf_op jit(solution)/shard_map/ppermute | solution.py:577
  215.0 19.6 %collective-permute-start.20 = (bf16[192,512]{1,0:T(8,128)(2,1)S(1)}, bf16[192,512]{1,0:T(8,128)(2,1)S(1)}, u32[]{:S(2)}, u32[]{:S(2)}) collective-permute-start(bf16[192,512]{1,0:T(8,128)(2,1)S(1)} %get-tuple-element.93), channel_id=1, source_target_pairs={{0,18},{2,16},{4,22},{6,20},{8,26},{10,24},{12,30},{14,28},{16,2},... | collective-permute-start | bytes 589832 | tf_op jit(solution)/shard_map/ppermute | solution.py:577
  221.7 12.9 %collective-permute-start.21 = (bf16[192,512]{1,0:T(8,128)(2,1)S(1)}, bf16[192,512]{1,0:T(8,128)(2,1)S(1)}, u32[]{:S(2)}, u32[]{:S(2)}) collective-permute-start(bf16[192,512]{1,0:T(8,128)(2,1)S(1)} %get-tuple-element.94), channel_id=1, source_target_pairs={{0,2},{2,0},{1,3},{3,1},{4,6},{6,4},{5,7},{7,5},{8,10},{10,8},{9,1... | collective-permute-start | bytes 589832 | tf_op jit(solution)/shard_map/ppermute | solution.py:36
  (24 other events, 50.4 us)
Sparse Core Ops, SparseCore 0:
  34.0 30.0 all-gather.2
  75.0 74.9 reduce-scatter.2
  152.3 66.4 reduce-scatter.4

commit v5 on v4

--- a/solution.py
+++ b/solution.py
@@ -457,43 +457,104 @@
     out_ref[...] = dot(left_ref[...], right_ref[...], TN).astype(BF16)
 
 
-def pieces_body(count, at_ref, *refs):
-    pieces, (right_ref, out_ref) = refs[:count], refs[count:]
-    for step, piece in enumerate(pieces):
-
-        @pl.when(pl.program_id(0) == step)
+def pieces_body(count, parts, at_ref, *refs):
+    pieces, (right_ref, keep_ref, low_ref, high_ref, both_ref) = refs[:count], refs[count:]
+    step = pl.program_id(0)
+    for which, piece in enumerate(pieces):
+
+        @pl.when(step // parts == which)
         def multiply(piece=piece):
-            out_ref[...] = dot(piece[...], right_ref[...], TN).astype(BF16)
-
-
-def scattered(pieces, right, after=()):
+            both_ref[...] = dot(piece[...], right_ref[...], TN).astype(BF16)
+
+    half = both_ref.shape[0] // 2
+    tall = low_ref.shape[0]
+    place = at_ref[1 + step]
+    for core in range(2):
+        mine = slice(core * half, (core + 1) * half)
+        other = slice((1 - core) * half, (2 - core) * half)
+
+        @pl.when(at_ref[0] == core)
+        def kept(mine=mine):
+            keep_ref[0] = both_ref[mine]
+
+        @pl.when((at_ref[0] == core) & (place < tall))
+        def low_sent(other=other):
+            low_ref[place % tall] = both_ref[other]
+
+        @pl.when((at_ref[0] == core) & (place >= tall))
+        def high_sent(other=other):
+            high_ref[place % tall] = both_ref[other]
+
+
+def core_sum_body(at_ref, keep_ref, low_ref, high_ref, out_ref):
+    half = low_ref.shape[0]
+    for index in range(2 * half):
+        other = low_ref[index] if index < half else high_ref[index - half]
+        out_ref[index] = (keep_ref[index].astype(F32) + other.astype(F32)).astype(BF16)
+
+
+def piece_products(pieces, right):
     rows, width = pieces[0].shape
     count = len(pieces)
-    block = width // 2 if count == 1 else width
-    parts = width // block
+    chips = lax.axis_size("seq") // 2
     cols = right.shape[1]
+    step = width * count // chips
+    parts = width // step
+    core = lax.axis_index("seq").astype(jnp.int32) % 2
     tp_id = lax.axis_index("tp").astype(jnp.int32)
-    places = jnp.stack([lax.rem(tp_id + count - step, count) if count > 1 else tp_id * 0 for step in range(count)])
+    places = [
+        lax.rem(tp_id + count - which, count) * parts + part
+        for which in range(count)
+        for part in range(parts)
+    ]
+    share = (step // 2, cols)
+    group = (chips // 2, *share)
 
     def picked(which):
-        def index(step, part, at):
-            held = jnp.where(step < which, 0, parts - 1)
-            return 0, jnp.where(step == which, part, held)
-
-        return pl.BlockSpec((rows, block), index)
-
-    (partial,) = ordered(
-        functools.partial(pieces_body, count),
+        def index(i, at):
+            held = jnp.where(i // parts < which, 0, parts - 1)
+            return 0, jnp.where(i // parts == which, i % parts, held)
+
+        return pl.BlockSpec((rows, step), index)
+
+    return ordered(
+        functools.partial(pieces_body, count, parts),
         [*pieces, right],
+        (),
+        [struct((chips, *share), BF16), struct(group, BF16), struct(group, BF16)],
+        (chips,),
+        [picked(which) for which in range(count)]
+        + [pl.BlockSpec(right.shape, lambda i, at: (0, 0))],
+        [pl.BlockSpec((1, *share), lambda i, at: (at[1 + i], 0, 0))]
+        + [pl.BlockSpec(group, lambda i, at: (0, 0, 0))] * 2,
+        jnp.stack([core] + places).astype(jnp.int32),
+        scratch=[pltpu.VMEM((step, cols), BF16)],
+    )
+
+
+def core_sum(keep, low, high, after):
+    full = pl.BlockSpec(keep.shape, lambda i, at: (0, 0, 0))
+    half = pl.BlockSpec(low.shape, lambda i, at: (0, 0, 0))
+    (total,) = ordered(
+        core_sum_body,
+        [keep, core_swap(low), core_swap(high)],
         after,
-        [struct((width * count, cols), BF16)],
-        (count, parts),
-        [picked(which) for which in range(count)]
-        + [pl.BlockSpec(right.shape, lambda step, part, at: (0, 0))],
-        [pl.BlockSpec((block, cols), lambda step, part, at: (at[step] * parts + part, 0))],
-        places,
-    )
-    return lax.psum_scatter(partial, "seq", scatter_dimension=0, tiled=True), partial
+        [struct(keep.shape, BF16)],
+        (1,),
+        [full, half, half],
+        [full],
+        jnp.zeros((1,), jnp.int32),
+    )
+    return total
+
+
+def over_chips(total):
+    chips = total.shape[0]
+    groups = [[2 * one + core for one in range(chips)] for core in range(2)]
+    flat = total.reshape(-1, total.shape[2])
+    return lax.psum_scatter(
+        flat, "seq", scatter_dimension=0, tiled=True, axis_index_groups=groups
+    )
 
 
 def chip_sum_body(count, keep_ref, *refs):
@@ -727,20 +788,22 @@
         4 * rows * length * query_cols,
         [pltpu.VMEM((heads, rows, HEAD_DIM), F32)] * 2,
     )
-    out_share, mark = scattered(grad_pieces, attn_flat)
+    out_keep, out_low, out_high = piece_products(grad_pieces, attn_flat)
     (grad_attn,) = call(
         functools.partial(grad_attn_body, tp_count),
         [struct((heads, rows, HEAD_DIM), BF16)],
         [me, *grad_pieces, out_weight],
         1,
         2 * rows * model * query_cols,
-        after=[mark],
+        after=[out_keep],
         grid=(heads // together,),
         in_specs=[SMEM]
         + [whole] * tp_count
         + [pl.BlockSpec((together * HEAD_DIM, model), lambda i: (i, 0))],
         out_specs=[per_head],
     )
+    out_total = core_sum(out_keep, out_low, out_high, [grad_attn])
+    out_share = over_chips(out_total)
     halves = [struct((chips, rows, 2 * kv_cols), BF16)] + [
         struct((rows, 2 * kv_cols), BF16)
     ] * chips
@@ -751,7 +814,7 @@
         1,
         10 * rows * length * query_cols,
         [pltpu.VMEM((heads, rows, HEAD_DIM), F32)] * 2,
-        after=[mark],
+        after=[out_total],
     )
     kv_came = [core_swap(piece) for piece in send]
     query_keep, query_low, query_high, _ = over_tokens(normed, grad_queries, natural=True)

time: 245 us -> 253 us (1.033)
  waiting for transfers between devices: 99.8 us -> 106 us
  Pallas kernels: 71.3 us -> 75.9 us
  starting transfers between devices: 25.2 us -> 22.2 us
    pallas_call x6 -> x7, Pallas kernels: 14.3 us -> 19 us  [ordered(): pl.pallas_call(with_order, out_shape=outs + [struct(value.shape, value.dt...]
    ppermute x2, waiting for transfers between devices: 4.67 us -> 8.14 us  [finish(): parts.append(lax.ppermute(outs[sections + step], ('seq', 'section'), pairs))]
    ppermute x2, starting transfers between devices: 6.68 us -> 3.84 us  [finish(): parts.append(lax.ppermute(outs[sections + step], ('seq', 'section'), pairs))]
    unnamed x67 -> x71, local copies, waits for them, and re-layouts: 16.1 us -> 16.9 us
  transfers between devices with their start and end apart: 25 -> 27, of which waited for: 14 -> 15; matrix products, arithmetic and copies ran while one was open for 2% -> 2% of each run, Pallas kernels for 26% -> 25%
where the time goes in v5:
time: 253 us
  waiting for transfers between devices  106 us (42%)
  Pallas kernels  75.9 us (30%)
  starting transfers between devices  22.2 us (9%)
  between operations  17.3 us (7%)
  local copies, waits for them, and re-layouts  17.2 us (7%)
  blocking collectives  9.17 us (4%)
  other arithmetic  5.11 us (2%)
    pallas_call x16, Pallas kernels, call(): pl.pallas_call(with_order, out_shape=out_shape, grid=grid, in_specs=list(...  56.9 us
    ppermute x8, waiting for transfers between devices, shifted(): return lax.ppermute(value, axis, pairs)  40.8 us
    ppermute x3, waiting for transfers between devices, sums_below(): terms.append(lax.ppermute(sums[steps], 'seq', pairs))  37 us
    pallas_call x7, Pallas kernels, ordered(): pl.pallas_call(with_order, out_shape=outs + [struct(value.shape, value.dt...  19 us
    unnamed x71, local copies, waits for them, and re-layouts  16.9 us
    ppermute x1, waiting for transfers between devices, step(): self.terms.append(lax.ppermute(sent, 'seq', pairs))  12.6 us
    ppermute x8, starting transfers between devices, shifted(): return lax.ppermute(value, axis, pairs)  10.6 us
    all_gather x1, blocking collectives, on_device(): all_docs = lax.all_gather(block_docs[0], 'seq', axis=0, tiled=True)  9.17 us
  transfers between devices with their start and end apart: 27, of which 15 were waited for; matrix products, arithmetic and copies ran while one was open for 2% of the time, Pallas kernels for 25%

profile of v5, /device:TPU:0, one launch (start us, length us, event | category | flops | bytes accessed | tf_op | source)
XLA Modules:
  0.0 253.3 jit_solution(13716272144630152301)
XLA Ops:
  8.7 3.0 %collective-permute-start.1 = (bf16[256,1536]{1,0:T(8,128)(2,1)S(1)}, bf16[256,1536]{1,0:T(8,128)(2,1)S(1)}, u32[]{:S(2)}, u32[]{:S(2)}) collective-permute-start(bf16[256,1536]{1,0:T(8,128)(2,1)S(1)} %bitcast_select_fusion.refs_1_.refs_3_.refs_0_), channel_id=1, source_target_pairs={{0,1},{1,0},{2,3},{3,2},{4,5},{5,4},{6,7},{7,6},{8,9},{9,8},{10,11... | collective-permute-start | bytes 2359304 | tf_op jit(solution)/shard_map/ppermute | solution.py:36
  13.1 9.2 %all-reduce = s32[16]{0:T(128)S(1)} all-reduce(s32[16]{0:T(128)S(1)} %bitcast_dynamic-update-slice_fusion), channel_id=2, replica_groups=mesh['seq'=8,'section'=2,'tp'=2] {'seq'}, use_global_device_ids=true, to_apply=%add | all-reduce | flops 16 | bytes 128 | tf_op jit(solution)/shard_map/all_gather | solution.py:726
  26.7 2.2 broadcast_select_fusion
  29.8 2.3 shard_map.135
  36.1 18.5 %collective-permute-done.refs_2_.refs_4_ = bf16[256,1536]{1,0:T(8,128)(2,1)} collective-permute-done((bf16[256,1536]{1,0:T(8,128)(2,1)S(1)}, bf16[256,1536]{1,0:T(8,128)(2,1)}, u32[]{:S(2)}, u32[]{:S(2)}) %collective-permute-start) | collective-permute-done | bytes 786464 | tf_op jit(solution)/shard_map/ppermute | solution.py:36
  54.6 6.3 %shard_map.136 = (bf16[256,3072]{1,0:T(8,128)(2,1)}, f32[256,128]{1,0:T(8,128)}, bf16[6,256,128]{2,1,0:T(8,128)(2,1)}, f32[6,256,128]{2,1,0:T(8,128)}) custom-call(s32[1]{0:T(128)} %bitcast.1.refs_0_, bf16[256,1536]{1,0:T(8,128)(2,1)} %bitcast.41, bf16[256,1536]{1,0:T(8,128)(2,1)} %collective-permute-done.refs_2_.refs_4_, bf16[3072,768]{1,0:T(8,128)(2,1)} %bitcast.54, ...), custom_call_target="tpu_custom_call" | custom-call | flops 1207959552 | bytes 9175044 | tf_op jit(solution)/shard_map/pallas_call | solution.py:54
  60.8 3.3 %all-gather.3.cloned.1.call-done.refs_2_.refs_6_ = bf16[2048,512]{1,0:T(8,128)(2,1)} async-done(((bf16[256,512]{1,0:T(8,128)(2,1)}), bf16[2048,512]{1,0:T(8,128)(2,1)}) %all-gather.3.cloned.1.call-update) | async-done | bytes 2097168 | tf_op jit(solution)/shard_map/all_gather | solution.py:752
  64.1 3.9 %shard_map.137 = (bf16[256,768]{1,0:T(8,128)(2,1)}, f32[6,256,128]{2,1,0:T(8,128)}) custom-call(s32[19]{0:T(128)} %copy-done.27, bf16[6,256,128]{2,1,0:T(8,128)(2,1)} %get-tuple-element.56.refs_1_, bf16[2048,512]{1,0:T(8,128)(2,1)} %all-gather.3.cloned.1.call-done.refs_2_.refs_6_), custom_call_target="tpu_custom_call" | custom-call | flops 1610612736 | bytes 3670092 | tf_op jit(solution)/shard_map/pallas_call | solution.py:54
  70.3 4.9 %shard_map.138 = (bf16[4,384,768]{2,1,0:T(8,128)(2,1)S(1)}, bf16[2,384,768]{2,1,0:T(8,128)(2,1)}, bf16[2,384,768]{2,1,0:T(8,128)(2,1)}) custom-call(s32[5]{0:T(128)S(1)} %stack.68.refs_0_, bf16[256,1536]{1,0:T(8,128)(2,1)S(1)} %bitcast.50, bf16[256,1536]{1,0:T(8,128)(2,1)S(1)} %collective-permute-done.2.refs_2_, bf16[256,768]{1,0:T(8,128)(2,1)S(1)} %copy-done.18), custom_call_target="tpu_custom_call" | custom-call | bytes 1024 | tf_op jit(solution)/shard_map/pallas_call | solution.py:378
  77.1 5.4 %shard_map.139.refs_4_.refs_3_ = bf16[6,256,128]{2,1,0:T(8,128)(2,1)} custom-call(s32[1]{0:T(128)} %bitcast.1.refs_0_, bf16[256,1536]{1,0:T(8,128)(2,1)} %bitcast.47, bf16[256,1536]{1,0:T(8,128)(2,1)} %copy-done.8, bf16[768,3072]{1,0:T(8,128)(2,1)} %bitcast.52, bf16[4,384,768]{2,1,0:T(8,128)(2,1)} %copy-done.4), custom_call_target="tpu_custom_call" | custom-call | flops 1207959552 | bytes 6684676 | tf_op jit(solution)/shard_map/pallas_call | solution.py:54
  83.5 2.2 shard_map.140.refs_7_
  87.3 6.1 %shard_map.141 = (bf16[4,256,512]{2,1,0:T(8,128)(2,1)}, bf16[256,512]{1,0:T(8,128)(2,1)}, bf16[256,512]{1,0:T(8,128)(2,1)}, bf16[256,512]{1,0:T(8,128)(2,1)}, bf...) custom-call(s32[19]{0:T(128)} %copy-done.27, bf16[6,256,128]{2,1,0:T(8,128)(2,1)} %get-tuple-element.56.refs_1_, ...), custom_call_target="tpu_custom_call" | custom-call | flops 4026531840 | bytes 7340108 | tf_op jit(solution)/shard_map/pallas_call | solution.py:54
  94.4 3.4 %shard_map.142 = (bf16[4,384,768]{2,1,0:T(8,128)(2,1)S(1)}, bf16[2,384,768]{2,1,0:T(8,128)(2,1)S(1)}, bf16[2,384,768]{2,1,0:T(8,128)(2,1)S(1)}) custom-call(s32[5]{0:T(128)S(1)} %stack.69.refs_0_, bf16[256,3072]{1,0:T(8,128)(2,1)S(1)} %copy-done.17, bf16[256,768]{1,0:T(8,128)(2,1)S(1)} %copy-done.19), custom_call_target="tpu_custom_call" | custom-call | bytes 1024 | tf_op jit(solution)/shard_map/pallas_call | solution.py:378
  100.5 2.4 collective-permute-done.5.refs_1_
  112.1 4.8 %shard_map.144 = (bf16[256,1536]{1,0:T(8,128)(2,1)}, bf16[256,1536]{1,0:T(8,128)(2,1)}) custom-call(s32[1]{0:T(128)} %bitcast.1.refs_0_, bf16[256,768]{1,0:T(8,128)(2,1)} %get-tuple-element.57.refs_3_.refs_4_.refs_1_, bf16[768,3072]{1,0:T(8,128)(2,1)} %bitcast.53, bf16[256,512]{1,0:T(8,128)(2,1)} %copy-done.20), custom_call_target="tpu_custom_call" | custom-call | flops 1207959552 | bytes 6684676 | tf_op jit(solution)/shard_map/pallas_call | solution.py:54
  116.9 5.7 %shard_map.145 = (bf16[256,1536]{1,0:T(8,128)(2,1)}, bf16[256,1664]{1,0:T(8,128)(2,1)}, f32[256,128]{1,0:T(8,128)}) custom-call(s32[1]{0:T(128)} %bitcast.1.refs_0_, bf16[256,768]{1,0:T(8,128)(2,1)} %get-tuple-element.69.refs_2_.refs_1_, bf16[3072,768]{1,0:T(8,128)(2,1)} %bitcast.55, bf16[256,1536]{1,0:T(8,128)(2,1)} %bitcast.42, ...), custom_call_target="tpu_custom_call" | custom-call | flops 1207959552 | bytes 8454148 | tf_op jit(solution)/shard_map/pallas_call | solution.py:54
  122.6 11.4 %collective-permute-done.11.refs_2_ = bf16[256,512]{1,0:T(8,128)(2,1)S(1)} collective-permute-done((bf16[256,512]{1,0:T(8,128)(2,1)S(1)}, bf16[256,512]{1,0:T(8,128)(2,1)S(1)}, u32[]{:S(2)}, u32[]{:S(2)}) %collective-permute-start.11) | collective-permute-done | bytes 262176 | tf_op jit(solution)/shard_map/ppermute | solution.py:587
  134.0 25.6 %collective-permute-done.12.refs_3_ = bf16[256,512]{1,0:T(8,128)(2,1)S(1)} collective-permute-done((bf16[256,512]{1,0:T(8,128)(2,1)S(1)}, bf16[256,512]{1,0:T(8,128)(2,1)S(1)}, u32[]{:S(2)}, u32[]{:S(2)}) %collective-permute-start.12) | collective-permute-done | bytes 262176 | tf_op jit(solution)/shard_map/ppermute | solution.py:587
  160.9 3.7 %shard_map.147 = (bf16[4,384,512]{2,1,0:T(8,128)(2,1)S(1)}, bf16[2,384,512]{2,1,0:T(8,128)(2,1)}, bf16[2,384,512]{2,1,0:T(8,128)(2,1)S(1)}, bf16[256,1664]{1,0:T(8,128)(2,1)}, bf16[256,1536]{1,0:T(8,128)(2,1)}) custom-call(s32[5]{0:T(128)S(1)} %stack.74.refs_0_, bf16[256,3072]{1,0:T(8,128)(2,1)S(1)} %copy-done.16, ...), custom_call_target="tpu_custom_call", output_to_operand_aliasing={{3}: (3, {}), {4}: (4, {})} | custom-call | bytes 1024 | tf_op jit(solution)/shard_map/pallas_call | solution.py:378
  167.9 4.7 %shard_map.149 = (bf16[256,1536]{1,0:T(8,128)(2,1)}, bf16[256,1664]{1,0:T(8,128)(2,1)}, f32[256,128]{1,0:T(8,128)}) custom-call(s32[1]{0:T(128)} %bitcast.1.refs_0_, bf16[256,512]{1,0:T(8,128)(2,1)} %copy-done.13, bf16[3072,512]{1,0:T(8,128)(2,1)} %bitcast.40, bf16[256,1536]{1,0:T(8,128)(2,1)} %copy-done.3, bf16[256,1536]{1,0:T(8,128)(2,1)} %copy-done.9, ...), custom_call_target="tpu_custom_call" | custom-call | flops 805306368 | bytes 6750212 | tf_op jit(solution)/shard_map/pallas_call | solution.py:54
  172.6 12.7 %collective-permute-done.14.refs_3_ = bf16[256,1536]{1,0:T(8,128)(2,1)} collective-permute-done((bf16[256,1536]{1,0:T(8,128)(2,1)}, bf16[256,1536]{1,0:T(8,128)(2,1)}, u32[]{:S(2)}, u32[]{:S(2)}) %collective-permute-start.14) | collective-permute-done | bytes 786464 | tf_op jit(solution)/shard_map/ppermute | solution.py:36
  187.3 2.3 shard_map.150
  192.6 2.3 shard_map.151.refs_6_
  195.0 8.6 %collective-permute-done.20.refs_5_ = bf16[256,1664]{1,0:T(8,128)(2,1)} collective-permute-done((bf16[256,1664]{1,0:T(8,128)(2,1)}, bf16[256,1664]{1,0:T(8,128)(2,1)}, u32[]{:S(2)}, u32[]{:S(2)}) %collective-permute-start.20) | collective-permute-done | bytes 852000 | tf_op jit(solution)/shard_map/ppermute | solution.py:36
  203.5 3.4 %shard_map.152.refs_4_ = bf16[256,1536]{1,0:T(8,128)(2,1)} custom-call(bf16[256,1536]{1,0:T(8,128)(2,1)} %bitcast.48, bf16[256,1536]{1,0:T(8,128)(2,1)} %bitcast.43, f32[256,128]{1,0:T(8,128)} %get-tuple-element.93.refs_2_, f32[256,128]{1,0:T(8,128)} %get-tuple-element.80.refs_5_.refs_3_, bf16[256,1536]{1,0:T(8,128)(2,1)} %get-tuple-element.94.refs_4_, ...), custom_call_target="tpu_custom_call" | custom-call | bytes 4259840 | tf_op jit(solution)/shard_map/pallas_call | solution.py:54
  207.0 12.6 %collective-permute-done.19.refs_3_ = bf16[2,384,512]{2,1,0:T(8,128)(2,1)} collective-permute-done((bf16[2,384,512]{2,1,0:T(8,128)(2,1)S(1)}, bf16[2,384,512]{2,1,0:T(8,128)(2,1)}, u32[]{:S(2)}, u32[]{:S(2)}) %collective-permute-start.19) | collective-permute-done | bytes 786464 | tf_op jit(solution)/shard_map/ppermute | solution.py:606
  220.7 2.4 shard_map.153
  223.8 3.8 %collective-permute-start.22 = (bf16[192,512]{1,0:T(8,128)(2,1)S(1)}, bf16[192,512]{1,0:T(8,128)(2,1)S(1)}, u32[]{:S(2)}, u32[]{:S(2)}) collective-permute-start(bf16[192,512]{1,0:T(8,128)(2,1)S(1)} %get-tuple-element.99), channel_id=1, source_target_pairs={{0,18},{2,16},{4,22},{6,20},{8,26},{10,24},{12,30},{14,28},{16,2},... | collective-permute-start | bytes 589832 | tf_op jit(solution)/shard_map/ppermute | solution.py:638
  228.2 3.1 %shard_map.154.refs_1_ = bf16[256,1536]{1,0:T(8,128)(2,1)} custom-call(bf16[256,1536]{1,0:T(8,128)(2,1)} %copy-done.3, f32[256,128]{1,0:T(8,128)} %copy-done.26, f32[256,128]{1,0:T(8,128)} %get-tuple-element.86.refs_4_.refs_2_, bf16[256,1536]{1,0:T(8,128)(2,1)} %get-tuple-element.90.refs_3_, bf16[256,1664]{1,0:T(8,128)(2,1)} %collective-permute-done.17.refs_4_, ...), custom_call_target="tpu_custom_call" | custom-call | bytes 3473408 | tf_op jit(solution)/shard_map/pallas_call | solution.py:54
  235.5 3.1 %collective-permute-done.21.refs_2_ = bf16[192,512]{1,0:T(8,128)(2,1)S(1)} collective-permute-done((bf16[192,512]{1,0:T(8,128)(2,1)S(1)}, bf16[192,512]{1,0:T(8,128)(2,1)S(1)}, u32[]{:S(2)}, u32[]{:S(2)}) %collective-permute-start.21) | collective-permute-done | bytes 196640 | tf_op jit(solution)/shard_map/ppermute | solution.py:638
  238.6 5.0 %collective-permute-done.22.refs_3_ = bf16[192,512]{1,0:T(8,128)(2,1)S(1)} collective-permute-done((bf16[192,512]{1,0:T(8,128)(2,1)S(1)}, bf16[192,512]{1,0:T(8,128)(2,1)S(1)}, u32[]{:S(2)}, u32[]{:S(2)}) %collective-permute-start.22) | collective-permute-done | bytes 196640 | tf_op jit(solution)/shard_map/ppermute | solution.py:638
  244.4 2.4 shard_map.157
  (128 shorter events, 45.4 us)
Async XLA Ops:
  7.2 56.9 %all-gather.3.cloned.1.call-start = ((), (), s32[]{:S(2)}) async-start(), calls=%async_computation.2 | async-start | bytes 2359296 | tf_op jit(solution)/shard_map/all_gather | solution.py:752
  8.7 21.0 %copy-start.3 = (bf16[256,1536]{1,0:T(8,128)(2,1)}, bf16[256,1536]{1,0:T(8,128)(2,1)S(1)}, u32[]{:S(2)}) copy-start(bf16[256,1536]{1,0:T(8,128)(2,1)S(1)} %bitcast_select_fusion.refs_1_.refs_3_.refs_0_) | copy-start | bytes 2359300
  8.7 21.0 %collective-permute-start.1 = (bf16[256,1536]{1,0:T(8,128)(2,1)S(1)}, bf16[256,1536]{1,0:T(8,128)(2,1)S(1)}, u32[]{:S(2)}, u32[]{:S(2)}) collective-permute-start(bf16[256,1536]{1,0:T(8,128)(2,1)S(1)} %bitcast_select_fusion.refs_1_.refs_3_.refs_0_), channel_id=1, source_target_pairs={{0,1},{1,0},{2,3},{3,2},{4,5},{5,4},{6,7},{7,6},{8,9},{9,8},{10,11... | collective-permute-start | bytes 2359304 | tf_op jit(solution)/shard_map/ppermute | solution.py:36
  33.9 158.8 %reduce-scatter.3.cloned.1.call-start = ((), (), s32[]{:S(2)}) async-start(), calls=%async_computation.3 | async-start | bytes 2949120 | tf_op jit(solution)/shard_map/reduce_scatter | solution.py:555
  33.9 20.7 %collective-permute-start = (bf16[256,1536]{1,0:T(8,128)(2,1)S(1)}, bf16[256,1536]{1,0:T(8,128)(2,1)}, u32[]{:S(2)}, u32[]{:S(2)}) collective-permute-start(bf16[256,1536]{1,0:T(8,128)(2,1)S(1)} %bitcast.44), channel_id=1, source_target_pairs={{0,1},{1,0},{2,3},{3,2},{4,5},{5,4},{6,7},{7,6},{8,9},{9,8},{10,11... | collective-permute-start | bytes 2359304 | tf_op jit(solution)/shard_map/ppermute | solution.py:36
  35.2 33.8 %collective-permute-start.2 = (bf16[256,1536]{1,0:T(8,128)(2,1)S(1)}, bf16[256,1536]{1,0:T(8,128)(2,1)S(1)}, u32[]{:S(2)}, u32[]{:S(2)}) collective-permute-start(bf16[256,1536]{1,0:T(8,128)(2,1)S(1)} %bitcast.49), channel_id=1, source_target_pairs={{0,1},{1,0},{2,3},{3,2},{4,5},{5,4},{6,7},{7,6},{8,9},{9,8},{10,11... | collective-permute-start | bytes 2359304 | tf_op jit(solution)/shard_map/ppermute | solution.py:36
  76.6 5.9 %collective-permute-start.3 = (bf16[2,384,768]{2,1,0:T(8,128)(2,1)}, bf16[2,384,768]{2,1,0:T(8,128)(2,1)}, u32[]{:S(2)}, u32[]{:S(2)}) collective-permute-start(bf16[2,384,768]{2,1,0:T(8,128)(2,1)} %get-tuple-element.61), channel_id=1, source_target_pairs={{0,4},{4,0},{8,12},{12,8},{16,20},{20,16},{24,28},{28,24},{1,5},{5... | collective-permute-start | bytes 3538952 | tf_op jit(solution)/shard_map/ppermute | solution.py:453
  76.6 5.9 %collective-permute-start.4 = (bf16[2,384,768]{2,1,0:T(8,128)(2,1)}, bf16[2,384,768]{2,1,0:T(8,128)(2,1)}, u32[]{:S(2)}, u32[]{:S(2)}) collective-permute-start(bf16[2,384,768]{2,1,0:T(8,128)(2,1)} %get-tuple-element.62), channel_id=1, source_target_pairs={{0,4},{4,0},{8,12},{12,8},{16,20},{20,16},{24,28},{28,24},{1,5},{5... | collective-permute-start | bytes 3538952 | tf_op jit(solution)/shard_map/ppermute | solution.py:453
  87.2 146.2 %reduce-scatter.5.cloned.1.call-start = ((), (), s32[]{:S(2)}) async-start(), calls=%async_computation.4 | async-start | bytes 2949120 | tf_op jit(solution)/shard_map/reduce_scatter | solution.py:824
  94.4 10.8 %copy-start.22 = (bf16[4,256,512]{2,1,0:T(8,128)(2,1)S(1)}, bf16[4,256,512]{2,1,0:T(8,128)(2,1)}, u32[]{:S(2)}) copy-start(bf16[4,256,512]{2,1,0:T(8,128)(2,1)} %get-tuple-element.63.refs_0_) | copy-start | bytes 3145732
  97.9 7.4 %collective-permute-start.9 = (bf16[2,384,768]{2,1,0:T(8,128)(2,1)S(1)}, bf16[2,384,768]{2,1,0:T(8,128)(2,1)S(1)}, u32[]{:S(2)}, u32[]{:S(2)}) collective-permute-start(bf16[2,384,768]{2,1,0:T(8,128)(2,1)S(1)} %get-tuple-element.71), channel_id=1, source_target_pairs={{0,4},{4,0},{8,12},{12,8},{16,20},{20,16},{24,28},{28,24},{1,5},{5... | collective-permute-start | bytes 3538952 | tf_op jit(solution)/shard_map/ppermute | solution.py:453
  99.5 5.7 %collective-permute-start.10 = (bf16[2,384,768]{2,1,0:T(8,128)(2,1)S(1)}, bf16[2,384,768]{2,1,0:T(8,128)(2,1)S(1)}, u32[]{:S(2)}, u32[]{:S(2)}) collective-permute-start(bf16[2,384,768]{2,1,0:T(8,128)(2,1)S(1)} %get-tuple-element.72), channel_id=1, source_target_pairs={{0,4},{4,0},{8,12},{12,8},{16,20},{20,16},{24,28},{28,24},{1,5},{5... | collective-permute-start | bytes 3538952 | tf_op jit(solution)/shard_map/ppermute | solution.py:453
  99.6 3.4 %collective-permute-start.5 = (bf16[256,512]{1,0:T(8,128)(2,1)}, bf16[256,512]{1,0:T(8,128)(2,1)S(1)}, u32[]{:S(2)}, u32[]{:S(2)}) collective-permute-start(bf16[256,512]{1,0:T(8,128)(2,1)} %get-tuple-element.64), channel_id=1, source_target_pairs={{0,4},{4,0},{8,12},{12,8},{16,20},{20,16},{24,28},{28,24},{1,5},{5... | collective-permute-start | bytes 786440 | tf_op jit(solution)/shard_map/ppermute | solution.py:453
  100.0 3.7 %collective-permute-start.6 = (bf16[256,512]{1,0:T(8,128)(2,1)}, bf16[256,512]{1,0:T(8,128)(2,1)S(1)}, u32[]{:S(2)}, u32[]{:S(2)}) collective-permute-start(bf16[256,512]{1,0:T(8,128)(2,1)} %get-tuple-element.65), channel_id=1, source_target_pairs={{0,4},{4,0},{8,12},{12,8},{16,20},{20,16},{24,28},{28,24},{1,5},{5... | collective-permute-start | bytes 786440 | tf_op jit(solution)/shard_map/ppermute | solution.py:453
  100.1 4.3 %collective-permute-start.7 = (bf16[256,512]{1,0:T(8,128)(2,1)}, bf16[256,512]{1,0:T(8,128)(2,1)S(1)}, u32[]{:S(2)}, u32[]{:S(2)}) collective-permute-start(bf16[256,512]{1,0:T(8,128)(2,1)} %get-tuple-element.66), channel_id=1, source_target_pairs={{0,4},{4,0},{8,12},{12,8},{16,20},{20,16},{24,28},{28,24},{1,5},{5... | collective-permute-start | bytes 786440 | tf_op jit(solution)/shard_map/ppermute | solution.py:453
  102.9 2.3 collective-permute-start.8
  108.1 25.9 %collective-permute-start.11 = (bf16[256,512]{1,0:T(8,128)(2,1)S(1)}, bf16[256,512]{1,0:T(8,128)(2,1)S(1)}, u32[]{:S(2)}, u32[]{:S(2)}) collective-permute-start(bf16[256,512]{1,0:T(8,128)(2,1)S(1)} %get-tuple-element.77), channel_id=1, source_target_pairs={{8,0},{12,4},{16,8},{20,12},{24,16},{28,20},{9,1},{13,5},{17,9},{2... | collective-permute-start | bytes 786440 | tf_op jit(solution)/shard_map/ppermute | solution.py:587
  109.4 50.2 %collective-permute-start.12 = (bf16[256,512]{1,0:T(8,128)(2,1)S(1)}, bf16[256,512]{1,0:T(8,128)(2,1)S(1)}, u32[]{:S(2)}, u32[]{:S(2)}) collective-permute-start(bf16[256,512]{1,0:T(8,128)(2,1)S(1)} %get-tuple-element.78), channel_id=1, source_target_pairs={{16,0},{20,4},{24,8},{28,12},{17,1},{21,5},{25,9},{29,13},{18,2},{... | collective-permute-start | bytes 786440 | tf_op jit(solution)/shard_map/ppermute | solution.py:587
  110.7 48.9 %collective-permute-start.13 = (bf16[256,512]{1,0:T(8,128)(2,1)S(1)}, bf16[256,512]{1,0:T(8,128)(2,1)S(1)}, u32[]{:S(2)}, u32[]{:S(2)}) collective-permute-start(bf16[256,512]{1,0:T(8,128)(2,1)S(1)} %get-tuple-element.79), channel_id=1, source_target_pairs={{24,0},{28,4},{25,1},{29,5},{26,2},{30,6},{27,3},{31,7}} | collective-permute-start | bytes 786440 | tf_op jit(solution)/shard_map/ppermute | solution.py:587
  116.9 42.7 %copy-start.21 = (bf16[256,512]{1,0:T(8,128)(2,1)S(1)}, bf16[256,512]{1,0:T(8,128)(2,1)}, u32[]{:S(2)}) copy-start(bf16[256,512]{1,0:T(8,128)(2,1)} %copy-done.20) | copy-start | bytes 786436
  122.6 38.2 %copy-start.16 = (bf16[256,3072]{1,0:T(8,128)(2,1)S(1)}, bf16[256,3072]{1,0:T(8,128)(2,1)}, u32[]{:S(2)}) copy-start(bf16[256,3072]{1,0:T(8,128)(2,1)} %copy-done.15) | copy-start | bytes 4718596
  164.5 2.3 collective-permute-start.15
  164.6 20.7 %collective-permute-start.14 = (bf16[256,1536]{1,0:T(8,128)(2,1)}, bf16[256,1536]{1,0:T(8,128)(2,1)}, u32[]{:S(2)}, u32[]{:S(2)}) collective-permute-start(bf16[256,1536]{1,0:T(8,128)(2,1)} %get-tuple-element.83), channel_id=1, source_target_pairs={{0,1},{1,0},{2,3},{3,2},{4,5},{5,4},{6,7},{7,6},{8,9},{9,8},{10,11... | collective-permute-start | bytes 2359304 | tf_op jit(solution)/shard_map/ppermute | solution.py:36
  166.1 37.5 %collective-permute-start.20 = (bf16[256,1664]{1,0:T(8,128)(2,1)}, bf16[256,1664]{1,0:T(8,128)(2,1)}, u32[]{:S(2)}, u32[]{:S(2)}) collective-permute-start(bf16[256,1664]{1,0:T(8,128)(2,1)} %get-tuple-element.95), channel_id=1, source_target_pairs={{0,1},{1,0},{2,3},{3,2},{4,5},{5,4},{6,7},{7,6},{8,9},{9,8},{10,11... | collective-permute-start | bytes 2555912 | tf_op jit(solution)/shard_map/ppermute | solution.py:36
  166.7 40.3 %collective-permute-start.18 = (bf16[2,384,512]{2,1,0:T(8,128)(2,1)}, bf16[2,384,512]{2,1,0:T(8,128)(2,1)}, u32[]{:S(2)}, u32[]{:S(2)}) collective-permute-start(bf16[2,384,512]{2,1,0:T(8,128)(2,1)} %get-tuple-element.92), channel_id=1, source_target_pairs={{0,4},{4,0},{8,12},{12,8},{16,20},{20,16},{24,28},{28,24},{1,5},{5... | collective-permute-start | bytes 2359304 | tf_op jit(solution)/shard_map/ppermute | solution.py:453
  167.0 18.3 %copy-start.2 = (bf16[1,256,1536]{2,1,0:T(8,128)(2,1)S(1)}, bf16[1,256,1536]{2,1,0:T(8,128)(2,1)}, u32[]{:S(2)}) copy-start(bf16[1,256,1536]{2,1,0:T(8,128)(2,1)} %param.8) | copy-start | bytes 2359300
  167.0 52.5 %collective-permute-start.19 = (bf16[2,384,512]{2,1,0:T(8,128)(2,1)S(1)}, bf16[2,384,512]{2,1,0:T(8,128)(2,1)}, u32[]{:S(2)}, u32[]{:S(2)}) collective-permute-start(bf16[2,384,512]{2,1,0:T(8,128)(2,1)S(1)} %shard_map.148.refs_5_), channel_id=1, source_target_pairs={{0,8},{4,12},{8,0},{12,4},{16,24},{20,28},{24,16},{28,20},{1,9},{5... | collective-permute-start | bytes 2359304 | tf_op jit(solution)/shard_map/ppermute | solution.py:606
  189.6 38.5 %collective-permute-start.17 = (bf16[256,1664]{1,0:T(8,128)(2,1)}, bf16[256,1664]{1,0:T(8,128)(2,1)}, u32[]{:S(2)}, u32[]{:S(2)}) collective-permute-start(bf16[256,1664]{1,0:T(8,128)(2,1)} %get-tuple-element.91), channel_id=1, source_target_pairs={{0,1},{1,0},{2,3},{3,2},{4,5},{5,4},{6,7},{7,6},{8,9},{9,8},{10,11... | collective-permute-start | bytes 2555912 | tf_op jit(solution)/shard_map/ppermute | solution.py:36
  191.1 40.2 %collective-permute-start.16 = (bf16[256,1536]{1,0:T(8,128)(2,1)}, bf16[256,1536]{1,0:T(8,128)(2,1)}, u32[]{:S(2)}, u32[]{:S(2)}) collective-permute-start(bf16[256,1536]{1,0:T(8,128)(2,1)} %get-tuple-element.88.refs_1_), channel_id=1, source_target_pairs={{0,2},{2,0},{1,3},{3,1},{4,6},{6,4},{5,7},{7,5},{8,10},{10,8},{9,1... | collective-permute-start | bytes 2359304 | tf_op jit(solution)/shard_map/ppermute | solution.py:36
  223.8 14.8 %collective-permute-start.21 = (bf16[192,512]{1,0:T(8,128)(2,1)S(1)}, bf16[192,512]{1,0:T(8,128)(2,1)S(1)}, u32[]{:S(2)}, u32[]{:S(2)}) collective-permute-start(bf16[192,512]{1,0:T(8,128)(2,1)S(1)} %get-tuple-element.98), channel_id=1, source_target_pairs={{0,16},{2,18},{4,20},{6,22},{8,24},{10,26},{12,28},{14,30},{16,0},... | collective-permute-start | bytes 589832 | tf_op jit(solution)/shard_map/ppermute | solution.py:638
  223.8 19.8 %collective-permute-start.22 = (bf16[192,512]{1,0:T(8,128)(2,1)S(1)}, bf16[192,512]{1,0:T(8,128)(2,1)S(1)}, u32[]{:S(2)}, u32[]{:S(2)}) collective-permute-start(bf16[192,512]{1,0:T(8,128)(2,1)S(1)} %get-tuple-element.99), channel_id=1, source_target_pairs={{0,18},{2,16},{4,22},{6,20},{8,26},{10,24},{12,30},{14,28},{16,2},... | collective-permute-start | bytes 589832 | tf_op jit(solution)/shard_map/ppermute | solution.py:638
  227.6 16.0 %collective-permute-start.23 = (bf16[192,512]{1,0:T(8,128)(2,1)S(1)}, bf16[192,512]{1,0:T(8,128)(2,1)S(1)}, u32[]{:S(2)}, u32[]{:S(2)}) collective-permute-start(bf16[192,512]{1,0:T(8,128)(2,1)S(1)} %get-tuple-element.100), channel_id=1, source_target_pairs={{0,2},{2,0},{1,3},{3,1},{4,6},{6,4},{5,7},{7,5},{8,10},{10,8},{9,1... | collective-permute-start | bytes 589832 | tf_op jit(solution)/shard_map/ppermute | solution.py:36
  (28 other events, 73.5 us)
Sparse Core Ops, SparseCore 0:
  34.0 30.0 all-gather.2
  87.3 66.1 reduce-scatter.2
  155.8 66.9 reduce-scatter.4
